TPU v7x, 32 devices: a whole 2x2x4 slice. The times are simulated.
32 devices in a mesh: grp: 2 (over core), row: 8 (over z, x), head: 2 (over y).
Axes of the slice: x: 2, y: 2, z: 4, core: 2. Of those that a mesh axis runs over, the one named last changes fastest.
Arguments:
- tokens: int32 [2, 256], P('grp'), may hold values from 0 to 22
- lengths: int32 [2], P('grp'), may hold values from 128 to 256, as said below
- recycle: int32 [2], P('grp'), may hold values from 1 to 4, as said below
- resolved: int32 [2, 256], P('grp'), may hold values from 0 to 1, as said below
- coords: float32 [2, 3, 256], P('grp')
- plm_embed: bfloat16 [23, 1280], replicated, may hold values from -6 to 6
- plm_uv: bfloat16 [2, 1280, 2560], P(None, None, 'head'), may hold values from -0.15625 to 0.15625
- plm_qk: bfloat16 [1280, 256], replicated, may hold values from -0.15625 to 0.15625
- plm_affine: float32 [4, 256], replicated, may hold values from -1 to 1
- plm_out: bfloat16 [2560, 1280], P('head'), may hold values from -0.125 to 0.125
- w_in: float32 [1280, 256], replicated, may hold values from -0.15625 to 0.15625
- w_pairin: float32 [2, 256, 128], replicated, may hold values from -0.375 to 0.375
- w_tri: float32 [6, 128, 128], replicated, may hold values from -0.5 to 0.5
- vecs: float32 [4, 128], replicated
- row_in: float32 [1280], replicated, may hold values from 2e-07 to 2e-06
- col_in: float32 [256], replicated, may hold values from 2e-07 to 2e-06
- row_pairin: float32 [2, 256], replicated, may hold values from 2e-07 to 2e-06
- col_pairin: float32 [2, 128], replicated, may hold values from 2e-07 to 2e-06
- row_tri: float32 [6, 128], replicated, may hold values from 2e-07 to 2e-06
- col_tri: float32 [6, 128], replicated, may hold values from 2e-07 to 2e-06
- sq_vecs: float32 [4, 128], replicated, may hold values from 1e-07 to 0.001
Outputs:
- loss_sum: float32 [], replicated
- loss_count: float32 [], replicated
- grad_in: float32 [1280, 256], replicated
- new_row_in: float32 [1280], replicated
- new_col_in: float32 [256], replicated
- new_in: float32 [1280, 256], replicated
- grad_pairin: float32 [2, 256, 128], replicated
- new_row_pairin: float32 [2, 256], replicated
- new_col_pairin: float32 [2, 128], replicated
- new_pairin: float32 [2, 256, 128], replicated
- grad_tri: float32 [6, 128, 128], replicated
- new_row_tri: float32 [6, 128], replicated
- new_col_tri: float32 [6, 128], replicated
- new_tri: float32 [6, 128, 128], replicated
- grad_vecs: float32 [4, 128], replicated
- new_sq_vecs: float32 [4, 128], replicated
- new_vecs: float32 [4, 128], replicated
Inputs may be any that keep to these rules, and one draw needn't show every extreme that they name: `lengths`: one of the two items has length 256, the other at least 128 and less than 256. One of the two items has recycle count 4, the other a smaller one. Each item has resolved residues among its first 128 positions.
All inputs are finite; a program needn't handle non-finite values.
Results may differ from a plain program's by a relative error of at most 0.0076.
Values may be sent and summed in bfloat16 or wider, within the bound.
A program may use at most 704 MiB of HBM per device.

v0:
```python
import math

import jax
import jax.numpy as jnp
from jax import lax
from jax.sharding import PartitionSpec as P

STEP = 10


highest = lax.Precision.HIGHEST


def normalize(value):
    centre = value - jnp.mean(value, -1, keepdims=True)
    scale = lax.rsqrt(jnp.mean(centre * centre, -1, keepdims=True) + 1e-05)
    return (centre * scale, scale)


def norm_back(normal, scale, grad):
    return scale * (
        grad
        - jnp.mean(grad, -1, keepdims=True)
        - normal * jnp.mean(grad * normal, -1, keepdims=True)
    )


def plm_layer(tok, length, plm_embed, plm_uv, plm_qk, plm_affine, plm_out):
    onehot = (tok[:, None] == jnp.arange(plm_embed.shape[0])[None, :]).astype(jnp.bfloat16)
    embed = jnp.dot(onehot, plm_embed, preferred_element_type=jnp.float32)
    normed = normalize(embed)[0].astype(jnp.bfloat16)
    ugate = jax.nn.silu(jnp.dot(normed, plm_uv[0], preferred_element_type=jnp.float32))
    value = jax.nn.silu(jnp.dot(normed, plm_uv[1], preferred_element_type=jnp.float32)).astype(
        jnp.bfloat16
    )
    shared = jax.nn.silu(jnp.dot(normed, plm_qk, preferred_element_type=jnp.float32))
    query = (shared * plm_affine[0] + plm_affine[1]).astype(jnp.bfloat16)
    keyed = (shared * plm_affine[2] + plm_affine[3]).astype(jnp.bfloat16)
    scores = jnp.dot(query, keyed.T, preferred_element_type=jnp.float32) / math.sqrt(
        plm_qk.shape[1]
    )
    valid = jnp.arange(tok.shape[0]) < length
    attn = jax.nn.softmax(jnp.where(valid[None, :], scores, -1000000000.0), axis=-1).astype(
        jnp.bfloat16
    )
    mixed = (ugate * jnp.dot(attn, value, preferred_element_type=jnp.float32)).astype(jnp.bfloat16)
    partial_out = jnp.dot(mixed, plm_out, preferred_element_type=jnp.float32)
    state = embed + lax.psum(partial_out, "head")
    return (normalize(state)[0].astype(jnp.bfloat16), scores)


def factored(grad, weight, row_old, col_old):
    beta = 1.0 - STEP ** (-0.8)
    sq = grad * grad + 1e-30
    row_new = beta * row_old + (1.0 - beta) * jnp.mean(sq, -1)
    col_new = beta * col_old + (1.0 - beta) * jnp.mean(sq, -2)
    second = row_new[..., :, None] * col_new[..., None, :] / jnp.mean(row_new, -1)[..., None, None]
    step = grad * lax.rsqrt(second)
    rms = jnp.sqrt(jnp.mean(step * step, axis=(-2, -1), keepdims=True))
    step = step / jnp.maximum(1.0, rms)
    scale = jnp.maximum(0.001, jnp.sqrt(jnp.mean(weight * weight, axis=(-2, -1), keepdims=True)))
    return (row_new, col_new, weight - 0.3 * scale * step)


def unfactored(grad, weight, sq_old):
    beta = 1.0 - STEP ** (-0.8)
    sq_new = beta * sq_old + (1.0 - beta) * (grad * grad + 1e-30)
    step = grad * lax.rsqrt(sq_new)
    rms = jnp.sqrt(jnp.mean(step * step, -1, keepdims=True))
    step = step / jnp.maximum(1.0, rms)
    scale = jnp.maximum(0.001, jnp.sqrt(jnp.mean(weight * weight, -1, keepdims=True)))
    return (sq_new, weight - 0.3 * scale * step)


def shards(
    tokens,
    lengths,
    recycle,
    resolved,
    coords,
    plm_embed,
    plm_uv,
    plm_qk,
    plm_affine,
    plm_out,
    w_in,
    w_pairin,
    w_tri,
    vecs,
    row_in,
    col_in,
    row_pairin,
    col_pairin,
    row_tri,
    col_tri,
    sq_vecs,
):
    total_len = tokens.shape[1]
    rows_dev = total_len // lax.axis_size("row")
    cols_dev = total_len // lax.axis_size("head")
    row_start = lax.axis_index("row") * rows_dev
    col_start = lax.axis_index("head") * cols_dev
    length = lengths[0]
    frozen_in, scores = plm_layer(tokens[0], length, plm_embed, plm_uv, plm_qk, plm_affine, plm_out)
    valid = ((jnp.arange(total_len) < length) & (resolved[0] > 0)).astype(jnp.float32)
    valid_rows = lax.dynamic_slice_in_dim(valid, row_start, rows_dev, 0)
    valid_cols = lax.dynamic_slice_in_dim(valid, col_start, cols_dev, 0)
    pair_weight = recycle[0].astype(jnp.float32) * valid_rows[:, None] * valid_cols[None, :]
    place_rows = lax.dynamic_slice_in_dim(coords[0], row_start, rows_dev, 1)
    place_cols = lax.dynamic_slice_in_dim(coords[0], col_start, cols_dev, 1)
    delta = place_rows[:, :, None] - place_cols[:, None, :]
    true_dist = jnp.sqrt(jnp.sum(delta * delta, 0))
    pair_scores = lax.dynamic_slice(scores, (row_start, col_start), (rows_dev, cols_dev))
    single = jnp.dot(
        frozen_in, w_in.astype(jnp.bfloat16), preferred_element_type=jnp.float32
    ).astype(jnp.bfloat16)
    single_rows = lax.dynamic_slice_in_dim(single, row_start, rows_dev, 0)
    single_cols = lax.dynamic_slice_in_dim(single, col_start, cols_dev, 0)
    pair_low = w_pairin.astype(jnp.bfloat16)
    side_a = jnp.dot(single_rows, pair_low[0], preferred_element_type=jnp.float32)
    side_b = jnp.dot(single_cols, pair_low[1], preferred_element_type=jnp.float32)
    pair = pair_scores[:, :, None] * vecs[0] + side_a[:, None, :] + side_b[None, :, :]
    normal_one, scale_one = normalize(pair)
    pnorm = (normal_one * vecs[1]).astype(jnp.bfloat16)
    tri_low = w_tri.astype(jnp.bfloat16)
    proj = jnp.einsum("ijc,mcd->mijd", pnorm, tri_low[:5], preferred_element_type=jnp.float32)
    sig_left = jax.nn.sigmoid(proj[1])
    sig_right = jax.nn.sigmoid(proj[3])
    gate = jax.nn.sigmoid(proj[4])
    left = (sig_left * proj[0]).astype(jnp.bfloat16)
    right = (sig_right * proj[2]).astype(jnp.bfloat16)
    gathered = lax.all_gather(right, "row", axis=0, tiled=True)
    partial_update = jnp.einsum("ikc,jkc->ijc", left, gathered, preferred_element_type=jnp.float32)
    update = lax.psum_scatter(partial_update, "head", scatter_dimension=1, tiled=True)
    normal_two, scale_two = normalize(update)
    unorm = (normal_two * vecs[2]).astype(jnp.bfloat16)
    branch = jnp.einsum("ijc,cd->ijd", unorm, tri_low[5], preferred_element_type=jnp.float32)
    final = pair + gate * branch
    logit = jnp.einsum("ijc,c->ij", final, vecs[3], precision=highest)
    diff = jax.nn.softplus(logit) - true_dist
    root = jnp.sqrt(diff * diff + 1.0)
    loss_sum, loss_count = lax.psum(
        (jnp.sum(pair_weight * (root - 1.0)), jnp.sum(pair_weight)), ("grp", "row", "head")
    )
    dlogit = pair_weight / loss_count * diff / root * jax.nn.sigmoid(logit)
    grad_dist = jnp.einsum("ij,ijc->c", dlogit, final, precision=highest)
    dfinal = dlogit[:, :, None] * vecs[3]
    dbranch = (dfinal * gate).astype(jnp.bfloat16)
    dgate = dfinal * branch
    grad_out = jnp.einsum("ijc,ijd->cd", unorm, dbranch, preferred_element_type=jnp.float32)
    dunorm = jnp.einsum("ijd,cd->ijc", dbranch, tri_low[5], preferred_element_type=jnp.float32)
    grad_gain_two = jnp.einsum("ijc,ijc->c", dunorm, normal_two, precision=highest)
    dupdate = norm_back(normal_two, scale_two, dunorm * vecs[2]).astype(jnp.bfloat16)
    dupdate_all = lax.all_gather(dupdate, "head", axis=1, tiled=True)
    dleft = jnp.einsum("ijc,jkc->ikc", dupdate_all, gathered, preferred_element_type=jnp.float32)
    dright = lax.psum_scatter(
        jnp.einsum("ijc,ikc->jkc", dupdate_all, left, preferred_element_type=jnp.float32),
        "row",
        scatter_dimension=0,
        tiled=True,
    )
    dproj = jnp.stack(
        [
            dleft * sig_left,
            dleft * proj[0] * sig_left * (1.0 - sig_left),
            dright * sig_right,
            dright * proj[2] * sig_right * (1.0 - sig_right),
            dgate * gate * (1.0 - gate),
        ]
    ).astype(jnp.bfloat16)
    grad_proj = jnp.einsum("ijc,mijd->mcd", pnorm, dproj, preferred_element_type=jnp.float32)
    dpnorm = jnp.einsum("mijd,mcd->ijc", dproj, tri_low[:5], preferred_element_type=jnp.float32)
    grad_gain_one = jnp.einsum("ijc,ijc->c", dpnorm, normal_one, precision=highest)
    dpair = dfinal + norm_back(normal_one, scale_one, dpnorm * vecs[1])
    grad_scores = jnp.einsum("ij,ijc->c", pair_scores, dpair, precision=highest)
    dside_a = jnp.sum(dpair, 1)
    dside_b = jnp.sum(dpair, 0)
    grad_pair = jnp.stack(
        [
            jnp.dot(single_rows.astype(jnp.float32).T, dside_a, precision=highest),
            jnp.dot(single_cols.astype(jnp.float32).T, dside_b, precision=highest),
        ]
    )
    dsingle_rows = jnp.dot(dside_a, pair_low[0].astype(jnp.float32).T, precision=highest)
    dsingle_cols = jnp.dot(dside_b, pair_low[1].astype(jnp.float32).T, precision=highest)
    frozen_rows = lax.dynamic_slice_in_dim(frozen_in, row_start, rows_dev, 0).astype(jnp.float32)
    frozen_cols = lax.dynamic_slice_in_dim(frozen_in, col_start, cols_dev, 0).astype(jnp.float32)
    grad_node = jnp.dot(frozen_rows.T, dsingle_rows, precision=highest) + jnp.dot(
        frozen_cols.T, dsingle_cols, precision=highest
    )
    grad_tri_local = jnp.concatenate([grad_proj, grad_out[None]], 0)
    grad_vec_local = jnp.stack([grad_scores, grad_gain_one, grad_gain_two, grad_dist])
    grad_in, grad_pairin, grad_tri, grad_vecs = lax.psum(
        (grad_node, grad_pair, grad_tri_local, grad_vec_local), ("grp", "row", "head")
    )
    new_row_in, new_col_in, new_in = factored(grad_in, w_in, row_in, col_in)
    new_row_pairin, new_col_pairin, new_pairin = factored(
        grad_pairin, w_pairin, row_pairin, col_pairin
    )
    new_row_tri, new_col_tri, new_tri = factored(grad_tri, w_tri, row_tri, col_tri)
    new_sq_vecs, new_vecs = unfactored(grad_vecs, vecs, sq_vecs)
    return (
        loss_sum,
        loss_count,
        grad_in,
        new_row_in,
        new_col_in,
        new_in,
        grad_pairin,
        new_row_pairin,
        new_col_pairin,
        new_pairin,
        grad_tri,
        new_row_tri,
        new_col_tri,
        new_tri,
        grad_vecs,
        new_sq_vecs,
        new_vecs,
    )


def solution(mesh):
    in_specs = (
        P("grp", None),
        P("grp"),
        P("grp"),
        P("grp", None),
        P("grp", None, None),
        P(),
        P(None, None, "head"),
        P(),
        P(),
        P("head", None),
        P(),
        P(),
        P(),
        P(),
        P(),
        P(),
        P(),
        P(),
        P(),
        P(),
        P(),
    )
    out_specs = (
        P(),
        P(),
        P(),
        P(),
        P(),
        P(),
        P(),
        P(),
        P(),
        P(),
        P(),
        P(),
        P(),
        P(),
        P(),
        P(),
        P(),
    )
    return jax.shard_map(shards, mesh=mesh, in_specs=in_specs, out_specs=out_specs, check_vma=False)
```

profile of v0, /device:TPU:0, one launch (start us, length us, event | category | flops | bytes accessed | tf_op | source)
XLA Modules:
  0.0 898.6 jit_solution(8070778068736897222)
XLA Ops:
  9.7 1.3 fusion.123
  12.9 4.1 divide_multiply_fusion
  17.0 3.3 broadcast_select_fusion
  20.4 2.9 online-softmax
  23.3 5.6 fusion.60
  29.8 1.4 slice_bitcast_fusion.17
  31.2 1.2 multiply_reduce_fusion.14
  32.4 1.8 multiply_reduce_fusion.12
  34.2 43.4 %all-reduce.5.cloned.1.call-done = f32[256,1280]{1,0:T(8,128)} async-done(((f32[256,1280]{1,0:T(8,128)}), f32[256,1280]{1,0:T(8,128)}) %all-reduce.5.cloned.1.call-update) | async-done | bytes 1310736 | tf_op jit(solution)/shard_map/psum | solution.py:48
  77.6 1.5 fusion.121
  81.1 1.3 fusion.30
  82.4 1.9 multiply_reduce_fusion.5
  84.9 2.4 convolution_bitcast_fusion
  87.3 2.7 multiply_convert_fusion.5
  90.1 1.7 copy-done.2
  92.1 1.0 copy.83
  93.0 123.8 %all-gather.3.cloned.1.call-done = bf16[256,128,128]{2,1,0:T(8,128)(2,1)} async-done(((bf16[32,128,128]{2,1,0:T(8,128)(2,1)}), bf16[256,128,128]{2,1,0:T(8,128)(2,1)}) %all-gather.3.cloned.1.call-update) | async-done | bytes 8388624 | tf_op jit(solution)/shard_map/all_gather | solution.py:132
  216.9 12.3 %copy.82 = bf16[256,128,128]{1,0,2:T(8,128)(2,1)} copy(bf16[256,128,128]{2,1,0:T(8,128)(2,1)} %all-gather.3.cloned.1.call-done) | data formatting | bytes 16777216 | tf_op jit(solution)/shard_map/all_gather | solution.py:132
  229.2 8.3 convolution_bitcast_fusion.1
  238.5 51.6 %reduce-scatter.3.cloned.1.call-done = f32[32,128,128]{1,0,2:T(8,128)} async-done(((f32[32,256,128]{1,0,2:T(8,128)}), f32[32,128,128]{1,0,2:T(8,128)}) %reduce-scatter.3.cloned.1.call-update) | async-done | bytes 2097168 | tf_op jit(solution)/shard_map/reduce_scatter | solution.py:134
  290.1 1.9 reduce_sum.322
  293.8 4.9 fusion.68
  299.4 39.5 %psum.51 = f32[]{:T(128)} all-reduce(f32[]{:T(128)} %get-tuple-element.80), channel_id=1, replica_groups=mesh['grp'=2,'row'=8,'head'=2] {'grp','row','head'}, use_global_device_ids=true, to_apply=%region_16.17 | all-reduce | flops 1 | bytes 8 | tf_op jit(solution)/shard_map/psum | solution.py:142
  339.6 2.4 fusion.40
  342.0 1.4 fusion.32
  343.4 2.5 multiply_convert_fusion.2
  346.0 34.1 %all-gather.5.cloned.1.call-done = bf16[32,256,128]{1,0,2:T(8,128)(2,1)} async-done(((bf16[32,128,128]{1,0,2:T(8,128)(2,1)}), bf16[32,256,128]{1,0,2:T(8,128)(2,1)}) %all-gather.5.cloned.1.call-update) | async-done | bytes 2097168 | tf_op jit(solution)/shard_map/all_gather | solution.py:154
  380.1 9.7 %fusion.126 = f32[128,128,256]{2,1,0:T(8,128)} fusion(bf16[32,128,128]{1,0,2:T(8,128)(2,1)S(1)} %copy.83, bf16[32,256,128]{1,0,2:T(8,128)(2,1)} %all-gather.5.cloned.1.call-done), kind=kOutput, calls=%fused_computation.233 | convolution fusion | flops 268435456 | bytes 19922944 | tf_op jit(solution)/shard_map/ijc,ikc->jkc/dot_general | solution.py:157
  389.8 18.2 %copy.89 = f32[128,128,256]{0,1,2:T(8,128)} copy(f32[128,128,256]{2,1,0:T(8,128)} %fusion.126) | data formatting | bytes 33554432 | tf_op jit(solution)/shard_map/ijc,ikc->jkc/dot_general | solution.py:157
  409.1 0.9 copy.94
  410.0 2.3 multiply_reduce_fusion.8
  414.7 4.2 multiply_reduce_fusion
  418.9 12.6 %convolution_bitcast_fusion.5 = f32[1,128,128]{1,2,0:T(8,128)} fusion(f32[128]{0:T(128)S(1)} %copy-done.57, f32[32,128]{1,0:T(8,128)S(1)} %fusion.97, bf16[32,128,128]{1,0,2:T(8,128)(2,1)S(1)} %copy-done.21, f32[5,32,128,128]{3,2,0,1:T(8,128)} %copy-done.2), kind=kOutput, calls=%fused_computation.84 | convolution fusion | flops 137363456 | bytes 3228160 | tf_op jit(solution)/shard_map/ijc,ijd->cd/dot_general | solution.py:150
  431.4 3.3 convolution_bitcast_fusion.6
  435.0 2.6 fusion.127
  437.6 2.0 copy.87
  439.6 3.2 fusion.49
  442.8 4.0 fusion.47
  446.8 243.4 %reduce-scatter.5.cloned.1.call-done = f32[32,128,128]{2,1,0:T(8,128)} async-done(((f32[256,128,128]{2,1,0:T(8,128)}), f32[32,128,128]{2,1,0:T(8,128)}) %reduce-scatter.5.cloned.1.call-update) | async-done | bytes 2097168 | tf_op jit(solution)/shard_map/reduce_scatter | solution.py:156
  690.2 3.9 fusion.43
  694.1 4.1 fusion.45
  698.2 2.9 fusion.52
  701.1 6.5 convolution_bitcast_fusion.2
  707.6 4.2 fusion.75
  711.9 1.9 copy.90
  713.8 4.6 multiply_reduce_fusion.6
  718.4 3.9 fusion.112
  723.4 7.1 convolution_bitcast_fusion.7
  730.5 1.8 fusion.86
  732.3 2.1 copy.109
  734.3 1.7 pad_maximum_fusion
  736.8 3.3 convolution_add_fusion
  740.2 2.0 multiply_reduce_fusion.1
  742.2 39.5 %all-reduce = (f32[]{:T(128)}, f32[4,128]{1,0:T(4,128)S(1)}) all-reduce(f32[]{:T(128)} %get-tuple-element.81, f32[4,128]{1,0:T(4,128)S(1)} %pad_maximum_fusion.2), channel_id=1, replica_groups=mesh['grp'=2,'row'=8,'head'=2] {'grp','row','head'}, use_global_device_ids=true, to_apply=%region_14.15 | all-reduce | flops 513 | bytes 4104 | tf_op jit(solution)/shard_map/psum | solution.py:142
  782.5 91.3 %all-reduce.7.cloned.1.call-done = (f32[1280,256]{1,0:T(8,128)}, f32[2,256,128]{2,1,0:T(8,128)}, f32[6,128,128]{1,2,0:T(8,128)}) async-done(((f32[1280,256]{1,0:T(8,128)}, f32[2,256,128]{2,1,0:T(8,128)}, f32[6,128,128]{1,2,0:T(8,128)}), (f32[1280,256]{1,0:T(8,128)}, f32[2,256,128]{2,1,0:T(8,128)}, f32[6,128,128]{1,2,0:T(8,128)})) %all-reduce.7.cloned.1.call-update) | async-done | bytes 1966096 | tf_op jit(solution)/shard_map/psum | solution.py:193
  873.8 1.3 fusion.70
  875.1 1.9 copy.95
  877.0 1.1 fusion.73
  878.3 1.2 multiply_reduce_fusion.13
  879.7 1.3 multiply_reduce_fusion.11
  881.2 0.9 copy.96
  883.7 1.1 multiply_reduce_fusion.7
  886.4 3.3 multiply_subtract_fusion
  889.7 1.1 copy.150
  (224 shorter events, 19.4 us)
Async XLA Ops:
  7.2 16.1 %copy-start = (bf16[1280,1280]{1,0:T(8,128)(2,1)S(1)}, bf16[1280,1280]{1,0:T(8,128)(2,1)}, u32[]{:S(2)}) copy-start(bf16[1280,1280]{1,0:T(8,128)(2,1)} %param.30) | copy-start | bytes 9830404
  7.2 70.4 %all-reduce.5.cloned.1.call-start = ((), (), s32[]{:S(2)}) async-start(), calls=%async_computation.2 | async-start | bytes 2621440 | tf_op jit(solution)/shard_map/psum | solution.py:48
  12.3 4.7 copy-start.37
  23.3 7.9 copy-start.29
  28.9 48.6 %copy-start.7 = (f32[256,1280]{1,0:T(8,128)S(1)}, f32[256,1280]{1,0:T(8,128)}, u32[]{:S(2)}) copy-start(f32[256,1280]{1,0:T(8,128)} %copy-done.6) | copy-start | bytes 3932164
  29.0 187.9 %all-gather.3.cloned.1.call-start = ((), (), s32[]{:S(2)}) async-start(), calls=%async_computation.3 | async-start | bytes 9437184 | tf_op jit(solution)/shard_map/all_gather | solution.py:132
  79.5 5.5 copy-start.48
  80.4 6.9 copy-start.18
  80.8 6.5 copy-start.35
  80.9 3.4 copy-start.25
  87.3 4.4 copy-start.2
  91.8 198.4 %reduce-scatter.3.cloned.1.call-start = ((), (), s32[]{:S(2)}) async-start(), calls=%async_computation.4 | async-start | bytes 6291456 | tf_op jit(solution)/shard_map/reduce_scatter | solution.py:134
  237.5 142.7 %all-gather.5.cloned.1.call-start = ((), (), s32[]{:S(2)}) async-start(), calls=%async_computation.5 | async-start | bytes 3145728 | tf_op jit(solution)/shard_map/all_gather | solution.py:154
  238.5 54.1 %copy-start.55 = (f32[128]{0:T(128)S(1)}, f32[128]{0:T(128)}, u32[]{:S(2)}) copy-start(f32[128]{0:T(128)} %get-tuple-element.108) | copy-start | bytes 1540
  293.0 5.7 copy-start.20
  293.8 4.9 copy-start.13
  293.8 45.8 %copy-start.56 = (f32[128]{0:T(128)S(1)}, f32[128]{0:T(128)}, u32[]{:S(2)}) copy-start(f32[128]{0:T(128)} %get-tuple-element.107) | copy-start | bytes 1540
  346.0 344.2 %reduce-scatter.5.cloned.1.call-start = ((), (), s32[]{:S(2)}) async-start(), calls=%async_computation.6 | async-start | bytes 18874368 | tf_op jit(solution)/shard_map/reduce_scatter | solution.py:156
  408.1 5.5 copy-start.69
  408.1 6.1 copy-start.72
  408.1 465.7 %all-reduce.7.cloned.1.call-start = ((), (), s32[]{:S(2)}) async-start(), calls=%async_computation.7 | async-start | bytes 3932160 | tf_op jit(solution)/shard_map/psum | solution.py:193
  414.7 4.2 copy-start.21
  414.7 4.2 copy-start.57
  418.9 12.6 %copy-start.14 = (f32[32,128,128]{2,1,0:T(8,128)S(1)}, f32[32,128,128]{2,1,0:T(8,128)}, u32[]{:S(2)}) copy-start(f32[32,128,128]{2,1,0:T(8,128)} %copy-done.13) | copy-start | bytes 6291460
  418.9 15.9 %slice-start = ((s8[8388608]{0:T(1024)(128)(4,1)}), s8[4194304]{0:T(1024)(128)(4,1)S(1)}, s32[]{:S(2)}) async-start(s8[8388608]{0:T(1024)(128)(4,1)} %bitcast.289), calls=%async_computation.8 | async-start | bytes 8388608
  431.4 3.3 slice-start.1
  431.4 3.6 copy-start.10
  690.2 3.9 copy-start.12
  694.1 4.1 copy-start.15
  698.2 2.9 copy-start.34
  698.2 2.9 copy-start.49
  711.9 6.5 copy-start.44
  713.8 4.7 copy-start.9
  713.8 8.6 copy-start.28
  713.8 8.9 copy-start.36
  718.4 5.0 copy-start.58
  723.4 7.1 copy-start.19
  736.8 3.3 copy-start.16
  740.1 41.6 %copy-start.64 = (f32[4,128]{1,0:T(4,128)S(1)}, f32[4,128]{1,0:T(4,128)}, u32[]{:S(2)}) copy-start(f32[4,128]{1,0:T(4,128)} %param.41) | copy-start | bytes 6148
  740.1 41.8 %copy-start.47 = (f32[4,128]{1,0:T(4,128)S(1)}, f32[4,128]{1,0:T(4,128)}, u32[]{:S(2)}) copy-start(f32[4,128]{1,0:T(4,128)} %param.34) | copy-start | bytes 6148
  740.1 41.8 %copy-start.70 = (f32[4]{0:T(128)S(1)}, f32[4]{0:T(128)}, u32[]{:S(2)}) copy-start(f32[4]{0:T(128)} %maximum_multiply_fusion) | copy-start | bytes 52
  740.1 138.0 %copy-start.65 = (f32[2,256]{1,0:T(2,128)S(1)}, f32[2,256]{1,0:T(2,128)}, u32[]{:S(2)}) copy-start(f32[2,256]{1,0:T(2,128)} %param.37) | copy-start | bytes 6148
  740.1 138.2 %copy-start.66 = (f32[2,128]{1,0:T(2,128)S(1)}, f32[2,128]{1,0:T(2,128)}, u32[]{:S(2)}) copy-start(f32[2,128]{1,0:T(2,128)} %param.38) | copy-start | bytes 3076
  740.1 139.4 %copy-start.59 = (f32[6,128]{1,0:T(8,128)S(1)}, f32[6,128]{1,0:T(8,128)}, u32[]{:S(2)}) copy-start(f32[6,128]{1,0:T(8,128)} %param.39) | copy-start | bytes 9220
  740.1 139.5 %copy-start.60 = (f32[6,128]{1,0:T(8,128)S(1)}, f32[6,128]{1,0:T(8,128)}, u32[]{:S(2)}) copy-start(f32[6,128]{1,0:T(8,128)} %param.40) | copy-start | bytes 9220
  740.2 140.8 %copy-start.23 = (f32[6,128,128]{1,2,0:T(8,128)S(1)}, f32[6,128,128]{1,2,0:T(8,128)}, u32[]{:S(2)}) copy-start(f32[6,128,128]{1,2,0:T(8,128)} %copy.94) | copy-start | bytes 1179652
  740.2 140.8 %copy-start.68 = (f32[6]{0:T(128)S(1)}, f32[6]{0:T(128)}, u32[]{:S(2)}) copy-start(f32[6]{0:T(128)} %maximum_multiply_fusion.1) | copy-start | bytes 76
  781.7 100.7 %copy-start.53 = (f32[4,128]{1,0:T(4,128)}, f32[4,128]{1,0:T(4,128)S(1)}, u32[]{:S(2)}) copy-start(f32[4,128]{1,0:T(4,128)S(1)} %get-tuple-element.131) | copy-start | bytes 6148
  781.8 100.6 %copy-start.54 = (f32[4,128]{1,0:T(4,128)}, f32[4,128]{1,0:T(4,128)S(1)}, u32[]{:S(2)}) copy-start(f32[4,128]{1,0:T(4,128)S(1)} %get-tuple-element.132) | copy-start | bytes 6148
  873.8 7.2 copy-start.17
  873.8 8.4 copy-start.4
  877.0 5.4 copy-start.67
  877.0 5.5 copy-start.52
  878.3 7.3 copy-start.45
  878.3 7.2 copy-start.50
  879.6 5.2 copy-start.40
  879.7 5.1 copy-start.41
  881.0 4.6 copy-start.22
  881.0 4.6 copy-start.30
  881.0 4.6 copy-start.71
  882.5 3.1 copy-start.51
  883.1 6.7 copy-start.38
  886.4 3.3 copy-start.5
  886.4 5.1 copy-start.1
  (17 other events, 23.4 us)
Sparse Core Ops, SparseCore 0:
  29.1 48.4 all-reduce.4
  91.9 124.9 all-gather.2
  237.6 52.4 reduce-scatter.2
  346.1 34.0 all-gather.4
  408.2 281.9 reduce-scatter.4
  740.2 133.5 all-reduce.6
where the time goes:
time: 908 us; the launch traced here: 899 us
  waiting for transfers between devices  588 us (65%)
  matrix products  85.4 us (9%)
  blocking collectives  79 us (9%)
  other arithmetic  72.3 us (8%)
  local copies, waits for them, and re-layouts  51.9 us (6%)
  between operations  18.8 us (2%)
    reduce_scatter x1, waiting for transfers between devices, shards(): lax.psum_scatter(jnp.einsum('ijc,ikc->jkc', dupdate_all, left, preferred_...  243 us
    all_gather x1, waiting for transfers between devices, shards(): gathered = lax.all_gather(right, 'row', axis=0, tiled=True)  124 us
    psum x1, waiting for transfers between devices, shards(): lax.psum((grad_node, grad_pair, grad_tri_local, grad_vec_local), ('grp',...  91.3 us
    psum x2, blocking collectives, shards(): lax.psum((jnp.sum(pair_weight * (root - 1.0)), jnp.sum(pair_weight)), ('g...  79 us
    reduce_scatter x1, waiting for transfers between devices, shards(): lax.psum_scatter(partial_update, 'head', scatter_dimension=1, tiled=True)  51.6 us
    psum x1, waiting for transfers between devices, plm_layer(): state = embed + lax.psum(partial_out, 'head')  43.4 us
    all_gather x1, waiting for transfers between devices, shards(): dupdate_all = lax.all_gather(dupdate, 'head', axis=1, tiled=True)  34.1 us
    dot_general x1, local copies, waits for them, and re-layouts, shards(): jnp.einsum('ijc,ikc->jkc', dupdate_all, left, preferred_element_type=jnp....  18.2 us
  transfers between devices with their start and end apart: 6, of which 6 were waited for; matrix products, arithmetic and copies ran while one was open for 5% of the time, Pallas kernels for 0%

commit v1 on v0

v1 whole, which is shorter than its diff:
```python
import math

import jax
import jax.numpy as jnp
from jax import lax
from jax.sharding import PartitionSpec as P

STEP = 10
highest = lax.Precision.HIGHEST


def normalize(value):
    centre = value - jnp.mean(value, -1, keepdims=True)
    scale = lax.rsqrt(jnp.mean(centre * centre, -1, keepdims=True) + 1e-05)
    return (centre * scale, scale)


def norm_back(normal, scale, grad):
    return scale * (
        grad
        - jnp.mean(grad, -1, keepdims=True)
        - normal * jnp.mean(grad * normal, -1, keepdims=True)
    )


def factored(grad, weight, row_old, col_old):
    beta = 1.0 - STEP ** (-0.8)
    sq = grad * grad + 1e-30
    row_new = beta * row_old + (1.0 - beta) * jnp.mean(sq, -1)
    col_new = beta * col_old + (1.0 - beta) * jnp.mean(sq, -2)
    second = row_new[..., :, None] * col_new[..., None, :] / jnp.mean(row_new, -1)[..., None, None]
    step = grad * lax.rsqrt(second)
    rms = jnp.sqrt(jnp.mean(step * step, axis=(-2, -1), keepdims=True))
    step = step / jnp.maximum(1.0, rms)
    scale = jnp.maximum(0.001, jnp.sqrt(jnp.mean(weight * weight, axis=(-2, -1), keepdims=True)))
    return (row_new, col_new, weight - 0.3 * scale * step)


def unfactored(grad, weight, sq_old):
    beta = 1.0 - STEP ** (-0.8)
    sq_new = beta * sq_old + (1.0 - beta) * (grad * grad + 1e-30)
    step = grad * lax.rsqrt(sq_new)
    rms = jnp.sqrt(jnp.mean(step * step, -1, keepdims=True))
    step = step / jnp.maximum(1.0, rms)
    scale = jnp.maximum(0.001, jnp.sqrt(jnp.mean(weight * weight, -1, keepdims=True)))
    return (sq_new, weight - 0.3 * scale * step)


def dot32(a, b):
    return jnp.dot(a, b, precision=highest)


def shards(
    tokens, lengths, recycle, resolved, coords, plm_embed, plm_uv, plm_qk, plm_affine, plm_out,
    w_in, w_pairin, w_tri, vecs, row_in, col_in, row_pairin, col_pairin, row_tri, col_tri, sq_vecs,
):
    f32, bf16 = jnp.float32, jnp.bfloat16
    total_len = tokens.shape[1]
    vocab = plm_embed.shape[0]
    length = lengths[0]
    onehot = (tokens[0][:, None] == jnp.arange(vocab)[None, :]).astype(f32)
    key_ok = (jnp.arange(total_len) < length).astype(f32)
    count = jnp.sum(onehot, 0)
    count_key = dot32(key_ok[None, :], onehot)[0]
    embed = plm_embed.astype(f32)
    normed = normalize(embed)[0].astype(bf16)
    ugate = jax.nn.silu(jnp.dot(normed, plm_uv[0], preferred_element_type=f32))
    value = jax.nn.silu(jnp.dot(normed, plm_uv[1], preferred_element_type=f32)).astype(bf16)
    shared = jax.nn.silu(jnp.dot(normed, plm_qk, preferred_element_type=f32))
    query = (shared * plm_affine[0] + plm_affine[1]).astype(bf16)
    keyed = (shared * plm_affine[2] + plm_affine[3]).astype(bf16)
    scores = jnp.dot(query, keyed.T, preferred_element_type=f32) / math.sqrt(plm_qk.shape[1])
    masked = jnp.where(count_key[None, :] > 0, scores, -1000000000.0)
    top = jnp.exp(masked - jnp.max(masked, -1, keepdims=True))
    attn = (top / jnp.sum(top * count_key, -1, keepdims=True)).astype(bf16).astype(f32)
    mixed = (ugate * dot32(attn * count_key, value.astype(f32))).astype(bf16)
    partial_out = jnp.dot(mixed, plm_out, preferred_element_type=f32)
    state = embed + lax.psum(partial_out, "head")
    frozen = normalize(state)[0].astype(bf16)

    single = jnp.dot(frozen, w_in.astype(bf16), preferred_element_type=f32).astype(bf16)
    pair_low = w_pairin.astype(bf16)
    side_a = jnp.dot(single, pair_low[0], preferred_element_type=f32)
    side_b = jnp.dot(single, pair_low[1], preferred_element_type=f32)
    pair = scores[:, :, None] * vecs[0] + side_a[:, None, :] + side_b[None, :, :]
    normal_one, scale_one = normalize(pair)
    pnorm = (normal_one * vecs[1]).astype(bf16)
    tri_low = w_tri.astype(bf16)
    proj = jnp.einsum("ijc,mcd->mijd", pnorm, tri_low[:5], preferred_element_type=f32)
    sig_left = jax.nn.sigmoid(proj[1])
    sig_right = jax.nn.sigmoid(proj[3])
    gate = jax.nn.sigmoid(proj[4])
    left = (sig_left * proj[0]).astype(bf16).astype(f32)
    right = (sig_right * proj[2]).astype(bf16).astype(f32)
    update = jnp.einsum("ikc,jkc->ijc", left * count[None, :, None], right, precision=highest)
    normal_two, scale_two = normalize(update)
    unorm = (normal_two * vecs[2]).astype(bf16)
    branch = jnp.einsum("ijc,cd->ijd", unorm, tri_low[5], preferred_element_type=f32)
    final = pair + gate * branch
    logit = jnp.einsum("ijc,c->ij", final, vecs[3], precision=highest)

    valid = key_ok * (resolved[0] > 0).astype(f32)
    weight = recycle[0].astype(f32) * valid[:, None] * valid[None, :]
    delta = coords[0][:, :, None] - coords[0][:, None, :]
    true_dist = jnp.sqrt(jnp.sum(delta * delta, 0))
    dist = dot32(dot32(onehot, jax.nn.softplus(logit)), onehot.T)
    diff = dist - true_dist
    root = jnp.sqrt(diff * diff + 1.0)
    loss_sum, loss_count = lax.psum(
        (jnp.sum(weight * (root - 1.0)), jnp.sum(weight)), "grp"
    )
    ddist = dot32(dot32(onehot.T, weight * diff / root), onehot)

    dlogit = ddist / loss_count * jax.nn.sigmoid(logit)
    grad_dist = jnp.einsum("ij,ijc->c", dlogit, final, precision=highest)
    dfinal = dlogit[:, :, None] * vecs[3]
    dbranch = (dfinal * gate).astype(bf16)
    dgate = dfinal * branch
    grad_out = jnp.einsum("ijc,ijd->cd", unorm, dbranch, preferred_element_type=f32)
    dunorm = jnp.einsum("ijd,cd->ijc", dbranch, tri_low[5], preferred_element_type=f32)
    grad_gain_two = jnp.einsum("ijc,ijc->c", dunorm, normal_two, precision=highest)
    dupdate = norm_back(normal_two, scale_two, dunorm * vecs[2])
    dleft = jnp.einsum("ijc,jkc->ikc", dupdate, right, precision=highest) * count[None, :, None]
    dright = jnp.einsum("ijc,ikc->jkc", dupdate, left, precision=highest) * count[None, :, None]
    dproj = jnp.stack(
        [
            dleft * sig_left,
            dleft * proj[0] * sig_left * (1.0 - sig_left),
            dright * sig_right,
            dright * proj[2] * sig_right * (1.0 - sig_right),
            dgate * gate * (1.0 - gate),
        ]
    ).astype(bf16)
    grad_proj = jnp.einsum("ijc,mijd->mcd", pnorm, dproj, preferred_element_type=f32)
    dpnorm = jnp.einsum("mijd,mcd->ijc", dproj, tri_low[:5], preferred_element_type=f32)
    grad_gain_one = jnp.einsum("ijc,ijc->c", dpnorm, normal_one, precision=highest)
    dpair = dfinal + norm_back(normal_one, scale_one, dpnorm * vecs[1])
    grad_scores = jnp.einsum("ij,ijc->c", scores, dpair, precision=highest)
    dside_a = jnp.sum(dpair, 1)
    dside_b = jnp.sum(dpair, 0)
    single32 = single.astype(f32)
    grad_pair = jnp.stack([dot32(single32.T, dside_a), dot32(single32.T, dside_b)])
    dsingle = dot32(dside_a, pair_low[0].astype(f32).T) + dot32(dside_b, pair_low[1].astype(f32).T)
    grad_node = dot32(frozen.astype(f32).T, dsingle)
    grad_tri = jnp.concatenate([grad_proj, grad_out[None]], 0)
    grad_vecs = jnp.stack([grad_scores, grad_gain_one, grad_gain_two, grad_dist])
    grad_in, grad_pairin, grad_tri, grad_vecs = lax.psum(
        (grad_node, grad_pair, grad_tri, grad_vecs), "grp"
    )
    new_row_in, new_col_in, new_in = factored(grad_in, w_in, row_in, col_in)
    new_row_pairin, new_col_pairin, new_pairin = factored(grad_pairin, w_pairin, row_pairin, col_pairin)
    new_row_tri, new_col_tri, new_tri = factored(grad_tri, w_tri, row_tri, col_tri)
    new_sq_vecs, new_vecs = unfactored(grad_vecs, vecs, sq_vecs)
    return (
        loss_sum, loss_count, grad_in, new_row_in, new_col_in, new_in, grad_pairin, new_row_pairin,
        new_col_pairin, new_pairin, grad_tri, new_row_tri, new_col_tri, new_tri, grad_vecs,
        new_sq_vecs, new_vecs,
    )


def solution(mesh):
    whole = P()
    in_specs = (
        P("grp", None), P("grp"), P("grp"), P("grp", None), P("grp", None, None), whole,
        P(None, None, "head"), whole, whole, P("head", None),
    ) + (whole,) * 11
    return jax.shard_map(
        shards, mesh=mesh, in_specs=in_specs, out_specs=(whole,) * 17, check_vma=False
    )
```

time: 908 us -> 175 us (0.19)
  waiting for transfers between devices: 588 us -> 23.8 us
  blocking collectives: 79 us -> 6.59 us
  matrix products: 85.4 us -> 44.1 us
  local copies, waits for them, and re-layouts: 51.9 us -> 28.1 us
  other arithmetic: 72.3 us -> 52.4 us
    reduce_scatter x2 -> x0, waiting for transfers between devices: 295 us -> none  [the longest x1 243 us: shards(): lax.psum_scatter(jnp.einsum('ijc,ikc->jkc', dupdate_all, left, preferred_...]
    all_gather x2 -> x0, waiting for transfers between devices: 158 us -> none  [the longest x1 124 us: shards(): gathered = lax.all_gather(right, 'row', axis=0, tiled=True)]
    psum x2, waiting for transfers between devices: 135 us -> 23.7 us  [the longest x1 16.1 us: shards(): state = embed + lax.psum(partial_out, 'head')]
    psum x2, blocking collectives: 79 us -> 6.59 us  [shards(): lax.psum((jnp.sum(weight * (root - 1.0)), jnp.sum(weight)), 'grp')]
    dot_general x23 -> x29, matrix products: 77.2 us -> 39.9 us  [the longest x11 6.94 us: dot32(): return jnp.dot(a, b, precision=highest)]
    dot_general x3, local copies, waits for them, and re-layouts: 22.1 us -> 7.82 us  [the longest x1 2.61 us: shards(): jnp.einsum('ikc,jkc->ijc', left * count[None, :, None], right, precision=...]
    all_gather x1 -> x0, local copies, waits for them, and re-layouts: 12.3 us -> none  [shards(): gathered = lax.all_gather(right, 'row', axis=0, tiled=True)]
  transfers between devices with their start and end apart: 6 -> 2, of which waited for: 6 -> 2; matrix products, arithmetic and copies ran while one was open for 5% -> 10% of each run, Pallas kernels for 0% -> 0%
where the time goes in v1:
time: 175 us; the launch traced here: 173 us
  other arithmetic  52.4 us (30%)
  matrix products  44.1 us (25%)
  local copies, waits for them, and re-layouts  28.1 us (16%)
  waiting for transfers between devices  23.8 us (14%)
  between operations  18.3 us (10%)
  blocking collectives  6.59 us (4%)
    psum x1, waiting for transfers between devices, shards(): state = embed + lax.psum(partial_out, 'head')  16.1 us
    unnamed x138, local copies, waits for them, and re-layouts  9.27 us
    unnamed x4, other arithmetic  7.59 us
    psum x1, waiting for transfers between devices, shards(): lax.psum((grad_node, grad_pair, grad_tri, grad_vecs), 'grp')  7.59 us
    dot_general x11, matrix products, dot32(): return jnp.dot(a, b, precision=highest)  6.94 us
    psum x2, blocking collectives, shards(): lax.psum((jnp.sum(weight * (root - 1.0)), jnp.sum(weight)), 'grp')  6.59 us
    reduce_sum x3, other arithmetic, factored(): jnp.mean(weight * weight, axis=(-2, -1), keepdims=True)  6.33 us
    sub x3, other arithmetic, factored(): return (row_new, col_new, weight - 0.3 * scale * step)  6.19 us
  transfers between devices with their start and end apart: 2, of which 2 were waited for; matrix products, arithmetic and copies ran while one was open for 10% of the time, Pallas kernels for 0%

profile of v1, /device:TPU:0, one launch (start us, length us, event | category | flops | bytes accessed | tf_op | source)
XLA Modules:
  0.0 173.3 jit_solution(11444761738797684978)
XLA Ops:
  7.2 1.1 convert_reduce_fusion
  8.4 1.0 fusion.82
  9.4 2.6 %multiply_convert_fusion.6 = bf16[23,1280]{1,0:T(8,128)(2,1)S(1)} fusion(bf16[2,1280,1280]{2,1,0:T(8,128)(2,1)} %param.27, bf16[23,1280]{1,0:T(8,128)(2,1)} %param.26, f32[23]{0:T(128)S(1)} %add_rsqrt_fusion.3, f32[23]{0:T(128)S(1)} %broadcast_multiply_fusion.9), kind=kOutput, calls=%fused_computation.154 | convolution fusion | flops 75631360 | bytes 3397304 | tf_op jit(solution)/shard_map/dot_general | solution.py:68
  12.0 2.6 %fusion.2 = f32[23,1280]{1,0:T(8,128)S(1)} fusion(bf16[2,1280,1280]{2,1,0:T(8,128)(2,1)} %param.27, bf16[23,1280]{1,0:T(8,128)(2,1)S(1)} %copy-done.6, f32[23]{0:T(128)S(1)} %add_rsqrt_fusion.3, f32[23]{0:T(128)S(1)} %broadcast_multiply_fusion.9), kind=kOutput, calls=%fused_computation.2 | convolution fusion | flops 75484160 | bytes 3453624 | tf_op jit(solution)/shard_map/dot_general | solution.py:67
  16.4 1.2 fusion.145
  19.0 2.4 %multiply_reduce_fusion.5 = (f32[6]{0:T(128)}, bf16[6,128,128]{2,1,0:T(8,128)(2,1)}) fusion(f32[6,128,128]{2,1,0:T(8,128)} %param.33), kind=kLoop, calls=%fused_computation.42 | loop fusion | flops 294906 | bytes 589848 | tf_op jit(solution)/shard_map/reduce_sum | solution.py:35
  21.9 1.7 multiply_reduce_fusion.12
  24.1 0.9 multiply_reduce_fusion.2
  25.7 16.1 %all-reduce.5.cloned.1.call-done = f32[23,1280]{1,0:T(8,128)} async-done(((f32[23,1280]{1,0:T(8,128)}), f32[23,1280]{1,0:T(8,128)}) %all-reduce.5.cloned.1.call-update) | async-done | bytes 117776 | tf_op jit(solution)/shard_map/psum | solution.py:78
  41.8 1.1 fusion.89
  42.9 1.1 multiply_reduce_fusion.14
  44.0 1.0 multiply_convert_fusion.5
  45.0 1.5 convolution_convert_fusion
  47.5 1.2 convolution_bitcast_fusion
  48.7 1.1 copy-done.2
  49.8 0.9 convert_multiply_fusion
  50.7 2.2 %copy.160 = bf16[23,23,128]{0,1,2:T(8,128)(2,1)} copy(bf16[23,23,128]{2,1,0:T(8,128)(2,1)} %get-tuple-element.131) | data formatting | bytes 270848 | tf_op jit(solution)/shard_map/convert_element_type | solution.py:94
  52.9 2.6 %copy.150 = f32[23,23,128]{1,0,2:T(8,128)} copy(f32[23,23,128]{2,1,0:T(8,128)} %get-tuple-element.129) | data formatting | bytes 541696 | tf_op jit(solution)/shard_map/mul | solution.py:95
  55.5 4.4 %bitcast_reduce_fusion = (f32[23,23]{0,1:T(8,128)S(1)}, f32[128,23,23]{2,1,0:T(8,128)}) fusion(bf16[23,23,128]{0,1,2:T(8,128)(2,1)} %copy.160, f32[23,23,128]{1,0,2:T(8,128)} %copy.150), kind=kOutput, calls=%fused_computation.8 | convolution fusion | flops 18755696 | bytes 679236 | tf_op jit(solution)/shard_map/ikc,jkc->ijc/dot_general | solution.py:95
  59.9 2.6 %copy.151 = f32[128,23,23]{0,1,2:T(8,128)} copy(f32[128,23,23]{2,1,0:T(8,128)} %get-tuple-element.149) | data formatting | bytes 541696 | tf_op jit(solution)/shard_map/ikc,jkc->ijc/dot_general | solution.py:95
  64.0 1.2 multiply_reduce_fusion.9
  65.2 1.3 fusion.93
  66.5 2.6 %fusion.91 = f32[1,23,23]{2,0,1:T(1,128)S(1)} fusion(f32[23,23,128]{2,1,0:T(8,128)S(1)} %fusion.93, f32[23,128]{1,0:T(8,128)S(1)} %fusion.88, f32[23,128]{1,0:T(8,128)S(1)} %fusion.87, f32[128]{0:T(128)} %copy-done.30, f32[23,23]{1,0:T(8,128)S(1)} %copy.144, f32[4,128]{1,0:T(4,128)} %param.34, f32[5,23,23,128]{3,2,0,1:T(8,128)} %copy-done.2), kind=kOutput, calls=%fused_computation.161 | convolution fusion | flops 1354240 | bytes 582280 | tf_op jit(solution)/shard_map/ijc,c->ij/dot_general | solution.py:100
  69.8 1.1 multiply_reduce_fusion.3
  70.8 0.9 fusion.47
  71.8 3.3 %psum.51 = f32[]{:T(128)} all-reduce(f32[]{:T(128)} %get-tuple-element.114), channel_id=1, replica_groups=mesh['grp'=2,'row'=8,'head'=2] {'grp'}, use_global_device_ids=true, to_apply=%region_16.17 | all-reduce | flops 1 | bytes 8 | tf_op jit(solution)/shard_map/psum | solution.py:109
  75.1 1.6 fusion.9
  76.7 1.9 %multiply_reduce_fusion.6 = (f32[128]{0:T(128)}, f32[23,23,128]{2,1,0:T(8,128)S(1)}) fusion(f32[128,23,23]{0,1,2:T(8,128)} %copy.151, f32[23,23]{1,0:T(8,128)} %copy-done.15, f32[23,23]{1,0:T(8,128)S(1)} %broadcast_multiply_fusion.4, bf16[6,128,128]{2,1,0:T(8,128)(2,1)} %get-tuple-element.133, f32[128]{0:T(128)} %get-tuple-element.140, ...), kind=kOutput, calls=%fused_computation.88 | convolution fusion | flops 18011264 | bytes 886408 | tf_op jit(solution)/shard_map/ijd,cd->ijc/dot_general | solution.py:120
  79.0 1.1 subtract_multiply_fusion
  80.1 2.6 %copy.161 = f32[23,23,128]{1,0,2:T(8,128)} copy(f32[23,23,128]{2,1,0:T(8,128)} %subtract_multiply_fusion) | data formatting | bytes 541696 | tf_op jit(solution)/shard_map/mul | solution.py:19
  82.7 4.2 %fusion.146 = f32[128,23,23]{2,1,0:T(8,128)} fusion(bf16[23,23,128]{0,1,2:T(8,128)(2,1)} %copy.160, f32[23,23,128]{1,0,2:T(8,128)} %copy.161), kind=kOutput, calls=%fused_computation.263 | convolution fusion | flops 18688512 | bytes 677120 | tf_op jit(solution)/shard_map/ijc,jkc->ikc/dot_general | solution.py:123
  86.8 2.6 %copy.162 = f32[128,23,23]{0,1,2:T(8,128)} copy(f32[128,23,23]{2,1,0:T(8,128)} %fusion.146) | data formatting | bytes 541696 | tf_op jit(solution)/shard_map/ijc,jkc->ikc/dot_general | solution.py:123
  89.5 1.8 %fusion.65 = bf16[5,23,23,128]{3,2,1,0:T(8,128)(2,1)} fusion(f32[128,23,23]{0,1,2:T(8,128)} %copy.162, f32[23]{0:T(128)} %convert_reduce_fusion.1, f32[5,23,23,128]{3,2,0,1:T(8,128)} %copy-done.2), kind=kLoop, calls=%fused_computation.134 | loop fusion | flops 406271 | bytes 683100
  91.3 1.9 %fusion.63 = bf16[5,23,23,128]{3,2,1,0:T(8,128)(2,1)} fusion(bf16[5,23,23,128]{3,2,1,0:T(8,128)(2,1)} %fusion.65, f32[5,23,23,128]{3,2,0,1:T(8,128)} %copy-done.2, f32[128,23,23]{0,1,2:T(8,128)} %copy.162, f32[23]{0:T(128)} %convert_reduce_fusion.1), kind=kLoop, calls=%fused_computation.132 | loop fusion | flops 609408 | bytes 989696
  93.2 2.2 %copy.163 = bf16[23,23,128]{0,1,2:T(8,128)(2,1)} copy(bf16[23,23,128]{2,1,0:T(8,128)(2,1)} %get-tuple-element.130) | data formatting | bytes 270848 | tf_op jit(solution)/shard_map/convert_element_type | solution.py:93
  95.4 4.2 %fusion.147 = f32[128,23,23]{2,1,0:T(8,128)} fusion(bf16[23,23,128]{0,1,2:T(8,128)(2,1)} %copy.163, f32[23,23,128]{1,0,2:T(8,128)} %copy.161), kind=kOutput, calls=%fused_computation.264 | convolution fusion | flops 18688512 | bytes 677120 | tf_op jit(solution)/shard_map/ijc,ikc->jkc/dot_general | solution.py:124
  99.6 2.6 %copy.165 = f32[128,23,23]{0,1,2:T(8,128)} copy(f32[128,23,23]{2,1,0:T(8,128)} %fusion.147) | data formatting | bytes 541696 | tf_op jit(solution)/shard_map/ijc,ikc->jkc/dot_general | solution.py:124
  102.2 1.9 %fusion.69 = bf16[5,23,23,128]{3,2,1,0:T(8,128)(2,1)} fusion(bf16[5,23,23,128]{3,2,1,0:T(8,128)(2,1)} %fusion.63, f32[128,23,23]{0,1,2:T(8,128)} %copy.165, f32[23]{0:T(128)} %convert_reduce_fusion.1, f32[5,23,23,128]{3,2,0,1:T(8,128)} %copy-done.2), kind=kLoop, calls=%fused_computation.138 | loop fusion | flops 406272 | bytes 707072
  104.1 1.9 %fusion.67 = bf16[5,23,23,128]{3,2,1,0:T(8,128)(2,1)} fusion(bf16[5,23,23,128]{3,2,1,0:T(8,128)(2,1)} %fusion.69, f32[5,23,23,128]{3,2,0,1:T(8,128)} %copy-done.2, f32[128,23,23]{0,1,2:T(8,128)} %copy.165, f32[23]{0:T(128)} %convert_reduce_fusion.1), kind=kLoop, calls=%fused_computation.136 | loop fusion | flops 609408 | bytes 989696
  106.1 1.8 %fusion.72 = bf16[5,23,23,128]{3,2,1,0:T(8,128)(2,1)} fusion(bf16[5,23,23,128]{3,2,1,0:T(8,128)(2,1)} %fusion.67, f32[23,23,128]{2,1,0:T(8,128)S(1)} %copy-done.8, f32[128]{0:T(128)S(1)} %copy-done.47, f32[23,23]{1,0:T(8,128)S(1)} %copy-done.26, f32[5,23,23,128]{3,2,0,1:T(8,128)} %copy-done.2), kind=kLoop, calls=%fused_computation.140 | loop fusion | flops 609408 | bytes 697412 | tf_op jit(solution)/shard_map/stack | solution.py:125
  107.9 2.1 %fusion.31 = (f32[128]{0:T(128)}, f32[23,23,128,1]{2,1,0,3:T(8,128)S(1)}) fusion(f32[23,23]{1,0:T(8,128)S(1)} %add_rsqrt_fusion.1, f32[23,23]{1,0:T(8,128)S(1)} %broadcast_multiply_fusion.5, f32[23,128]{1,0:T(8,128)S(1)} %fusion.88, f32[23,128]{1,0:T(8,128)S(1)} %fusion.87, f32[128]{0:T(128)S(1)} %copy-done.31, f32[23,23]{1,0:T(8,128)S(1)} %copy.144, ...), kind=kOutput, calls=%fused_computation.70 | convolution fusion | flops 87145216 | bytes 1174272 | tf_op jit(solution)/shard_map/mijd,mcd->ijc/dot_general | solution.py:135
  111.5 1.5 convolution_bitcast_fusion.4
  113.1 1.8 %convolution_bitcast_fusion.1 = f32[5,128,128]{1,2,0:T(8,128)S(1)} fusion(bf16[5,23,23,128]{3,2,1,0:T(8,128)(2,1)} %fusion.72, f32[128]{0:T(128)S(1)} %copy-done.41, f32[23,23]{1,0:T(8,128)S(1)} %add_rsqrt_fusion.1, f32[23,23]{1,0:T(8,128)S(1)} %broadcast_multiply_fusion.5, f32[23,128]{1,0:T(8,128)S(1)} %fusion.88, f32[23,128]{1,0:T(8,128)S(1)} %fusion.87, ...), kind=kOutput, calls=%fused_computation.15 | convolution fusion | flops 87145344 | bytes 1035724 | tf_op jit(solution)/shard_map/ijc,mijd->mcd/dot_general | solution.py:134
  115.3 1.8 %fusion.148 = f32[1280,256]{1,0:T(8,128)} fusion(bf16[23,1280]{1,0:T(8,128)(2,1)S(1)} %multiply_convert_fusion.5, f32[23,256]{1,0:T(8,128)S(1)} %convolution_add_fusion), kind=kOutput, calls=%fused_computation.265 | convolution fusion | flops 90439680 | bytes 1393152 | tf_op jit(solution)/shard_map/dot_general | solution.py:50
  117.8 0.8 pad_maximum_fusion
  118.7 2.3 %multiply_reduce_fusion.1 = f32[]{:T(128)} fusion(f32[1280,256]{1,0:T(8,128)} %param.31), kind=kLoop, calls=%fused_computation.13 | loop fusion | flops 655359 | bytes 1310724 | tf_op jit(solution)/shard_map/reduce_sum | solution.py:35
  121.0 1.9 %copy.167 = f32[6,128,128]{1,2,0:T(8,128)} copy(f32[6,128,128]{2,1,0:T(8,128)} %param.33) | data formatting | bytes 786432 | tf_op args[12]
  125.1 1.7 %convolution_bitcast_fusion.6 = f32[1,128]{1,0:T(1,128)S(1)} fusion(f32[23,23,1]{1,2,0:T(1,128)S(1)} %copy.175, f32[23,23,128,1]{2,1,0,3:T(8,128)} %copy-done.9, f32[23,23]{1,0:T(8,128)S(1)} %copy-done.22, f32[23,23]{1,0:T(8,128)S(1)} %copy-done.24, f32[128]{0:T(128)S(1)} %copy-done.48, f32[23,23]{1,0:T(8,128)S(1)} %copy-done.27, f32[128]{0:T(128)S(1)} %copy-done.42, ...), kind=kOutput, calls=%fused_computation.28 | convolution fusion | flops 1625088 | bytes 311260 | tf_op jit(solution)/shard_map/ij,ijc->c/dot_general | solution.py:138
  126.8 1.6 convolution_bitcast_fusion.5
  128.4 3.3 %all-reduce = (f32[]{:T(128)}, f32[4,128]{1,0:T(4,128)S(1)}) all-reduce(f32[]{:T(128)} %get-tuple-element.115, f32[4,128]{1,0:T(4,128)S(1)} %pad_maximum_fusion.2), channel_id=1, replica_groups=mesh['grp'=2,'row'=8,'head'=2] {'grp'}, use_global_device_ids=true, to_apply=%region_14.15 | all-reduce | flops 513 | bytes 4104 | tf_op jit(solution)/shard_map/psum | solution.py:109
  132.5 7.6 %all-reduce.7.cloned.1.call-done = (f32[1280,256]{1,0:T(8,128)}, f32[2,256,128]{2,1,0:T(8,128)}, f32[6,128,128]{1,2,0:T(8,128)}) async-done(((f32[1280,256]{1,0:T(8,128)}, f32[2,256,128]{2,1,0:T(8,128)}, f32[6,128,128]{1,2,0:T(8,128)}), (f32[1280,256]{1,0:T(8,128)}, f32[2,256,128]{2,1,0:T(8,128)}, f32[6,128,128]{1,2,0:T(8,128)})) %all-reduce.7.cloned.1.call-update) | async-done | bytes 1966096 | tf_op jit(solution)/shard_map/psum | solution.py:147
  140.1 1.9 %copy.168 = f32[6,128,128]{2,1,0:T(8,128)} copy(f32[6,128,128]{1,2,0:T(8,128)} %get-tuple-element.120) | data formatting | bytes 786432
  142.0 1.8 %fusion.11 = (f32[6,128]{1,0:T(8,128)}, f32[6,128]{1,0:T(8,128)S(1)}) fusion(f32[6,128,128]{1,2,0:T(8,128)} %get-tuple-element.120), kind=kLoop, calls=%fused_computation.44 | loop fusion | flops 391680 | bytes 399360 | tf_op jit(solution)/shard_map/reduce_sum | solution.py:30
  143.8 1.6 fusion.7
  145.4 1.3 fusion.143
  148.1 2.4 %multiply_reduce_fusion = f32[]{:T(128)} fusion(f32[1280,256]{1,0:T(8,128)} %get-tuple-element.159, f32[]{:T(128)S(6)} %div.221, f32[256]{0:T(256)S(1)} %multiply_add_fusion.10, f32[1280]{0:T(1024)S(1)} %get-tuple-element.160), kind=kLoop, calls=%fused_computation.11 | loop fusion | flops 1638399 | bytes 1316872 | tf_op jit(solution)/shard_map/reduce_sum | solution.py:33
  151.3 0.8 fusion.142
  153.6 0.8 fusion.141
  155.2 1.3 multiply_reduce_fusion.4
  156.5 2.1 %multiply_subtract_fusion.1 = f32[6,128,128]{1,2,0:T(8,128)} fusion(f32[6,128,128]{1,2,0:T(8,128)} %copy.167, f32[6]{0:T(128)S(1)} %sqrt_maximum_fusion.1, f32[6]{0:T(128)} %maximum_multiply_fusion.1, f32[6,128,128]{1,2,0:T(8,128)} %get-tuple-element.120, f32[6]{0:T(128)S(1)} %broadcast_multiply_fusion.6, f32[6,128]{1,0:T(8,128)S(1)} %multiply_add_fusion.5, ...), kind=kLoop, calls=%fused_computation.39 | loop fusion | flops 589824 | bytes 1185864 | tf_op jit(solution)/shard_map/sub | solution.py:36
  158.5 1.9 %copy.169 = f32[6,128,128]{2,1,0:T(8,128)} copy(f32[6,128,128]{1,2,0:T(8,128)} %multiply_subtract_fusion.1) | data formatting | bytes 786432
  160.5 3.3 %multiply_subtract_fusion = f32[1280,256]{1,0:T(8,128)} fusion(f32[1280,256]{1,0:T(8,128)} %param.31, f32[]{:T(128)S(6)} %max.67, f32[]{:T(128)S(6)} %mul.638, f32[1280,256]{1,0:T(8,128)} %get-tuple-element.159, f32[]{:T(128)S(6)} %div.221, f32[256]{0:T(256)} %copy-done.40, f32[1280]{0:T(1024)S(1)} %get-tuple-element.160), kind=kLoop, calls=%fused_computation.10 | loop fusion | flops 1966080 | bytes 3938316 | tf_op jit(solution)/shard_map/sub | solution.py:36
  163.8 0.9 multiply_subtract_fusion.2
  164.7 1.1 copy.218
  (194 shorter events, 15.6 us)
Async XLA Ops:
  7.2 9.2 %copy-start = (bf16[1280,1280]{1,0:T(8,128)(2,1)S(1)}, bf16[1280,1280]{1,0:T(8,128)(2,1)}, u32[]{:S(2)}) copy-start(bf16[1280,1280]{1,0:T(8,128)(2,1)} %param.30) | copy-start | bytes 9830404
  7.2 34.6 %all-reduce.5.cloned.1.call-start = ((), (), s32[]{:S(2)}) async-start(), calls=%async_computation | async-start | bytes 245760 | tf_op jit(solution)/shard_map/psum | solution.py:78
  9.4 2.6 %copy-start.6 = (bf16[23,1280]{1,0:T(8,128)(2,1)S(1)}, bf16[23,1280]{1,0:T(8,128)(2,1)}, u32[]{:S(2)}) copy-start(bf16[23,1280]{1,0:T(8,128)(2,1)} %param.26) | copy-start | bytes 176644
  12.0 3.3 %copy-start.13 = (bf16[1280,256]{1,0:T(8,128)(2,1)S(1)}, bf16[1280,256]{1,0:T(8,128)(2,1)}, u32[]{:S(2)}) copy-start(bf16[1280,256]{1,0:T(8,128)(2,1)} %param.28) | copy-start | bytes 1966084
  12.0 3.5 %copy-start.49 = (f32[4,256]{1,0:T(4,128)S(1)}, f32[4,256]{1,0:T(4,128)}, u32[]{:S(2)}) copy-start(f32[4,256]{1,0:T(4,128)} %param.29) | copy-start | bytes 12292
  12.0 3.6 %copy-start.63 = (s32[1,256]{1,0:T(1,128)S(1)}, s32[1,256]{1,0:T(1,128)}, u32[]{:S(2)}) copy-start(s32[1,256]{1,0:T(1,128)} %param.21) | copy-start | bytes 3076
  15.9 9.1 %copy-start.18 = (f32[23,23]{0,1:T(8,128)}, f32[23,23]{0,1:T(8,128)S(1)}, u32[]{:S(2)}) copy-start(f32[23,23]{0,1:T(8,128)S(1)} %get-tuple-element.147) | copy-start | bytes 6352
  16.4 1.3 copy-start.54
  16.4 2.6 %copy-start.50 = (f32[1,3,256]{2,0,1:T(1,128)S(1)}, f32[1,3,256]{2,0,1:T(1,128)}, u32[]{:S(2)}) copy-start(f32[1,3,256]{2,0,1:T(1,128)} %param.25) | copy-start | bytes 9220
  16.4 4.9 %copy-start.35 = (f32[4,128]{1,0:T(4,128)S(1)}, f32[4,128]{1,0:T(4,128)}, u32[]{:S(2)}) copy-start(f32[4,128]{1,0:T(4,128)} %param.34) | copy-start | bytes 6148
  17.6 122.5 %all-reduce.7.cloned.1.call-start = ((), (), s32[]{:S(2)}) async-start(), calls=%async_computation.1 | async-start | bytes 3932160 | tf_op jit(solution)/shard_map/psum | solution.py:147
  21.9 25.3 %copy-start.30 = (f32[128]{0:T(128)}, f32[128]{0:T(128)S(1)}, u32[]{:S(2)}) copy-start(f32[128]{0:T(128)S(1)} %get-tuple-element.143) | copy-start | bytes 1540
  41.8 5.6 %copy-start.11 = (bf16[6,128,128]{2,1,0:T(8,128)(2,1)S(1)}, bf16[6,128,128]{2,1,0:T(8,128)(2,1)}, u32[]{:S(2)}) copy-start(bf16[6,128,128]{2,1,0:T(8,128)(2,1)} %get-tuple-element.133) | copy-start | bytes 589828
  45.0 4.8 %copy-start.37 = (f32[23]{0:T(128)S(1)}, f32[23]{0:T(128)}, u32[]{:S(2)}) copy-start(f32[23]{0:T(128)} %convert_reduce_fusion.1) | copy-start | bytes 280
  48.7 1.1 copy-start.2
  63.2 6.0 %copy-start.64 = (s32[1,256]{1,0:T(1,128)S(1)}, s32[1,256]{1,0:T(1,128)}, u32[]{:S(2)}) copy-start(s32[1,256]{1,0:T(1,128)} %param.21) | copy-start | bytes 3076
  63.2 6.6 %copy-start.14 = (f32[256,256]{1,0:T(8,128)S(1)}, f32[256,256]{1,0:T(8,128)}, u32[]{:S(2)}) copy-start(f32[256,256]{1,0:T(8,128)} %multiply_reduce_fusion.2) | copy-start | bytes 786436
  63.2 6.6 %copy-start.55 = (f32[1,256]{1,0:T(1,128)S(1)}, f32[1,256]{1,0:T(1,128)}, u32[]{:S(2)}) copy-start(f32[1,256]{1,0:T(1,128)} %compare_select_fusion.2) | copy-start | bytes 3076
  63.2 6.6 %copy-start.56 = (f32[256]{0:T(256)S(1)}, f32[256]{0:T(256)}, u32[]{:S(2)}) copy-start(f32[256]{0:T(256)} %select_multiply_fusion) | copy-start | bytes 3076
  65.2 5.6 %copy-start.15 = (f32[23,23]{1,0:T(8,128)}, f32[23,23]{1,0:T(8,128)S(1)}, u32[]{:S(2)}) copy-start(f32[23,23]{1,0:T(8,128)S(1)} %add_rsqrt_fusion) | copy-start | bytes 6352
  66.5 5.3 %copy-start.7 = (f32[23,23,128]{2,1,0:T(8,128)}, f32[23,23,128]{2,1,0:T(8,128)S(1)}, u32[]{:S(2)}) copy-start(f32[23,23,128]{2,1,0:T(8,128)S(1)} %fusion.93) | copy-start | bytes 812548
  75.0 3.5 %copy-start.3 = (f32[128,23,23]{0,1,2:T(8,128)S(1)}, f32[128,23,23]{0,1,2:T(8,128)}, u32[]{:S(2)}) copy-start(f32[128,23,23]{0,1,2:T(8,128)} %copy.151) | copy-start | bytes 812548
  75.1 3.5 %copy-start.16 = (f32[23,23]{1,0:T(8,128)S(1)}, f32[23,23]{1,0:T(8,128)}, u32[]{:S(2)}) copy-start(f32[23,23]{1,0:T(8,128)} %copy-done.15) | copy-start | bytes 6352
  75.1 3.5 %copy-start.45 = (f32[128]{0:T(128)S(1)}, f32[128]{0:T(128)}, u32[]{:S(2)}) copy-start(f32[128]{0:T(128)} %get-tuple-element.141) | copy-start | bytes 1540
  76.6 2.3 %copy-start.25 = (f32[23,23]{1,0:T(8,128)}, f32[23,23]{1,0:T(8,128)S(1)}, u32[]{:S(2)}) copy-start(f32[23,23]{1,0:T(8,128)S(1)} %fusion.9) | copy-start | bytes 6352
  102.2 3.9 %copy-start.8 = (f32[23,23,128]{2,1,0:T(8,128)S(1)}, f32[23,23,128]{2,1,0:T(8,128)}, u32[]{:S(2)}) copy-start(f32[23,23,128]{2,1,0:T(8,128)} %copy-done.7) | copy-start | bytes 812548
  102.2 3.9 %copy-start.26 = (f32[23,23]{1,0:T(8,128)S(1)}, f32[23,23]{1,0:T(8,128)}, u32[]{:S(2)}) copy-start(f32[23,23]{1,0:T(8,128)} %copy-done.25) | copy-start | bytes 6352
  102.2 3.9 %copy-start.47 = (f32[128]{0:T(128)S(1)}, f32[128]{0:T(128)}, u32[]{:S(2)}) copy-start(f32[128]{0:T(128)} %get-tuple-element.140) | copy-start | bytes 1540
  102.2 5.6 %copy-start.12 = (bf16[6,128,128]{2,1,0:T(8,128)(2,1)S(1)}, bf16[6,128,128]{2,1,0:T(8,128)(2,1)}, u32[]{:S(2)}) copy-start(bf16[6,128,128]{2,1,0:T(8,128)(2,1)} %get-tuple-element.133) | copy-start | bytes 589828
  102.2 5.6 %copy-start.31 = (f32[128]{0:T(128)S(1)}, f32[128]{0:T(128)}, u32[]{:S(2)}) copy-start(f32[128]{0:T(128)} %copy-done.30) | copy-start | bytes 1540
  104.1 5.8 %copy-start.41 = (f32[128]{0:T(128)S(1)}, f32[128]{0:T(128)}, u32[]{:S(2)}) copy-start(f32[128]{0:T(128)} %get-tuple-element.142) | copy-start | bytes 1540
  107.8 3.6 %copy-start.4 = (f32[128,23,23]{0,1,2:T(8,128)S(1)}, f32[128,23,23]{0,1,2:T(8,128)}, u32[]{:S(2)}) copy-start(f32[128,23,23]{0,1,2:T(8,128)} %copy.151) | copy-start | bytes 812548
  107.9 3.6 %copy-start.17 = (f32[23,23]{1,0:T(8,128)S(1)}, f32[23,23]{1,0:T(8,128)}, u32[]{:S(2)}) copy-start(f32[23,23]{1,0:T(8,128)} %copy-done.15) | copy-start | bytes 6352
  107.9 3.6 %copy-start.46 = (f32[128]{0:T(128)S(1)}, f32[128]{0:T(128)}, u32[]{:S(2)}) copy-start(f32[128]{0:T(128)} %get-tuple-element.141) | copy-start | bytes 1540
  110.0 3.1 %copy-start.9 = (f32[23,23,128,1]{2,1,0,3:T(8,128)}, f32[23,23,128,1]{2,1,0,3:T(8,128)S(1)}, u32[]{:S(2)}) copy-start(f32[23,23,128,1]{2,1,0,3:T(8,128)S(1)} %get-tuple-element.154) | copy-start | bytes 812548
  118.6 4.3 %copy-start.19 = (f32[23,23]{0,1:T(8,128)S(1)}, f32[23,23]{0,1:T(8,128)}, u32[]{:S(2)}) copy-start(f32[23,23]{0,1:T(8,128)} %copy-done.18) | copy-start | bytes 6352
  118.6 5.1 %copy-start.36 = (f32[4,128]{1,0:T(4,128)S(1)}, f32[4,128]{1,0:T(4,128)}, u32[]{:S(2)}) copy-start(f32[4,128]{1,0:T(4,128)} %param.34) | copy-start | bytes 6148
  118.7 5.2 %copy-start.57 = (f32[2]{0:T(128)S(1)}, f32[2]{0:T(128)}, u32[]{:S(2)}) copy-start(f32[2]{0:T(128)} %get-tuple-element.134) | copy-start | bytes 28
  118.7 5.7 %copy-start.60 = (f32[6]{0:T(128)S(1)}, f32[6]{0:T(128)}, u32[]{:S(2)}) copy-start(f32[6]{0:T(128)} %get-tuple-element.132) | copy-start | bytes 76
  118.7 6.3 %copy-start.22 = (f32[23,23]{1,0:T(8,128)S(1)}, f32[23,23]{1,0:T(8,128)}, u32[]{:S(2)}) copy-start(f32[23,23]{1,0:T(8,128)} %copy-done.21) | copy-start | bytes 6352
  118.7 6.3 %copy-start.24 = (f32[23,23]{1,0:T(8,128)S(1)}, f32[23,23]{1,0:T(8,128)}, u32[]{:S(2)}) copy-start(f32[23,23]{1,0:T(8,128)} %copy-done.23) | copy-start | bytes 6352
  118.7 6.3 %copy-start.27 = (f32[23,23]{1,0:T(8,128)S(1)}, f32[23,23]{1,0:T(8,128)}, u32[]{:S(2)}) copy-start(f32[23,23]{1,0:T(8,128)} %copy-done.25) | copy-start | bytes 6352
  118.7 6.3 %copy-start.32 = (f32[128]{0:T(128)S(1)}, f32[128]{0:T(128)}, u32[]{:S(2)}) copy-start(f32[128]{0:T(128)} %copy-done.30) | copy-start | bytes 1540
  118.7 6.3 %copy-start.42 = (f32[128]{0:T(128)S(1)}, f32[128]{0:T(128)}, u32[]{:S(2)}) copy-start(f32[128]{0:T(128)} %get-tuple-element.142) | copy-start | bytes 1540
  118.7 6.3 %copy-start.48 = (f32[128]{0:T(128)S(1)}, f32[128]{0:T(128)}, u32[]{:S(2)}) copy-start(f32[128]{0:T(128)} %get-tuple-element.140) | copy-start | bytes 1540
  123.0 5.4 %copy-start.58 = (f32[128]{0:T(128)S(1)}, f32[128]{0:T(128)}, u32[]{:S(2)}) copy-start(f32[128]{0:T(128)} %get-tuple-element.151) | copy-start | bytes 1540
  123.0 5.4 %copy-start.59 = (f32[128]{0:T(128)S(1)}, f32[128]{0:T(128)}, u32[]{:S(2)}) copy-start(f32[128]{0:T(128)} %get-tuple-element.153) | copy-start | bytes 1540
  123.0 8.8 %copy-start.51 = (f32[4,128]{1,0:T(4,128)S(1)}, f32[4,128]{1,0:T(4,128)}, u32[]{:S(2)}) copy-start(f32[4,128]{1,0:T(4,128)} %param.41) | copy-start | bytes 6148
  131.7 10.3 %copy-start.43 = (f32[4,128]{1,0:T(4,128)}, f32[4,128]{1,0:T(4,128)S(1)}, u32[]{:S(2)}) copy-start(f32[4,128]{1,0:T(4,128)S(1)} %get-tuple-element.171) | copy-start | bytes 6148
  131.9 10.2 %copy-start.44 = (f32[4,128]{1,0:T(4,128)}, f32[4,128]{1,0:T(4,128)S(1)}, u32[]{:S(2)}) copy-start(f32[4,128]{1,0:T(4,128)S(1)} %get-tuple-element.172) | copy-start | bytes 6148
  143.8 7.4 %copy-start.5 = (f32[2,256,128]{2,1,0:T(8,128)S(1)}, f32[2,256,128]{2,1,0:T(8,128)}, u32[]{:S(2)}) copy-start(f32[2,256,128]{2,1,0:T(8,128)} %get-tuple-element.163) | copy-start | bytes 786436
  146.7 13.7 %copy-start.20 = (f32[1280]{0:T(1024)}, f32[1280]{0:T(1024)S(1)}, u32[]{:S(2)}) copy-start(f32[1280]{0:T(1024)S(1)} %get-tuple-element.160) | copy-start | bytes 15364
  147.4 4.7 %copy-start.40 = (f32[256]{0:T(256)}, f32[256]{0:T(256)S(1)}, u32[]{:S(2)}) copy-start(f32[256]{0:T(256)S(1)} %multiply_add_fusion.10) | copy-start | bytes 3076
  152.1 2.3 %copy-start.33 = (f32[2,256]{1,0:T(2,128)}, f32[2,256]{1,0:T(2,128)S(1)}, u32[]{:S(2)}) copy-start(f32[2,256]{1,0:T(2,128)S(1)} %get-tuple-element.164) | copy-start | bytes 6148
  152.2 2.3 %copy-start.52 = (f32[2]{0:T(128)}, f32[2]{0:T(128)S(1)}, u32[]{:S(2)}) copy-start(f32[2]{0:T(128)S(1)} %broadcast_multiply_fusion.7) | copy-start | bytes 28
  154.4 9.3 %copy-start.28 = (f32[6,128]{1,0:T(8,128)}, f32[6,128]{1,0:T(8,128)S(1)}, u32[]{:S(2)}) copy-start(f32[6,128]{1,0:T(8,128)S(1)} %get-tuple-element.168) | copy-start | bytes 9220
  155.2 8.6 %copy-start.29 = (f32[6,128]{1,0:T(8,128)}, f32[6,128]{1,0:T(8,128)S(1)}, u32[]{:S(2)}) copy-start(f32[6,128]{1,0:T(8,128)S(1)} %multiply_add_fusion.5) | copy-start | bytes 9220
  160.4 3.3 %copy-start.10 = (f32[2,256,128]{2,1,0:T(8,128)S(1)}, f32[2,256,128]{2,1,0:T(8,128)}, u32[]{:S(2)}) copy-start(f32[2,256,128]{2,1,0:T(8,128)} %param.32) | copy-start | bytes 786436
  160.4 3.3 %copy-start.34 = (f32[2,256]{1,0:T(2,128)S(1)}, f32[2,256]{1,0:T(2,128)}, u32[]{:S(2)}) copy-start(f32[2,256]{1,0:T(2,128)} %copy-done.33) | copy-start | bytes 6148
  160.5 3.3 %copy-start.39 = (f32[2,128]{1,0:T(2,128)S(1)}, f32[2,128]{1,0:T(2,128)}, u32[]{:S(2)}) copy-start(f32[2,128]{1,0:T(2,128)} %copy-done.38) | copy-start | bytes 3076
  160.5 3.3 %copy-start.53 = (f32[2]{0:T(128)S(1)}, f32[2]{0:T(128)}, u32[]{:S(2)}) copy-start(f32[2]{0:T(128)} %copy-done.52) | copy-start | bytes 28
  160.5 3.3 %copy-start.61 = (f32[2]{0:T(128)S(1)}, f32[2]{0:T(128)}, u32[]{:S(2)}) copy-start(f32[2]{0:T(128)} %maximum_multiply_fusion.2) | copy-start | bytes 28
  160.5 3.3 %copy-start.62 = (f32[2]{0:T(128)S(1)}, f32[2]{0:T(128)}, u32[]{:S(2)}) copy-start(f32[2]{0:T(128)} %sqrt_maximum_fusion.2) | copy-start | bytes 28
  160.5 4.2 %copy-start.1 = (f32[1280,256]{1,0:T(8,128)S(1)}, f32[1280,256]{1,0:T(8,128)}, u32[]{:S(2)}) copy-start(f32[1280,256]{1,0:T(8,128)} %get-tuple-element.159) | copy-start | bytes 3932164
  (4 other events, 3.4 us)
Sparse Core Ops, SparseCore 0:
  17.8 24.0 all-reduce.4
  118.8 21.3 all-reduce.6

commit v2 on v1

v2 whole, which is shorter than its diff:
```python
import functools
import math

import jax
import jax.numpy as jnp
from jax import lax
from jax.experimental import pallas as pl
from jax.experimental.pallas import tpu as pltpu
from jax.sharding import PartitionSpec as P


STEP = 10
BETA = 1.0 - STEP ** (-0.8)
RATE = 0.3
MESH = pl.DeviceIdType.MESH
f32 = jnp.float32
bf16 = jnp.bfloat16
ROWS = 24
WIDE = 32


def dot(a, b):
    return jnp.dot(a, b, preferred_element_type=f32)


def dot_nt(a, b):
    return lax.dot_general(a, b, (((1,), (1,)), ((), ())), preferred_element_type=f32)


def dot_tn(a, b):
    return lax.dot_general(a, b, (((0,), (0,)), ((), ())), preferred_element_type=f32)


def silu(x):
    return x * jax.nn.sigmoid(x)


def mean_last(x):
    return jnp.mean(x, -1, keepdims=True)


def split(x, parts):
    out = []
    for _ in range(parts):
        part = x.astype(bf16)
        out.append(part)
        x = x - part.astype(f32)
    return out


def iota(shape, dim):
    return lax.broadcasted_iota(jnp.int32, shape, dim)


def tables_kernel(
    tokens_h, lengths_h, recycle_h, resolved_h, coords_h, embed_h, uv_h, qk_h, affine_h, out_h,
    w_in_h, w_pairin_h, w_tri_h, vecs_h,
    frozen_o, single_o, gtri_o, tail_o,
    tokens_v, lengths_s, recycle_s, resolved_v, coords_v, embed_v, uv_v, qk_v, affine_v, out_v,
    w_in_v, w_pairin_v, w_tri_v, vecs_v,
    emb, mixed, part, frozen_v, single_v, w_in_b, w_tri_b, cnt_b, true_d, cols,
    pair, sb, n1, s1, pnorm, proj, sig_l, sig_r, gate, left, right, upd, n2, s2, unorm,
    branch, final, dbranch, dwork, dleft, dright, dproj, stack_d, gtri_v, tail_v,
    load_sem, part_send, part_recv, peer_send, peer_recv, local_sem,
    *, heads, unit_chunk, col_chunk,
):
    grp = lax.axis_index("grp")
    head = lax.axis_index("head")
    other = 1 - grp
    seq = tokens_v.shape[1]
    units = uv_v.shape[2]
    width = emb.shape[1]
    chans = vecs_v.shape[1]
    vocab = embed_v.shape[0]
    n_unit = units // unit_chunk
    n_col = width // col_chunk

    loads = []

    def load(src, dst):
        copy = pltpu.make_async_copy(src, dst, load_sem.at[len(loads)])
        loads.append(copy)
        copy.start()
        return copy

    c_small = [
        load(embed_h, embed_v),
        load(tokens_h, tokens_v),
        load(lengths_h, lengths_s),
        load(recycle_h, recycle_s),
        load(affine_h, affine_v),
    ]
    c_qk = load(qk_h, qk_v)
    c_uv = []
    for c in range(n_unit):
        s = pl.ds(c * unit_chunk, unit_chunk)
        c_uv.append([load(uv_h.at[i, :, s], uv_v.at[i, :, s]) for i in range(2)])
    c_out = []
    for c in range(n_col):
        s = pl.ds(c * col_chunk, col_chunk)
        c_out.append(load(out_h.at[:, s], out_v.at[:, s]))
    c_pairs = [load(resolved_h, resolved_v), load(coords_h, coords_v)]
    c_par = [
        load(w_in_h, w_in_v),
        load(w_pairin_h, w_pairin_v),
        load(w_tri_h, w_tri_v),
        load(vecs_h, vecs_v),
    ]

    barrier = pltpu.get_barrier_semaphore()
    pl.semaphore_signal(barrier, inc=1, device_id={"grp": other}, device_id_type=MESH)
    for d in range(1, heads):
        peer = lax.rem(head + d, heads)
        pl.semaphore_signal(barrier, inc=1, device_id={"head": peer}, device_id_type=MESH)

    for c in c_small:
        c.wait()
    emb[...] = jnp.zeros_like(emb)
    emb[0:vocab, :] = embed_v[...].astype(f32)
    e = emb[...]
    centre = e - mean_last(e)
    normed = (centre * lax.rsqrt(mean_last(centre * centre) + 1e-05)).astype(bf16)

    length = lengths_s[0]
    recycle = recycle_s[0].astype(f32)
    tok = tokens_v[...]
    onehot = (iota((WIDE, seq), 0) == tok).astype(f32)
    key_ok = (iota((1, seq), 1) < length).astype(f32)
    one_b = onehot.astype(bf16)
    cnt_col = jnp.sum(onehot, -1, keepdims=True)
    cnt_b[...] = jnp.broadcast_to(cnt_col, (WIDE, chans))
    ones = jnp.ones((16, seq), bf16)
    cnt_row = dot_nt(ones, one_b)[0:1, :]
    key_row = dot_nt(ones, (onehot * key_ok).astype(bf16))[0:1, :]

    c_qk.wait()
    shared = silu(dot(normed, qk_v[...]))
    query = (shared * affine_v[0:1, :] + affine_v[1:2, :]).astype(bf16)
    keyed = (shared * affine_v[2:3, :] + affine_v[3:4, :]).astype(bf16)
    scores = dot_nt(query, keyed) / math.sqrt(qk_v.shape[1])
    masked = jnp.where(key_row > 0, scores, -1000000000.0)
    top = jnp.exp(masked - jnp.max(masked, -1, keepdims=True))
    attn = (top / jnp.sum(top * key_row, -1, keepdims=True)).astype(bf16).astype(f32)
    attn = jnp.concatenate(split(attn * key_row, 2), 0)

    for c in range(n_unit):
        s = slice(c * unit_chunk, (c + 1) * unit_chunk)
        c_uv[c][0].wait()
        ugate = silu(dot(normed, uv_v[0, :, s]))
        c_uv[c][1].wait()
        value = silu(dot(normed, uv_v[1, :, s])).astype(bf16)
        seen = dot(attn, value)
        mixed[:, s] = (ugate * (seen[0:WIDE] + seen[WIDE : 2 * WIDE])).astype(bf16)

    pl.semaphore_wait(barrier, heads)

    half = col_chunk // 2
    sends = []
    for c in range(n_col):
        s = slice(c * col_chunk, (c + 1) * col_chunk)
        c_out[c].wait()
        p = dot(mixed[...], out_v[:, s])
        part[head, c, :, 0:col_chunk] = p[0:16].astype(bf16)
        part[head, c, :, col_chunk : col_chunk + half] = jnp.concatenate(
            [p[16:24, 0:half], p[16:24, half:col_chunk]], 0
        ).astype(bf16)
        for d in range(1, heads):
            copy = pltpu.make_async_remote_copy(
                src_ref=part.at[head, c],
                dst_ref=part.at[head, c],
                send_sem=part_send.at[d - 1, c],
                recv_sem=part_recv.at[head, c],
                device_id={"head": lax.rem(head + d, heads)},
                device_id_type=MESH,
            )
            copy.start()
            sends.append(copy)

    for c in c_pairs + c_par:
        c.wait()
    w_in_b[...] = w_in_v[...].astype(bf16)
    for m in range(6):
        w_tri_b[:, m * chans : (m + 1) * chans] = w_tri_v[m].astype(bf16)
    valid = key_ok * (resolved_v[...] > 0).astype(f32)
    cols[...] = jnp.zeros_like(cols)
    cols[0:3, :] = coords_v[0]
    cols[3:4, :] = valid
    one_v = (onehot * valid).astype(bf16)
    weight_j = recycle * valid
    blk = 128
    n_blk = seq // blk
    places = []
    for b in range(n_blk):
        t = cols[:, b * blk : (b + 1) * blk].T
        places.append(t)
        d2 = None
        for k in range(3):
            delta = t[:, k : k + 1] - cols[k : k + 1, :]
            d2 = delta * delta if d2 is None else d2 + delta * delta
        true_d[b * blk : (b + 1) * blk, :] = jnp.sqrt(d2)
    n_valid = jnp.sum(valid, -1, keepdims=True)
    loss_count = recycle * n_valid * n_valid

    present = cnt_b[0:ROWS, :] > 0
    sc = jnp.where((cnt_row > 0) & (cnt_col > 0), scores, 0.0)[0:ROWS]

    for c in range(n_col):
        for d in range(1, heads):
            peer = lax.rem(head + d, heads)
            pltpu.make_async_remote_copy(
                src_ref=part.at[peer, c],
                dst_ref=part.at[peer, c],
                send_sem=part_send.at[d - 1, c],
                recv_sem=part_recv.at[peer, c],
                device_id={"head": peer},
                device_id_type=MESH,
            ).wait_recv()
        s = slice(c * col_chunk, (c + 1) * col_chunk)
        low = None
        for k in range(heads):
            a = part[k, c, :, 0:col_chunk].astype(f32)
            b = part[k, c, :, col_chunk : col_chunk + half].astype(f32)
            b = jnp.concatenate([b[0:8], b[8:16]], 1)
            low = [a, b] if low is None else [low[0] + a, low[1] + b]
        emb[0:16, s] += low[0]
        emb[16:24, s] += low[1]
    state = emb[0:ROWS, :]
    centre = state - mean_last(state)
    frozen = centre * lax.rsqrt(mean_last(centre * centre) + 1e-05)
    frozen_v[...] = jnp.concatenate([frozen, jnp.zeros((WIDE - ROWS, width), f32)], 0).astype(bf16)

    peers = []

    def give(src, dst):
        k = len(peers)
        away = pltpu.make_async_remote_copy(
            src_ref=src,
            dst_ref=dst,
            send_sem=peer_send.at[k],
            recv_sem=peer_recv.at[k],
            device_id={"grp": other},
            device_id_type=MESH,
        )
        away.start()
        here = pltpu.make_async_copy(src, dst, local_sem.at[k])
        here.start()
        peers.append((away, here))

    give(frozen_v, frozen_o.at[grp])
    single = dot(frozen_v[...], w_in_b[...]).astype(bf16)
    single_v[...] = single[0:ROWS].astype(f32)
    give(single_v, single_o.at[grp])
    side_a = dot(single, w_pairin_v[0].astype(bf16))[0:ROWS]
    side_b = dot(single, w_pairin_v[1].astype(bf16))[0:ROWS]
    side_a = jnp.where(present, side_a, 0.0)
    side_b = jnp.where(present, side_b, 0.0)
    v0 = vecs_v[0:1, :]
    v1 = vecs_v[1:2, :]
    v2 = vecs_v[2:3, :]
    v3 = vecs_v[3:4, :]
    v0c = v0 - mean_last(v0)
    side_ac = side_a - mean_last(side_a)
    side_bc = side_b - mean_last(side_b)

    n_chunk = ROWS // 2
    two = 2 * ROWS

    def rows(k):
        return slice(k * two, (k + 1) * two)

    def both(f, k):
        return jnp.concatenate([f(2 * k), f(2 * k + 1)], 0)

    for k in range(n_chunk):
        r = rows(k)
        sbk = both(lambda u: jnp.broadcast_to(sc[:, u : u + 1], (ROWS, chans)), k)
        sb[r] = sbk
        pair[r] = sbk * v0 + both(lambda u: side_a + side_b[u : u + 1, :], k)
        centre = sbk * v0c + both(lambda u: side_ac + side_bc[u : u + 1, :], k)
        scale = lax.rsqrt(mean_last(centre * centre) + 1e-05)
        normal = centre * scale
        n1[r] = normal
        s1[r] = jnp.broadcast_to(scale, (two, chans))
        pnorm[r] = (normal * v1).astype(bf16)
    proj[...] = dot(pnorm[...], w_tri_b[:, 0 : 5 * chans])
    for k in range(n_chunk):
        r = rows(k)
        sl = jax.nn.sigmoid(proj[r, chans : 2 * chans])
        sr = jax.nn.sigmoid(proj[r, 3 * chans : 4 * chans])
        sig_l[r] = sl
        sig_r[r] = sr
        left[r] = (sl * proj[r, 0:chans]).astype(bf16).astype(f32)
        right[r] = (sr * proj[r, 2 * chans : 3 * chans]).astype(bf16).astype(f32)
        gate[r] = jax.nn.sigmoid(proj[r, 4 * chans : 5 * chans])
        dwork[r] = left[r] * both(
            lambda u: jnp.broadcast_to(cnt_b[u : u + 1, :], (ROWS, chans)), k
        )

    def triangle(dst, moving, fixed, row_of, weighted):
        group = 4
        for a0 in range(0, ROWS, group):
            total = [None] * group
            for b in range(vocab):
                x = moving(b)
                for q in range(group):
                    y = x * fixed[pl.ds(row_of(a0 + q, b), 1), :]
                    total[q] = y if total[q] is None else total[q] + y
            for q in range(group):
                a = a0 + q
                t = total[q]
                if weighted:
                    t = t * cnt_b[a : a + 1, :]
                dst[a * ROWS : (a + 1) * ROWS, :] = t

    triangle(
        upd, lambda u: dwork[u * ROWS : (u + 1) * ROWS, :], right, lambda v, u: u * ROWS + v, False
    )
    for k in range(n_chunk):
        r = rows(k)
        x = upd[r]
        centre = x - mean_last(x)
        scale = lax.rsqrt(mean_last(centre * centre) + 1e-05)
        normal = centre * scale
        n2[r] = normal
        s2[r] = jnp.broadcast_to(scale, (two, chans))
        unorm[r] = (normal * v2).astype(bf16)
    branch[...] = dot(unorm[...], w_tri_b[:, 5 * chans : 6 * chans])
    lane = iota((ROWS, chans), 1)
    logit = jnp.zeros((ROWS, chans), f32)
    for k in range(n_chunk):
        r = rows(k)
        fin = pair[r] + gate[r] * branch[r]
        final[r] = fin
        col = jnp.sum(fin * v3, -1, keepdims=True)
        for q in range(2):
            logit = jnp.where(lane == 2 * k + q, col[q * ROWS : (q + 1) * ROWS], logit)

    dist = jnp.maximum(logit, 0.0) + jnp.log1p(jnp.exp(-jnp.abs(logit)))
    dist = jnp.concatenate([dist, jnp.zeros((WIDE - ROWS, chans), f32)], 0)
    for k, d in enumerate(split(dist, 3)):
        stack_d[k * WIDE : (k + 1) * WIDE, :] = d
    by_col = dot(stack_d[:, 0:WIDE], one_b).astype(bf16)
    one3 = jnp.concatenate([one_b, one_b, one_b], 0)
    loss_row = jnp.zeros((1, seq), f32)
    by_first = jnp.zeros((WIDE, seq), f32)
    for b in range(n_blk):
        s = slice(b * blk, (b + 1) * blk)
        diff = dot_tn(one3[:, s], by_col) - true_d[s, :]
        sq = diff * diff + 1.0
        inv = lax.rsqrt(sq)
        loss_row = loss_row + jnp.sum(
            places[b][:, 3:4] * (sq * inv - 1.0), 0, keepdims=True
        )
        for q in split(diff * inv, 2):
            by_first = by_first + dot(one_v[:, s], q)
    loss = jnp.sum(loss_row * weight_j, -1, keepdims=True)
    by_pair = dot_nt(jnp.concatenate(split(by_first * weight_j, 2), 0), one_b)
    by_pair = (by_pair[0:WIDE] + by_pair[WIDE : 2 * WIDE])[0:ROWS]
    dlogit = by_pair * jax.nn.sigmoid(logit)[:, 0:WIDE]

    g_dist = jnp.zeros((two, chans), f32)
    for k in range(n_chunk):
        r = rows(k)
        g = both(lambda u: jnp.broadcast_to(dlogit[:, u : u + 1], (ROWS, chans)), k)
        g_dist = g_dist + g * final[r]
        dfinal = g * v3
        gt = gate[r]
        pair[r] = dfinal
        dbranch[r] = (dfinal * gt).astype(bf16)
        dproj[r, 4 * chans : 5 * chans] = (dfinal * branch[r] * gt * (1.0 - gt)).astype(bf16)
    dwork[...] = dot_nt(dbranch[...], w_tri_b[:, 5 * chans : 6 * chans])
    gtri_v[5] = dot_tn(unorm[...], dbranch[...])
    give(gtri_v.at[5], gtri_o.at[grp, 5])
    gtri_v[4] = dot_tn(pnorm[...], dproj[:, 4 * chans : 5 * chans])
    give(gtri_v.at[4], gtri_o.at[grp, 4])
    g_two = jnp.zeros((two, chans), f32)
    for k in range(n_chunk):
        r = rows(k)
        dn = dwork[r]
        normal = n2[r]
        g_two = g_two + dn * normal
        dn = dn * v2
        upd[r] = s2[r] * (dn - mean_last(dn) - normal * mean_last(dn * normal))
    triangle(
        dleft, lambda v: upd[v * ROWS : (v + 1) * ROWS, :], right, lambda u, v: u * ROWS + v, True
    )
    for k in range(n_chunk):
        r = rows(k)
        d, sl = dleft[r], sig_l[r]
        dproj[r, 0:chans] = (d * sl).astype(bf16)
        dproj[r, chans : 2 * chans] = (d * proj[r, 0:chans] * sl * (1.0 - sl)).astype(bf16)
    for m in range(2):
        gtri_v[m] = dot_tn(pnorm[...], dproj[:, m * chans : (m + 1) * chans])
        give(gtri_v.at[m], gtri_o.at[grp, m])
    triangle(
        dright, lambda t: upd[pl.ds(t, ROWS, stride=ROWS), :], left, lambda u, t: u * ROWS + t, True
    )
    for k in range(n_chunk):
        r = rows(k)
        d, sr = dright[r], sig_r[r]
        dproj[r, 2 * chans : 3 * chans] = (d * sr).astype(bf16)
        dproj[r, 3 * chans : 4 * chans] = (
            d * proj[r, 2 * chans : 3 * chans] * sr * (1.0 - sr)
        ).astype(bf16)
    for m in range(2, 4):
        gtri_v[m] = dot_tn(pnorm[...], dproj[:, m * chans : (m + 1) * chans])
        give(gtri_v.at[m], gtri_o.at[grp, m])
    dwork[...] = dot_nt(dproj[...], w_tri_b[:, 0 : 5 * chans])
    g_one = jnp.zeros((two, chans), f32)
    g_score = jnp.zeros((two, chans), f32)
    d_a = jnp.zeros((ROWS, chans), f32)
    tail_v[...] = jnp.zeros_like(tail_v)
    for k in range(n_chunk):
        r = rows(k)
        dn = dwork[r]
        normal = n1[r]
        g_one = g_one + dn * normal
        dn = dn * v1
        dpair = pair[r] + s1[r] * (dn - mean_last(dn) - normal * mean_last(dn * normal))
        g_score = g_score + sb[r] * dpair
        d_a = d_a + dpair[0:ROWS] + dpair[ROWS:two]
        for q in range(2):
            tail_v[2 * k + q : 2 * k + q + 1, chans : 2 * chans] = jnp.sum(
                dpair[q * ROWS : (q + 1) * ROWS], 0, keepdims=True
            )
    tail_v[0:ROWS, 0:chans] = d_a
    for k, g in enumerate((g_score, g_one, g_two, g_dist)):
        tail_v[ROWS + k : ROWS + k + 1, 0:chans] = jnp.sum(g, 0, keepdims=True)
    tail_v[ROWS + 4 : ROWS + 5, 0:chans] = jnp.broadcast_to(loss, (1, chans))
    tail_v[ROWS + 5 : ROWS + 6, 0:chans] = jnp.broadcast_to(loss_count, (1, chans))
    give(tail_v, tail_o.at[grp])

    for c in sends:
        c.wait_send()
    for away, here in peers:
        away.wait()
        here.wait()


def update_kernel(
    frozen_h, single_h, gtri_h, tail_h, w_in_h, w_pairin_h, w_tri_h, vecs_h,
    row_in_h, col_in_h, row_pairin_h, col_pairin_h, row_tri_h, col_tri_h, sq_vecs_h,
    loss_o, count_o, g_in_o, row_in_o, col_in_o, new_in_o, g_pairin_o, row_pairin_o, col_pairin_o,
    new_pairin_o, g_tri_o, row_tri_o, col_tri_o, new_tri_o, g_vecs_o, sq_vecs_o, new_vecs_o,
    frozen_v, single_v, gtri_v, tail_v, w_in_v, w_pairin_v, w_tri_v, vecs_v,
    row_in_v, col_in_v, row_pairin_v, col_pairin_v, row_tri_v, col_tri_v, sq_vecs_v,
    loss_s, count_s, g_in, row_in_n, col_in_n, new_in, g_pairin, row_pairin_n, col_pairin_n,
    new_pairin, g_tri, row_tri_n, col_tri_n, new_tri, g_vecs, sq_vecs_n, new_vecs,
    ds_v, old_v, new_v, load_sem, store_sem,
):
    chans = vecs_v.shape[1]
    width, node = w_in_v.shape
    n_mat = w_tri_v.shape[0]
    loads = []

    def load(src, dst):
        copy = pltpu.make_async_copy(src, dst, load_sem.at[len(loads)])
        loads.append(copy)
        copy.start()
        return copy

    c_tail = load(tail_h, tail_v)
    c_pw = load(w_pairin_h, w_pairin_v)
    c_frozen = [
        load(frozen_h.at[i % 2], frozen_v.at[pl.ds(i * WIDE, WIDE)]) for i in range(4)
    ]
    c_single = load(single_h, single_v)
    c_gtri = load(gtri_h, gtri_v)
    c_small = [
        load(row_in_h, row_in_v), load(col_in_h, col_in_v), load(row_pairin_h, row_pairin_v),
        load(col_pairin_h, col_pairin_v), load(row_tri_h, row_tri_v), load(col_tri_h, col_tri_v),
        load(sq_vecs_h, sq_vecs_v), load(vecs_h, vecs_v),
    ]
    c_tri = load(w_tri_h, w_tri_v)
    c_in = load(w_in_h, w_in_v)
    stores = []

    def store(src, dst):
        copy = pltpu.make_async_copy(src, dst, store_sem.at[len(stores)])
        stores.append(copy)
        copy.start()

    c_tail.wait()
    totals = tail_v[0, ROWS : ROWS + 8, 0:chans] + tail_v[1, ROWS : ROWS + 8, 0:chans]
    loss_s[...] = totals[4:5, :]
    count_s[...] = totals[5:6, :]
    inv = 1.0 / totals[5:6, :]
    inv2 = jnp.concatenate([inv, inv], 1)
    d_side = [tail_v[i, 0:ROWS, :] * inv2 for i in range(2)]

    c_pw.wait()
    pads = jnp.zeros((WIDE - ROWS, node), f32)
    halves = [[], []]
    side_parts = []
    for i in range(2):
        parts = split(d_side[i], 2)
        side_parts.append(parts)
        st = jnp.concatenate([p.astype(f32) for p in parts], 0).astype(bf16)
        ds = dot_nt(st[:, 0:chans], w_pairin_v[0].astype(bf16)) + dot_nt(
            st[:, chans : 2 * chans], w_pairin_v[1].astype(bf16)
        )
        ds = ds[0:ROWS] + ds[ROWS : 2 * ROWS]
        for k, p in enumerate(split(ds, 2)):
            at = (2 * k + i) * WIDE
            ds_v[at : at + WIDE, :] = jnp.concatenate([p.astype(f32), pads], 0).astype(bf16)
    for c in c_frozen:
        c.wait()
    g_in[...] = dot_tn(frozen_v[...], ds_v[...])
    store(g_in, g_in_o)

    c_single.wait()
    sg = jnp.concatenate([single_v[0], single_v[1], single_v[0], single_v[1]], 0).astype(bf16)
    st = jnp.concatenate(
        [side_parts[i][k].astype(f32) for k in range(2) for i in range(2)], 0
    ).astype(bf16)
    for k in range(2):
        g_pairin[k] = dot_tn(sg, st[:, k * chans : (k + 1) * chans])
    store(g_pairin, g_pairin_o)

    c_gtri.wait()
    for m in range(n_mat):
        g_tri[m] = (gtri_v[0, m] + gtri_v[1, m]) * inv
    store(g_tri, g_tri_o)
    for c in c_small:
        c.wait()
    g_vecs[...] = totals[0:4, :] * inv
    store(g_vecs, g_vecs_o)

    n_in = width // chans
    n_pr = w_pairin_v.shape[1] // chans
    old_v[...] = jnp.zeros_like(old_v)
    for b in range(n_in):
        old_v[b : b + 1, :] = row_in_v[b : b + 1, :]
    at_pair = n_in
    for k in range(2):
        for b in range(n_pr):
            j = at_pair + k * n_pr + b
            old_v[j : j + 1, :] = row_pairin_v[k : k + 1, b * chans : (b + 1) * chans]
    at_tri = at_pair + 2 * n_pr
    old_v[at_tri : at_tri + n_mat, :] = row_tri_v[...]
    old = old_v[...].T
    lane = iota((chans, chans), 1)
    fresh = [jnp.zeros((chans, chans), f32)]

    def whole(x):
        return jnp.sum(jnp.sum(x, 0, keepdims=True), -1, keepdims=True)

    def adafactor(grad, weight, new, col_old, n_blk, at, n_cols, set_col):
        n_rows = n_blk * chans
        colsum = jnp.zeros((8, n_cols), f32)
        scaled = jnp.zeros((8, n_cols), f32)
        rowsum = jnp.zeros((chans, 1), f32)
        wsum = jnp.zeros((8, n_cols), f32)
        roots = []

        def fold(x):
            return jnp.sum(x.reshape(chans // 8, 8, n_cols), 0)

        for b in range(n_blk):
            s = slice(b * chans, (b + 1) * chans)
            g = grad(s)
            sq = g * g + 1e-30
            row = BETA * old[:, at + b : at + b + 1] + (1.0 - BETA) * mean_last(sq)
            fresh[0] = jnp.where(lane == at + b, row, fresh[0])
            rowsum = rowsum + row
            root = lax.rsqrt(row)
            roots.append(root)
            colsum = colsum + fold(sq)
            step = g * root
            scaled = scaled + fold(step * step)
            w = weight(s)
            wsum = wsum + fold(w * w)
        col = BETA * col_old + (1.0 - BETA) / n_rows * jnp.sum(colsum, 0, keepdims=True)
        set_col(col)
        row_mean = jnp.sum(rowsum, 0, keepdims=True) / n_rows
        size = n_rows * n_cols
        rms = jnp.sqrt(row_mean * jnp.sum(
            jnp.sum(scaled, 0, keepdims=True) / col, -1, keepdims=True
        ) / size)
        scale = jnp.maximum(0.001, jnp.sqrt(whole(wsum) / size))
        coef = RATE * scale / jnp.maximum(1.0, rms) * jnp.sqrt(row_mean)
        by_col = lax.rsqrt(col) * coef
        for b in range(n_blk):
            s = slice(b * chans, (b + 1) * chans)
            new(s, weight(s) - grad(s) * roots[b] * by_col)

    c_in.wait()
    n_half = col_in_v.shape[0]

    def set_in(col):
        for k in range(n_half):
            col_in_n[k : k + 1, :] = col[:, k * chans : (k + 1) * chans]

    def new_in_set(s, x):
        new_in[s, :] = x

    adafactor(
        lambda s: g_in[s, :], lambda s: w_in_v[s, :], new_in_set,
        jnp.concatenate([col_in_v[k : k + 1, :] for k in range(n_half)], 1), n_in, 0, node, set_in,
    )
    store(new_in, new_in_o)
    store(col_in_n, col_in_o)
    for k in range(2):
        def set_pair(col, k=k):
            col_pairin_n[k : k + 1, :] = col

        def new_pair(s, x, k=k):
            new_pairin[k, s, :] = x

        adafactor(
            lambda s, k=k: g_pairin[k, s, :], lambda s, k=k: w_pairin_v[k, s, :], new_pair,
            col_pairin_v[k : k + 1, :], n_pr, at_pair + k * n_pr, chans, set_pair,
        )
    store(new_pairin, new_pairin_o)
    store(col_pairin_n, col_pairin_o)
    c_tri.wait()
    for m in range(n_mat):
        def set_tri(col, m=m):
            col_tri_n[m : m + 1, :] = col

        def new_tri_set(s, x, m=m):
            new_tri[m, s, :] = x

        adafactor(
            lambda s, m=m: g_tri[m, s, :], lambda s, m=m: w_tri_v[m, s, :], new_tri_set,
            col_tri_v[m : m + 1, :], 1, at_tri + m, chans, set_tri,
        )
    store(new_tri, new_tri_o)
    store(col_tri_n, col_tri_o)
    new_v[...] = fresh[0].T
    for b in range(n_in):
        row_in_n[b : b + 1, :] = new_v[b : b + 1, :]
    for k in range(2):
        for b in range(n_pr):
            j = at_pair + k * n_pr + b
            row_pairin_n[k : k + 1, b * chans : (b + 1) * chans] = new_v[j : j + 1, :]
    row_tri_n[...] = new_v[at_tri : at_tri + n_mat, :]
    store(row_in_n, row_in_o)
    store(row_pairin_n, row_pairin_o)
    store(row_tri_n, row_tri_o)

    g = g_vecs[...]
    sq = BETA * sq_vecs_v[...] + (1.0 - BETA) * (g * g + 1e-30)
    sq_vecs_n[...] = sq
    step = g * lax.rsqrt(sq)
    step = step / jnp.maximum(1.0, jnp.sqrt(mean_last(step * step)))
    v = vecs_v[...]
    scale = jnp.maximum(0.001, jnp.sqrt(mean_last(v * v)))
    new_vecs[...] = v - RATE * scale * step
    store(sq_vecs_n, sq_vecs_o)
    store(new_vecs, new_vecs_o)
    store(loss_s, loss_o)
    store(count_s, count_o)
    for c in stores:
        c.wait()


def shards(
    tokens, lengths, recycle, resolved, coords, plm_embed, plm_uv, plm_qk, plm_affine, plm_out,
    w_in, w_pairin, w_tri, vecs, row_in, col_in, row_pairin, col_pairin, row_tri, col_tri, sq_vecs,
):
    heads = lax.axis_size("head")
    seq = tokens.shape[1]
    width = plm_embed.shape[1]
    units = plm_uv.shape[2]
    chans = vecs.shape[1]
    node = w_in.shape[1]
    unit_chunk = 256 if units % 256 == 0 else 128
    col_chunk = 256
    n_unit, n_col = units // unit_chunk, width // col_chunk
    anywhere = pl.BlockSpec(memory_space=pl.ANY)
    table = ROWS * ROWS

    def vm(*shape, dtype=f32):
        return pltpu.VMEM(shape, dtype)

    def like(x):
        return pltpu.VMEM(x.shape, x.dtype)

    operands = (
        tokens, lengths, recycle, resolved, coords, plm_embed, plm_uv, plm_qk, plm_affine, plm_out,
        w_in, w_pairin, w_tri, vecs,
    )
    scratch = [
        like(tokens), pltpu.SMEM((1,), jnp.int32), pltpu.SMEM((1,), jnp.int32), like(resolved),
        like(coords), like(plm_embed), like(plm_uv), like(plm_qk), like(plm_affine), like(plm_out),
        like(w_in), like(w_pairin), like(w_tri), like(vecs),
        vm(WIDE, width), vm(WIDE, units, dtype=bf16),
        vm(heads, n_col, 16, col_chunk + col_chunk // 2, dtype=bf16),
        vm(WIDE, width, dtype=bf16), vm(ROWS, node), vm(width, node, dtype=bf16),
        vm(chans, 6 * chans, dtype=bf16), vm(WIDE, chans), vm(seq, seq), vm(chans, seq),
        vm(table, chans), vm(table, chans), vm(table, chans), vm(table, chans),
        vm(table, chans, dtype=bf16), vm(table, 5 * chans), vm(table, chans), vm(table, chans),
        vm(table, chans), vm(table, chans), vm(table, chans), vm(table, chans), vm(table, chans),
        vm(table, chans), vm(table, chans, dtype=bf16),
        vm(table, chans), vm(table, chans), vm(table, chans, dtype=bf16), vm(table, chans),
        vm(table, chans), vm(table, chans), vm(table, 5 * chans, dtype=bf16),
        vm(3 * WIDE, chans, dtype=bf16), vm(6, chans, chans), vm(WIDE, 2 * chans),
        pltpu.SemaphoreType.DMA((12 + 2 * n_unit + n_col,)),
        pltpu.SemaphoreType.DMA((heads - 1, n_col)), pltpu.SemaphoreType.DMA((heads, n_col)),
        pltpu.SemaphoreType.DMA((9,)), pltpu.SemaphoreType.DMA((9,)), pltpu.SemaphoreType.DMA((9,)),
    ]
    sds = jax.ShapeDtypeStruct
    frozen, single, gtri, tail = pl.pallas_call(
        functools.partial(tables_kernel, heads=heads, unit_chunk=unit_chunk, col_chunk=col_chunk),
        out_shape=(
            sds((2, WIDE, width), bf16), sds((2, ROWS, node), f32), sds((2, 6, chans, chans), f32),
            sds((2, WIDE, 2 * chans), f32),
        ),
        in_specs=[anywhere] * len(operands),
        out_specs=[anywhere] * 4,
        scratch_shapes=scratch,
        compiler_params=pltpu.CompilerParams(
            collective_id=0, has_side_effects=True, vmem_limit_bytes=48 << 20
        ),
        name="tables",
    )(*operands)

    row_in2 = row_in.reshape(-1, chans)
    col_in2 = col_in.reshape(-1, chans)
    operands = (
        frozen, single, gtri, tail, w_in, w_pairin, w_tri, vecs, row_in2, col_in2, row_pairin,
        col_pairin, row_tri, col_tri, sq_vecs,
    )
    outs = (
        sds((1, chans), f32), sds((1, chans), f32), w_in, row_in2, col_in2, w_in, w_pairin,
        row_pairin, col_pairin, w_pairin, w_tri, row_tri, col_tri, w_tri, vecs, vecs, vecs,
    )
    outs = tuple(sds(x.shape, x.dtype) for x in outs)
    scratch = (
        [vm(4 * WIDE, width, dtype=bf16)] + [like(x) for x in operands[1:]] + [like(x) for x in outs]
        + [
            vm(4 * WIDE, node, dtype=bf16), vm(chans, chans), vm(chans, chans),
            pltpu.SemaphoreType.DMA((18,)), pltpu.SemaphoreType.DMA((17,)),
        ]
    )
    res = list(
        pl.pallas_call(
            update_kernel,
            out_shape=outs,
            in_specs=[anywhere] * len(operands),
            out_specs=[anywhere] * len(outs),
            scratch_shapes=scratch,
            compiler_params=pltpu.CompilerParams(vmem_limit_bytes=32 << 20),
            name="update",
        )(*operands)
    )
    res[0] = res[0][0, 0]
    res[1] = res[1][0, 0]
    res[3] = res[3].reshape(-1)
    res[4] = res[4].reshape(-1)
    return tuple(res)


def solution(mesh):
    whole = P()
    in_specs = (
        P("grp", None), P("grp"), P("grp"), P("grp", None), P("grp", None, None), whole,
        P(None, None, "head"), whole, whole, P("head", None),
    ) + (whole,) * 11
    return jax.shard_map(
        shards, mesh=mesh, in_specs=in_specs, out_specs=(whole,) * 17, check_vma=False
    )
```

time: 175 us -> 38.2 us (0.22)
  other arithmetic: 52.4 us -> 0 us
  matrix products: 44.1 us -> 0 us
  Pallas kernels: 0 us -> 27.1 us
  waiting for transfers between devices: 23.8 us -> 0 us
  local copies, waits for them, and re-layouts: 28.1 us -> 8.62 us
  between operations: 18.3 us -> 2.05 us
  blocking collectives: 6.59 us -> 0 us
    dot_general x31 -> x0, matrix products: 44.1 us -> none  [the longest x11 6.94 us: dot32(): return jnp.dot(a, b, precision=highest)]
    pallas_call x0 -> x2, Pallas kernels: none -> 27.1 us  [the longest x1 19.7 us: shards(): pl.pallas_call(functools.partial(tables_kernel, heads=heads, unit_chunk=u...]
    reduce_sum x27 -> x0, other arithmetic: 26 us -> none  [the longest x3 6.33 us: factored(): jnp.mean(weight * weight, axis=(-2, -1), keepdims=True)]
    psum x2 -> x0, waiting for transfers between devices: 23.7 us -> none  [the longest x1 16.1 us: shards(): state = embed + lax.psum(partial_out, 'head')]
    dot_general x3 -> x0, local copies, waits for them, and re-layouts: 7.82 us -> none  [the longest x1 2.61 us: shards(): jnp.einsum('ikc,jkc->ijc', left * count[None, :, None], right, precision=...]
    unnamed x4 -> x0, other arithmetic: 7.59 us -> none
    sub x4 -> x0, other arithmetic: 6.85 us -> none  [the longest x3 6.19 us: factored(): return (row_new, col_new, weight - 0.3 * scale * step)]
    psum x2 -> x0, blocking collectives: 6.59 us -> none  [shards(): lax.psum((jnp.sum(weight * (root - 1.0)), jnp.sum(weight)), 'grp')]
  transfers between devices with their start and end apart: 2 -> 0, of which waited for: 2 -> 0; matrix products, arithmetic and copies ran while one was open for 10% -> 0% of each run, Pallas kernels for 0% -> 0%
where the time goes in v2:
time: 38.2 us; the launch traced here: 37.8 us
  Pallas kernels  27.1 us (71%)
  local copies, waits for them, and re-layouts  8.62 us (23%)
  between operations  2.05 us (5%)
    pallas_call x1, Pallas kernels, shards(): pl.pallas_call(functools.partial(tables_kernel, heads=heads, unit_chunk=u...  19.7 us
    unnamed x33, local copies, waits for them, and re-layouts  8.62 us
    pallas_call x1, Pallas kernels, shards(): pl.pallas_call(update_kernel, out_shape=outs, in_specs=[anywhere] * len(o...  7.45 us

profile of v2, /device:TPU:0, one launch (start us, length us, event | category | flops | bytes accessed | tf_op | source)
XLA Modules:
  0.0 37.8 jit_solution(14356113767946162979)
XLA Ops:
  1.9 0.7 %copy.38.coords_h = f32[1,3,256]{2,1,0:T(4,128)S(1)} copy(f32[1,3,256]{2,0,1:T(1,128)} %param.25) | data formatting | bytes 6144 | tf_op args[4]
  2.6 0.0 copy-start
  2.6 1.3 %copy-done = f32[1280,256]{1,0:T(8,128)S(1)} copy-done((f32[1280,256]{1,0:T(8,128)S(1)}, f32[1280,256]{1,0:T(8,128)}, u32[]{:S(2)}) %copy-start) | copy-done | bytes 1310744
  4.0 0.0 copy-start.1
  4.0 1.0 %copy-done.1 = f32[6,128,128]{2,1,0:T(8,128)S(1)} copy-done((f32[6,128,128]{2,1,0:T(8,128)S(1)}, f32[6,128,128]{2,1,0:T(8,128)}, u32[]{:S(2)}) %copy-start.1) | copy-done | bytes 393240
  4.9 0.0 copy-start.2
  4.9 0.9 %copy-done.2 = f32[2,256,128]{2,1,0:T(8,128)S(1)} copy-done((f32[2,256,128]{2,1,0:T(8,128)S(1)}, f32[2,256,128]{2,1,0:T(8,128)}, u32[]{:S(2)}) %copy-start.2) | copy-done | bytes 262168
  5.9 0.0 copy-start.3
  5.9 1.1 %copy-done.3 = bf16[1280,256]{1,0:T(8,128)(2,1)S(1)} copy-done((bf16[1280,256]{1,0:T(8,128)(2,1)S(1)}, bf16[1280,256]{1,0:T(8,128)(2,1)}, u32[]{:S(2)}) %copy-start.3) | copy-done | bytes 655384
  7.0 0.0 copy-start.4
  7.0 0.8 %copy-done.4 = bf16[23,1280]{1,0:T(8,128)(2,1)S(1)} copy-done((bf16[23,1280]{1,0:T(8,128)(2,1)S(1)}, bf16[23,1280]{1,0:T(8,128)(2,1)}, u32[]{:S(2)}) %copy-start.4) | copy-done | bytes 58904
  7.8 0.0 copy-start.6
  7.8 0.7 %copy-done.6 = f32[4,128]{1,0:T(4,128)S(1)} copy-done((f32[4,128]{1,0:T(4,128)S(1)}, f32[4,128]{1,0:T(4,128)}, u32[]{:S(2)}) %copy-start.6) | copy-done | bytes 2072
  8.5 0.0 copy-start.7
  8.5 0.7 %copy-done.7 = f32[4,256]{1,0:T(4,128)S(1)} copy-done((f32[4,256]{1,0:T(4,128)S(1)}, f32[4,256]{1,0:T(4,128)}, u32[]{:S(2)}) %copy-start.7) | copy-done | bytes 4120
  9.2 0.0 copy-start.12
  9.2 0.7 %copy-done.12 = s32[1,256]{1,0:T(1,128)S(1)} copy-done((s32[1,256]{1,0:T(1,128)S(1)}, s32[1,256]{1,0:T(1,128)}, u32[]{:S(2)}) %copy-start.12) | copy-done | bytes 1048
  9.9 0.0 copy-start.13
  9.9 0.7 %copy-done.13 = s32[1,256]{1,0:T(1,128)S(1)} copy-done((s32[1,256]{1,0:T(1,128)S(1)}, s32[1,256]{1,0:T(1,128)}, u32[]{:S(2)}) %copy-start.13) | copy-done | bytes 1048
  10.5 0.0 copy-start.5
  10.5 0.0 copy-start.8
  10.5 0.0 copy-start.9
  10.5 0.0 copy-start.10
  10.6 0.0 copy-start.11
  10.6 0.0 copy-start.14
  10.6 0.0 copy-start.15
  10.6 19.7 %tables.1 = (bf16[2,32,1280]{2,1,0:T(8,128)(2,1)S(1)}, f32[2,24,256]{2,1,0:T(8,128)S(1)}, f32[2,6,128,128]{3,2,1,0:T(8,128)S(1)}, f32[2,32,256]{2,1,0:T(8,128)S(1)}) custom-call(s32[1,256]{1,0:T(1,128)S(1)} %copy-done.12, s32[1]{0:T(128)S(6)} %copy.39.lengths_h, s32[1]{0:T(128)S(6)} %copy.40.recycle_h, s32[1,256]{1,0:T(1,128)S(1)} %copy-done.13, ...), custom_call_target="tpu_custom_call" | custom-call | tf_op jit(solution)/shard_map/tables/pallas_call | solution.py:704
  30.3 0.0 copy-done.5
  30.3 0.0 copy-done.8
  30.3 0.0 copy-done.9
  30.3 0.0 copy-done.10
  30.3 0.0 copy-done.11
  30.3 0.0 copy-done.14
  30.3 0.0 copy-done.15
  30.3 7.4 %update.1 = (f32[1,128]{1,0:T(1,128)}, f32[1,128]{1,0:T(1,128)}, f32[1280,256]{1,0:T(8,128)}, f32[10,128]{1,0:T(8,128)}, f32[2,128]{1,0:T(2,128)}, /*index=5*/f3...) custom-call(bf16[2,32,1280]{2,1,0:T(8,128)(2,1)S(1)} %get-tuple-elem, ...), custom_call_target="tpu_custom_call" | custom-call | tf_op jit(solution)/shard_map/update/pallas_call | solution.py:738
Async XLA Ops:
  2.6 1.3 %copy-start = (f32[1280,256]{1,0:T(8,128)S(1)}, f32[1280,256]{1,0:T(8,128)}, u32[]{:S(2)}) copy-start(f32[1280,256]{1,0:T(8,128)} %w_in_h.3) | copy-start | bytes 3932164
  4.0 1.0 %copy-start.1 = (f32[6,128,128]{2,1,0:T(8,128)S(1)}, f32[6,128,128]{2,1,0:T(8,128)}, u32[]{:S(2)}) copy-start(f32[6,128,128]{2,1,0:T(8,128)} %w_tri_h.3) | copy-start | bytes 1179652
  4.9 0.9 %copy-start.2 = (f32[2,256,128]{2,1,0:T(8,128)S(1)}, f32[2,256,128]{2,1,0:T(8,128)}, u32[]{:S(2)}) copy-start(f32[2,256,128]{2,1,0:T(8,128)} %w_pairin_h.3) | copy-start | bytes 786436
  5.9 1.1 %copy-start.3 = (bf16[1280,256]{1,0:T(8,128)(2,1)S(1)}, bf16[1280,256]{1,0:T(8,128)(2,1)}, u32[]{:S(2)}) copy-start(bf16[1280,256]{1,0:T(8,128)(2,1)} %qk_h.1) | copy-start | bytes 1966084
  7.0 0.8 %copy-start.4 = (bf16[23,1280]{1,0:T(8,128)(2,1)S(1)}, bf16[23,1280]{1,0:T(8,128)(2,1)}, u32[]{:S(2)}) copy-start(bf16[23,1280]{1,0:T(8,128)(2,1)} %embed_h.1) | copy-start | bytes 176644
  7.8 0.7 %copy-start.6 = (f32[4,128]{1,0:T(4,128)S(1)}, f32[4,128]{1,0:T(4,128)}, u32[]{:S(2)}) copy-start(f32[4,128]{1,0:T(4,128)} %vecs_h.3) | copy-start | bytes 6148
  8.5 0.7 %copy-start.7 = (f32[4,256]{1,0:T(4,128)S(1)}, f32[4,256]{1,0:T(4,128)}, u32[]{:S(2)}) copy-start(f32[4,256]{1,0:T(4,128)} %affine_h.1) | copy-start | bytes 12292
  9.2 0.7 %copy-start.12 = (s32[1,256]{1,0:T(1,128)S(1)}, s32[1,256]{1,0:T(1,128)}, u32[]{:S(2)}) copy-start(s32[1,256]{1,0:T(1,128)} %tokens_h.1) | copy-start | bytes 3076
  9.9 0.7 %copy-start.13 = (s32[1,256]{1,0:T(1,128)S(1)}, s32[1,256]{1,0:T(1,128)}, u32[]{:S(2)}) copy-start(s32[1,256]{1,0:T(1,128)} %resolved_h.1) | copy-start | bytes 3076
  10.5 19.7 %copy-start.5 = (f32[1280]{0:T(1024)S(1)}, f32[1280]{0:T(1024)}, u32[]{:S(2)}) copy-start(f32[1280]{0:T(1024)} %param.35) | copy-start | bytes 15364
  10.5 19.7 %copy-start.8 = (f32[6,128]{1,0:T(8,128)S(1)}, f32[6,128]{1,0:T(8,128)}, u32[]{:S(2)}) copy-start(f32[6,128]{1,0:T(8,128)} %row_tri_h.1) | copy-start | bytes 9220
  10.5 19.7 %copy-start.9 = (f32[6,128]{1,0:T(8,128)S(1)}, f32[6,128]{1,0:T(8,128)}, u32[]{:S(2)}) copy-start(f32[6,128]{1,0:T(8,128)} %col_tri_h.1) | copy-start | bytes 9220
  10.5 19.7 %copy-start.10 = (f32[2,256]{1,0:T(2,128)S(1)}, f32[2,256]{1,0:T(2,128)}, u32[]{:S(2)}) copy-start(f32[2,256]{1,0:T(2,128)} %row_pairin_h.1) | copy-start | bytes 6148
  10.6 19.8 %copy-start.11 = (f32[4,128]{1,0:T(4,128)S(1)}, f32[4,128]{1,0:T(4,128)}, u32[]{:S(2)}) copy-start(f32[4,128]{1,0:T(4,128)} %sq_vecs_h.1) | copy-start | bytes 6148
  10.6 19.8 %copy-start.14 = (f32[256]{0:T(256)S(1)}, f32[256]{0:T(256)}, u32[]{:S(2)}) copy-start(f32[256]{0:T(256)} %param.36) | copy-start | bytes 3076
  10.6 19.8 %copy-start.15 = (f32[2,128]{1,0:T(2,128)S(1)}, f32[2,128]{1,0:T(2,128)}, u32[]{:S(2)}) copy-start(f32[2,128]{1,0:T(2,128)} %col_pairin_h.1) | copy-start | bytes 3076

commit v3 on v2

v3 whole, which is shorter than its diff:
```python
import functools
import math

import jax
import jax.numpy as jnp
from jax import lax
from jax.experimental import pallas as pl
from jax.experimental.pallas import tpu as pltpu
from jax.sharding import PartitionSpec as P


STEP = 10
BETA = 1.0 - STEP ** (-0.8)
RATE = 0.3
MESH = pl.DeviceIdType.MESH
f32 = jnp.float32
bf16 = jnp.bfloat16
ROWS = 24
WIDE = 32


def dot(a, b):
    return jnp.dot(a, b, preferred_element_type=f32)


def dot_nt(a, b):
    return lax.dot_general(a, b, (((1,), (1,)), ((), ())), preferred_element_type=f32)


def dot_tn(a, b):
    return lax.dot_general(a, b, (((0,), (0,)), ((), ())), preferred_element_type=f32)


def silu(x):
    return x * jax.nn.sigmoid(x)


def mean_last(x):
    return jnp.mean(x, -1, keepdims=True)


def split(x, parts):
    out = []
    for _ in range(parts):
        part = x.astype(bf16)
        out.append(part)
        x = x - part.astype(f32)
    return out


def iota(shape, dim):
    return lax.broadcasted_iota(jnp.int32, shape, dim)


def tables_kernel(
    tokens_h, lengths_s, recycle_s, resolved_h, coords_h, embed_h, uv_h, qk_h, affine_h, out_h,
    w_in_h, w_pairin_h, w_tri_h, vecs_h, row_in_h, row_pairin_h, row_tri_h,
    frozen_o, single_o, gtri_o, tail_o, old_o, scale_o,
    tokens_v, resolved_v, coords_v, embed_v, uv_v, qk_v, affine_v, out_v,
    w_in_v, w_pairin_v, w_tri_v, vecs_v, row_in_v, row_pairin_v, row_tri_v,
    emb, mixed, part, w_in_b, w_tri_b, cnt_b, true_d, cols,
    pair, sb, n1, s1, pnorm, proj, sig_l, sig_r, gate, left, right, upd, n2, s2, unorm,
    branch, final, dbranch, dwork, dleft, dright, dproj, stack_d, old_v,
    load_sem, part_send, part_recv, peer_send, peer_recv,
    *, heads, unit_chunk, depth_chunk,
):
    grp = lax.axis_index("grp")
    head = lax.axis_index("head")
    other = 1 - grp
    seq = tokens_v.shape[1]
    units = uv_v.shape[2]
    width = emb.shape[1]
    chans = vecs_v.shape[1]
    vocab = embed_v.shape[0]
    n_unit = units // unit_chunk
    n_depth = units // depth_chunk
    half = width // 2

    loads = []

    def load(src, dst):
        copy = pltpu.make_async_copy(src, dst, load_sem.at[len(loads)])
        loads.append(copy)
        copy.start()
        return copy

    c_small = [
        load(embed_h, embed_v),
        load(tokens_h, tokens_v),
        load(affine_h, affine_v),
    ]
    c_qk = load(qk_h, qk_v)
    c_uv = []
    for c in range(n_unit):
        s = pl.ds(c * unit_chunk, unit_chunk)
        c_uv.append([load(uv_h.at[i, :, s], uv_v.at[i, :, s]) for i in range(2)])
    c_out = []
    for c in range(n_depth):
        s = pl.ds(c * depth_chunk, depth_chunk)
        c_out.append(load(out_h.at[s], out_v.at[s]))
    c_pairs = [load(resolved_h, resolved_v), load(coords_h, coords_v)]
    c_par = [
        load(w_in_h, w_in_v),
        load(w_pairin_h, w_pairin_v),
        load(w_tri_h, w_tri_v),
        load(vecs_h, vecs_v),
        load(row_in_h, row_in_v),
        load(row_pairin_h, row_pairin_v),
        load(row_tri_h, row_tri_v),
    ]

    barrier = pltpu.get_barrier_semaphore()
    pl.semaphore_signal(barrier, inc=1, device_id={"grp": other}, device_id_type=MESH)
    for d in range(1, heads):
        peer = lax.rem(head + d, heads)
        pl.semaphore_signal(barrier, inc=1, device_id={"head": peer}, device_id_type=MESH)

    for c in c_small:
        c.wait()
    emb[...] = jnp.zeros_like(emb)
    emb[0:vocab, :] = embed_v[...].astype(f32)
    e = emb[...]
    centre = e - mean_last(e)
    normed = (centre * lax.rsqrt(mean_last(centre * centre) + 1e-05)).astype(bf16)

    length = lengths_s[0]
    recycle = recycle_s[0].astype(f32)
    tok = tokens_v[...]
    onehot = (iota((WIDE, seq), 0) == tok).astype(f32)
    key_ok = (iota((1, seq), 1) < length).astype(f32)
    one_b = onehot.astype(bf16)
    cnt_col = jnp.sum(onehot, -1, keepdims=True)
    cnt_b[...] = jnp.broadcast_to(cnt_col, (WIDE, chans))
    ones = jnp.ones((16, seq), bf16)
    cnt_row = dot_nt(ones, one_b)[0:1, :]
    key_row = dot_nt(ones, (onehot * key_ok).astype(bf16))[0:1, :]

    c_qk.wait()
    shared = silu(dot(normed, qk_v[...]))
    query = (shared * affine_v[0:1, :] + affine_v[1:2, :]).astype(bf16)
    keyed = (shared * affine_v[2:3, :] + affine_v[3:4, :]).astype(bf16)
    scores = dot_nt(query, keyed) / math.sqrt(qk_v.shape[1])
    masked = jnp.where(key_row > 0, scores, -1000000000.0)
    top = jnp.exp(masked - jnp.max(masked, -1, keepdims=True))
    attn = (top / jnp.sum(top * key_row, -1, keepdims=True)).astype(bf16).astype(f32)
    attn = jnp.concatenate(split(attn * key_row, 2), 0)

    for c in range(n_unit):
        s = slice(c * unit_chunk, (c + 1) * unit_chunk)
        c_uv[c][0].wait()
        ugate = silu(dot(normed, uv_v[0, :, s]))
        c_uv[c][1].wait()
        value = silu(dot(normed, uv_v[1, :, s])).astype(bf16)
        seen = dot(attn, value)
        mixed[:, s] = (ugate * (seen[0:WIDE] + seen[WIDE : 2 * WIDE])).astype(bf16)

    pl.semaphore_wait(barrier, heads)

    p = None
    for c in range(n_depth):
        s = slice(c * depth_chunk, (c + 1) * depth_chunk)
        c_out[c].wait()
        q = dot(mixed[:, s], out_v[s, :])
        p = q if p is None else p + q
    part[head, :, 0:width] = p[0:16].astype(bf16)
    part[head, :, width : width + half] = jnp.concatenate(
        [p[16:24, 0:half], p[16:24, half:width]], 0
    ).astype(bf16)
    sends = []
    for d in range(1, heads):
        copy = pltpu.make_async_remote_copy(
            src_ref=part.at[head],
            dst_ref=part.at[head],
            send_sem=part_send.at[d - 1],
            recv_sem=part_recv.at[head],
            device_id={"head": lax.rem(head + d, heads)},
            device_id_type=MESH,
        )
        copy.start()
        sends.append(copy)

    for c in c_pairs + c_par:
        c.wait()
    w_in_b[...] = w_in_v[...].astype(bf16)
    for m in range(6):
        w_tri_b[:, m * chans : (m + 1) * chans] = w_tri_v[m].astype(bf16)
    valid = key_ok * (resolved_v[...] > 0).astype(f32)
    cols[...] = jnp.zeros_like(cols)
    for k in range(3):
        cols[k : k + 1, :] = coords_v[k]
    cols[3:4, :] = valid
    one_v = (onehot * valid).astype(bf16)
    weight_j = recycle * valid
    blk = 128
    n_blk = seq // blk
    places = []
    for b in range(n_blk):
        t = cols[:, b * blk : (b + 1) * blk].T
        places.append(t)
        d2 = None
        for k in range(3):
            delta = t[:, k : k + 1] - cols[k : k + 1, :]
            d2 = delta * delta if d2 is None else d2 + delta * delta
        true_d[b * blk : (b + 1) * blk, :] = jnp.sqrt(d2)
    n_valid = jnp.sum(valid, -1, keepdims=True)
    loss_count = recycle * n_valid * n_valid

    present = cnt_b[0:ROWS, :] > 0
    sc = jnp.where((cnt_row > 0) & (cnt_col > 0), scores, 0.0)[0:ROWS]

    n_in = width // chans
    n_pr = w_pairin_v.shape[1] // chans
    at_tri = n_in + 2 * n_pr
    old_v[...] = jnp.zeros_like(old_v)
    old_v[0:n_in, :] = row_in_v[...]
    for k in range(2):
        for b in range(n_pr):
            j = n_in + k * n_pr + b
            old_v[j : j + 1, :] = row_pairin_v[k : k + 1, b * chans : (b + 1) * chans]
    old_v[at_tri : at_tri + 6, :] = row_tri_v[...]
    old = BETA * old_v[...].T
    for k in range(at_tri + 6):
        old_o[k * chans : (k + 1) * chans, :] = jnp.broadcast_to(old[:, k : k + 1], (chans, chans))
    scale_o[...] = jnp.zeros_like(scale_o)
    mats = [w_in_v] + [w_pairin_v.at[k] for k in range(2)] + [w_tri_v.at[m] for m in range(6)]
    for k, w in enumerate(mats):
        x = w[...]
        x = jnp.sum(jnp.sum(x * x, 0, keepdims=True), -1, keepdims=True) / (w.shape[0] * w.shape[1])
        x = RATE * jnp.maximum(0.001, jnp.sqrt(x))
        scale_o[k : k + 1, :] = jnp.broadcast_to(x, (1, chans))

    for d in range(1, heads):
        peer = lax.rem(head + d, heads)
        pltpu.make_async_remote_copy(
            src_ref=part.at[peer],
            dst_ref=part.at[peer],
            send_sem=part_send.at[d - 1],
            recv_sem=part_recv.at[peer],
            device_id={"head": peer},
            device_id_type=MESH,
        ).wait_recv()
    low = None
    for k in range(heads):
        a = part[k, :, 0:width].astype(f32)
        b = part[k, :, width : width + half].astype(f32)
        b = jnp.concatenate([b[0:8], b[8:16]], 1)
        low = [a, b] if low is None else [low[0] + a, low[1] + b]
    emb[0:16, :] += low[0]
    emb[16:24, :] += low[1]
    state = emb[0:ROWS, :]
    centre = state - mean_last(state)
    frozen = centre * lax.rsqrt(mean_last(centre * centre) + 1e-05)
    frozen = jnp.concatenate([frozen, jnp.zeros((WIDE - ROWS, width), f32)], 0).astype(bf16)
    frozen_o[grp] = frozen

    peers = []

    def give(ref):
        k = len(peers)
        copy = pltpu.make_async_remote_copy(
            src_ref=ref,
            dst_ref=ref,
            send_sem=peer_send.at[k],
            recv_sem=peer_recv.at[k],
            device_id={"grp": other},
            device_id_type=MESH,
        )
        copy.start()
        peers.append(copy)

    give(frozen_o.at[grp])
    single = dot(frozen, w_in_b[...]).astype(bf16)
    single_o[grp] = single[0:ROWS].astype(f32)
    give(single_o.at[grp])
    side_a = dot(single, w_pairin_v[0].astype(bf16))[0:ROWS]
    side_b = dot(single, w_pairin_v[1].astype(bf16))[0:ROWS]
    side_a = jnp.where(present, side_a, 0.0)
    side_b = jnp.where(present, side_b, 0.0)
    v0 = vecs_v[0:1, :]
    v1 = vecs_v[1:2, :]
    v2 = vecs_v[2:3, :]
    v3 = vecs_v[3:4, :]
    v0c = v0 - mean_last(v0)
    side_ac = side_a - mean_last(side_a)
    side_bc = side_b - mean_last(side_b)

    n_chunk = ROWS // 2
    two = 2 * ROWS

    def rows(k):
        return slice(k * two, (k + 1) * two)

    def both(f, k):
        return jnp.concatenate([f(2 * k), f(2 * k + 1)], 0)

    for k in range(n_chunk):
        r = rows(k)
        sbk = both(lambda u: jnp.broadcast_to(sc[:, u : u + 1], (ROWS, chans)), k)
        sb[r] = sbk
        pair[r] = sbk * v0 + both(lambda u: side_a + side_b[u : u + 1, :], k)
        centre = sbk * v0c + both(lambda u: side_ac + side_bc[u : u + 1, :], k)
        scale = lax.rsqrt(mean_last(centre * centre) + 1e-05)
        normal = centre * scale
        n1[r] = normal
        s1[r] = jnp.broadcast_to(scale, (two, chans))
        pnorm[r] = (normal * v1).astype(bf16)
    proj[...] = dot(pnorm[...], w_tri_b[:, 0 : 5 * chans])
    for k in range(n_chunk):
        r = rows(k)
        sl = jax.nn.sigmoid(proj[r, chans : 2 * chans])
        sr = jax.nn.sigmoid(proj[r, 3 * chans : 4 * chans])
        sig_l[r] = sl
        sig_r[r] = sr
        left[r] = (sl * proj[r, 0:chans]).astype(bf16).astype(f32)
        right[r] = (sr * proj[r, 2 * chans : 3 * chans]).astype(bf16).astype(f32)
        gate[r] = jax.nn.sigmoid(proj[r, 4 * chans : 5 * chans])
        dwork[r] = left[r] * both(
            lambda u: jnp.broadcast_to(cnt_b[u : u + 1, :], (ROWS, chans)), k
        )

    def triangle(dst, moving, fixed, row_of, weighted):
        group = 4
        for a0 in range(0, ROWS, group):
            total = [None] * group
            for b in range(vocab):
                x = moving(b)
                for q in range(group):
                    y = x * fixed[pl.ds(row_of(a0 + q, b), 1), :]
                    total[q] = y if total[q] is None else total[q] + y
            for q in range(group):
                a = a0 + q
                t = total[q]
                if weighted:
                    t = t * cnt_b[a : a + 1, :]
                dst[a * ROWS : (a + 1) * ROWS, :] = t

    triangle(
        upd, lambda u: dwork[u * ROWS : (u + 1) * ROWS, :], right, lambda v, u: u * ROWS + v, False
    )
    for k in range(n_chunk):
        r = rows(k)
        x = upd[r]
        centre = x - mean_last(x)
        scale = lax.rsqrt(mean_last(centre * centre) + 1e-05)
        normal = centre * scale
        n2[r] = normal
        s2[r] = jnp.broadcast_to(scale, (two, chans))
        unorm[r] = (normal * v2).astype(bf16)
    branch[...] = dot(unorm[...], w_tri_b[:, 5 * chans : 6 * chans])
    lane = iota((ROWS, chans), 1)
    logit = jnp.zeros((ROWS, chans), f32)
    for k in range(n_chunk):
        r = rows(k)
        fin = pair[r] + gate[r] * branch[r]
        final[r] = fin
        col = jnp.sum(fin * v3, -1, keepdims=True)
        for q in range(2):
            logit = jnp.where(lane == 2 * k + q, col[q * ROWS : (q + 1) * ROWS], logit)

    dist = jnp.maximum(logit, 0.0) + jnp.log1p(jnp.exp(-jnp.abs(logit)))
    dist = jnp.concatenate([dist, jnp.zeros((WIDE - ROWS, chans), f32)], 0)
    for k, d in enumerate(split(dist, 3)):
        stack_d[k * WIDE : (k + 1) * WIDE, :] = d
    by_col = dot(stack_d[:, 0:WIDE], one_b).astype(bf16)
    one3 = jnp.concatenate([one_b, one_b, one_b], 0)
    loss_row = jnp.zeros((1, seq), f32)
    by_first = jnp.zeros((WIDE, seq), f32)
    for b in range(n_blk):
        s = slice(b * blk, (b + 1) * blk)
        diff = dot_tn(one3[:, s], by_col) - true_d[s, :]
        sq = diff * diff + 1.0
        inv = lax.rsqrt(sq)
        loss_row = loss_row + jnp.sum(
            places[b][:, 3:4] * (sq * inv - 1.0), 0, keepdims=True
        )
        for q in split(diff * inv, 2):
            by_first = by_first + dot(one_v[:, s], q)
    loss = jnp.sum(loss_row * weight_j, -1, keepdims=True)
    by_pair = dot_nt(jnp.concatenate(split(by_first * weight_j, 2), 0), one_b)
    by_pair = (by_pair[0:WIDE] + by_pair[WIDE : 2 * WIDE])[0:ROWS]
    dlogit = by_pair * jax.nn.sigmoid(logit)[:, 0:WIDE]

    g_dist = jnp.zeros((two, chans), f32)
    for k in range(n_chunk):
        r = rows(k)
        g = both(lambda u: jnp.broadcast_to(dlogit[:, u : u + 1], (ROWS, chans)), k)
        g_dist = g_dist + g * final[r]
        dfinal = g * v3
        gt = gate[r]
        pair[r] = dfinal
        dbranch[r] = (dfinal * gt).astype(bf16)
        dproj[r, 4 * chans : 5 * chans] = (dfinal * branch[r] * gt * (1.0 - gt)).astype(bf16)
    dwork[...] = dot_nt(dbranch[...], w_tri_b[:, 5 * chans : 6 * chans])
    gtri_o[grp, 5] = dot_tn(unorm[...], dbranch[...])
    give(gtri_o.at[grp, 5])
    gtri_o[grp, 4] = dot_tn(pnorm[...], dproj[:, 4 * chans : 5 * chans])
    give(gtri_o.at[grp, 4])
    g_two = jnp.zeros((two, chans), f32)
    for k in range(n_chunk):
        r = rows(k)
        dn = dwork[r]
        normal = n2[r]
        g_two = g_two + dn * normal
        dn = dn * v2
        upd[r] = s2[r] * (dn - mean_last(dn) - normal * mean_last(dn * normal))
    triangle(
        dleft, lambda v: upd[v * ROWS : (v + 1) * ROWS, :], right, lambda u, v: u * ROWS + v, True
    )
    for k in range(n_chunk):
        r = rows(k)
        d, sl = dleft[r], sig_l[r]
        dproj[r, 0:chans] = (d * sl).astype(bf16)
        dproj[r, chans : 2 * chans] = (d * proj[r, 0:chans] * sl * (1.0 - sl)).astype(bf16)
    for m in range(2):
        gtri_o[grp, m] = dot_tn(pnorm[...], dproj[:, m * chans : (m + 1) * chans])
        give(gtri_o.at[grp, m])
    triangle(
        dright, lambda t: upd[pl.ds(t, ROWS, stride=ROWS), :], left, lambda u, t: u * ROWS + t, True
    )
    for k in range(n_chunk):
        r = rows(k)
        d, sr = dright[r], sig_r[r]
        dproj[r, 2 * chans : 3 * chans] = (d * sr).astype(bf16)
        dproj[r, 3 * chans : 4 * chans] = (
            d * proj[r, 2 * chans : 3 * chans] * sr * (1.0 - sr)
        ).astype(bf16)
    for m in range(2, 4):
        gtri_o[grp, m] = dot_tn(pnorm[...], dproj[:, m * chans : (m + 1) * chans])
        give(gtri_o.at[grp, m])
    dwork[...] = dot_nt(dproj[...], w_tri_b[:, 0 : 5 * chans])
    g_one = jnp.zeros((two, chans), f32)
    g_score = jnp.zeros((two, chans), f32)
    d_a = jnp.zeros((ROWS, chans), f32)
    tail_o[grp] = jnp.zeros((WIDE, 2 * chans), f32)
    for k in range(n_chunk):
        r = rows(k)
        dn = dwork[r]
        normal = n1[r]
        g_one = g_one + dn * normal
        dn = dn * v1
        dpair = pair[r] + s1[r] * (dn - mean_last(dn) - normal * mean_last(dn * normal))
        g_score = g_score + sb[r] * dpair
        d_a = d_a + dpair[0:ROWS] + dpair[ROWS:two]
        for q in range(2):
            tail_o[grp, 2 * k + q : 2 * k + q + 1, chans : 2 * chans] = jnp.sum(
                dpair[q * ROWS : (q + 1) * ROWS], 0, keepdims=True
            )
    tail_o[grp, 0:ROWS, 0:chans] = d_a
    for k, g in enumerate((g_score, g_one, g_two, g_dist)):
        tail_o[grp, ROWS + k : ROWS + k + 1, 0:chans] = jnp.sum(g, 0, keepdims=True)
    tail_o[grp, ROWS + 4 : ROWS + 5, 0:chans] = jnp.broadcast_to(loss, (1, chans))
    tail_o[grp, ROWS + 5 : ROWS + 6, 0:chans] = jnp.broadcast_to(loss_count, (1, chans))
    give(tail_o.at[grp])

    for c in sends:
        c.wait_send()
    for c in peers:
        c.wait()


def update_kernel(
    frozen_v, single_v, gtri_v, tail_v, old_v, scale_v, w_in_v, w_pairin_v, w_tri_v, vecs_v,
    row_in_v, col_in_v, row_pairin_v, col_pairin_v, row_tri_v, col_tri_v, sq_vecs_v,
    loss_o, count_o, g_in_o, row_in_o, col_in_o, new_in_o, g_pairin_o, row_pairin_o, col_pairin_o,
    new_pairin_o, g_tri_o, row_tri_o, col_tri_o, new_tri_o, g_vecs_o, sq_vecs_o, new_vecs_o,
    loss_s, count_s, g_in, row_in_n, col_in_n, new_in, g_pairin, row_pairin_n, col_pairin_n,
    new_pairin, g_tri, row_tri_n, col_tri_n, new_tri, g_vecs, sq_vecs_n, new_vecs,
    ds_v, sq_in, sq_rest, sum_in, sum_rest, store_sem,
):
    chans = vecs_v.shape[1]
    width, node = w_in_v.shape
    n_mat = w_tri_v.shape[0]
    stores = []

    def store(src, dst):
        copy = pltpu.make_async_copy(src, dst, store_sem.at[len(stores)])
        stores.append(copy)
        copy.start()

    totals = tail_v[0, ROWS : ROWS + 8, 0:chans] + tail_v[1, ROWS : ROWS + 8, 0:chans]
    inv = 1.0 / totals[5:6, :]
    inv2 = jnp.concatenate([inv, inv], 1)
    d_side = [tail_v[i, 0:ROWS, :] * inv2 for i in range(2)]

    pads = jnp.zeros((WIDE - ROWS, node), f32)
    side_parts = []
    for i in range(2):
        parts = split(d_side[i], 2)
        side_parts.append(parts)
        st = jnp.concatenate([p.astype(f32) for p in parts], 0).astype(bf16)
        ds = dot_nt(st[:, 0:chans], w_pairin_v[0].astype(bf16)) + dot_nt(
            st[:, chans : 2 * chans], w_pairin_v[1].astype(bf16)
        )
        ds = ds[0:ROWS] + ds[ROWS : 2 * ROWS]
        for k, p in enumerate(split(ds, 2)):
            at = (2 * k + i) * WIDE
            ds_v[at : at + WIDE, :] = jnp.concatenate([p.astype(f32), pads], 0).astype(bf16)
    fz = jnp.concatenate([frozen_v[0], frozen_v[1], frozen_v[0], frozen_v[1]], 0)
    g_in[...] = dot_tn(fz, ds_v[...])
    store(g_in, g_in_o)

    sg = jnp.concatenate([single_v[0], single_v[1], single_v[0], single_v[1]], 0).astype(bf16)
    st = jnp.concatenate(
        [side_parts[i][k].astype(f32) for k in range(2) for i in range(2)], 0
    ).astype(bf16)
    for k in range(2):
        g_pairin[k] = dot_tn(sg, st[:, k * chans : (k + 1) * chans])
    store(g_pairin, g_pairin_o)
    for m in range(n_mat):
        g_tri[m] = (gtri_v[0, m] + gtri_v[1, m]) * inv
    store(g_tri, g_tri_o)
    loss_s[...] = totals[4:5, :]
    count_s[...] = totals[5:6, :]
    g_vecs[...] = totals[0:4, :] * inv
    store(loss_s, loss_o)
    store(count_s, count_o)
    store(g_vecs, g_vecs_o)

    blk = chans
    n_in = width // blk
    n_pr = w_pairin_v.shape[1] // blk
    at_tri = 2 * n_pr
    for b in range(n_in):
        g = g_in[b * blk : (b + 1) * blk, :]
        sq_in[b * blk : (b + 1) * blk, :] = (g * g).astype(bf16)
    for k in range(2):
        for b in range(n_pr):
            g = g_pairin[k, b * blk : (b + 1) * blk, :]
            j = k * n_pr + b
            sq_rest[j * blk : (j + 1) * blk, :] = (g * g).astype(bf16)
    for m in range(n_mat):
        g = g_tri[m]
        j = at_tri + m
        sq_rest[j * blk : (j + 1) * blk, :] = (g * g).astype(bf16)
    sum_in[...] = dot(sq_in[...], jnp.ones((node, chans), bf16))
    sum_rest[...] = dot(sq_rest[...], jnp.ones((chans, chans), bf16))
    lane_in = dot_nt(jnp.ones((16, node), bf16), sq_in[...])[0:1]
    lane_rest = dot_nt(jnp.ones((16, chans), bf16), sq_rest[...])[0:1]

    def fresh(old, total, n):
        return BETA * old + ((1.0 - BETA) / n * total + (1.0 - BETA) * 1e-30)

    for b in range(n_in):
        row_in_n[b : b + 1, :] = fresh(
            row_in_v[b : b + 1, :], lane_in[:, b * blk : (b + 1) * blk], node
        )
    for k in range(2):
        s = slice(k * n_pr * blk, (k + 1) * n_pr * blk)
        row_pairin_n[k : k + 1, :] = fresh(row_pairin_v[k : k + 1, :], lane_rest[:, s], chans)
    for m in range(n_mat):
        s = slice((at_tri + m) * blk, (at_tri + m + 1) * blk)
        row_tri_n[m : m + 1, :] = fresh(row_tri_v[m : m + 1, :], lane_rest[:, s], chans)
    store(row_in_n, row_in_o)
    store(row_pairin_n, row_pairin_o)
    store(row_tri_n, row_tri_o)

    def fold(x):
        return jnp.sum(x.reshape(blk // 8, 8, x.shape[1]), 0)

    def adafactor(grad, weight, new, col_old, col_new, sums, old_at, n_blk, which, n_cols):
        n_rows = n_blk * blk
        halves = n_cols // chans
        col_sum = [jnp.zeros((8, chans), f32)] * halves
        scaled = [jnp.zeros((8, chans), f32)] * halves
        row_sum = jnp.zeros((8, chans), f32)
        for b in range(n_blk):
            s = slice(b * blk, (b + 1) * blk)
            o = slice((old_at + b) * blk, (old_at + b + 1) * blk)
            t = sums[0][(sums[1] + b) * blk : (sums[1] + b + 1) * blk, :]
            row = old_v[o, :] + ((1.0 - BETA) / n_cols * t + (1.0 - BETA) * 1e-30)
            row_sum = row_sum + fold(row)
            root = lax.rsqrt(row)
            for h in range(halves):
                c = slice(h * chans, (h + 1) * chans)
                g = grad[s, c]
                step = g * root
                new[s, c] = step
                col_sum[h] = col_sum[h] + fold(g * g)
                scaled[h] = scaled[h] + fold(step * step)
        row_mean = jnp.sum(row_sum, 0, keepdims=True) / n_rows
        power = jnp.zeros((1, chans), f32)
        by_col = []
        for h in range(halves):
            col = fresh(col_old(h), jnp.sum(col_sum[h], 0, keepdims=True), n_rows)
            col_new(h, col)
            power = power + jnp.sum(scaled[h], 0, keepdims=True) / col
            by_col.append(lax.rsqrt(col))
        rms = jnp.sqrt(row_mean * jnp.sum(power, -1, keepdims=True) / (n_rows * n_cols))
        coef = scale_v[which : which + 1, :] * jnp.sqrt(row_mean) / jnp.maximum(1.0, rms)
        for b in range(n_blk):
            s = slice(b * blk, (b + 1) * blk)
            for h in range(halves):
                c = slice(h * chans, (h + 1) * chans)
                new[s, c] = weight[s, c] - new[s, c] * (by_col[h] * coef)

    def put(ref, k):
        def put_col(h, col):
            at = k if k is not None else h
            ref[at : at + 1, :] = col

        return put_col

    adafactor(
        g_in, w_in_v, new_in, lambda h: col_in_v[h : h + 1, :], put(col_in_n, None), (sum_in, 0), 0,
        n_in, 0, node,
    )
    store(new_in, new_in_o)
    store(col_in_n, col_in_o)
    for k in range(2):
        adafactor(
            g_pairin.at[k], w_pairin_v.at[k], new_pairin.at[k],
            lambda h, k=k: col_pairin_v[k : k + 1, :], put(col_pairin_n, k),
            (sum_rest, k * n_pr), n_in + k * n_pr, n_pr, 1 + k, chans,
        )
    store(new_pairin, new_pairin_o)
    store(col_pairin_n, col_pairin_o)
    for m in range(n_mat):
        adafactor(
            g_tri.at[m], w_tri_v.at[m], new_tri.at[m],
            lambda h, m=m: col_tri_v[m : m + 1, :], put(col_tri_n, m),
            (sum_rest, at_tri + m), n_in + at_tri + m, 1, 3 + m, chans,
        )
    store(new_tri, new_tri_o)
    store(col_tri_n, col_tri_o)

    g = g_vecs[...]
    sq = BETA * sq_vecs_v[...] + (1.0 - BETA) * (g * g + 1e-30)
    sq_vecs_n[...] = sq
    step = g * lax.rsqrt(sq)
    step = step / jnp.maximum(1.0, jnp.sqrt(mean_last(step * step)))
    v = vecs_v[...]
    scale = jnp.maximum(0.001, jnp.sqrt(mean_last(v * v)))
    new_vecs[...] = v - RATE * scale * step
    store(sq_vecs_n, sq_vecs_o)
    store(new_vecs, new_vecs_o)
    for c in stores:
        c.wait()


def shards(
    tokens, lengths, recycle, resolved, coords, plm_embed, plm_uv, plm_qk, plm_affine, plm_out,
    w_in, w_pairin, w_tri, vecs, row_in, col_in, row_pairin, col_pairin, row_tri, col_tri, sq_vecs,
):
    heads = lax.axis_size("head")
    seq = tokens.shape[1]
    width = plm_embed.shape[1]
    units = plm_uv.shape[2]
    chans = vecs.shape[1]
    node = w_in.shape[1]
    unit_chunk = 256 if units % 256 == 0 else 128
    depth_chunk = units // 2 if units % 256 == 0 else units
    n_unit, n_depth = units // unit_chunk, units // depth_chunk
    anywhere = pl.BlockSpec(memory_space=pl.ANY)
    inside = pl.BlockSpec(memory_space=pltpu.VMEM)
    table = ROWS * ROWS

    def vm(*shape, dtype=f32):
        return pltpu.VMEM(shape, dtype)

    def like(x):
        return pltpu.VMEM(x.shape, x.dtype)

    coords = jnp.transpose(coords, (1, 0, 2))
    row_in2 = row_in.reshape(-1, chans)
    col_in2 = col_in.reshape(-1, chans)
    operands = (
        tokens, lengths, recycle, resolved, coords, plm_embed, plm_uv, plm_qk, plm_affine, plm_out,
        w_in, w_pairin, w_tri, vecs, row_in2, row_pairin, row_tri,
    )
    scratch = [
        like(tokens), like(resolved),
        like(coords), like(plm_embed), like(plm_uv), like(plm_qk), like(plm_affine), like(plm_out),
        like(w_in), like(w_pairin), like(w_tri), like(vecs), like(row_in2), like(row_pairin),
        like(row_tri), vm(WIDE, width), vm(WIDE, units, dtype=bf16),
        vm(heads, 16, width + width // 2, dtype=bf16), vm(width, node, dtype=bf16),
        vm(chans, 6 * chans, dtype=bf16), vm(WIDE, chans), vm(seq, seq), vm(chans, seq),
        vm(table, chans), vm(table, chans), vm(table, chans), vm(table, chans),
        vm(table, chans, dtype=bf16), vm(table, 5 * chans), vm(table, chans), vm(table, chans),
        vm(table, chans), vm(table, chans), vm(table, chans), vm(table, chans), vm(table, chans),
        vm(table, chans), vm(table, chans, dtype=bf16),
        vm(table, chans), vm(table, chans), vm(table, chans, dtype=bf16), vm(table, chans),
        vm(table, chans), vm(table, chans), vm(table, 5 * chans, dtype=bf16),
        vm(3 * WIDE, chans, dtype=bf16), vm(chans, chans),
        pltpu.SemaphoreType.DMA((13 + 2 * n_unit + n_depth,)),
        pltpu.SemaphoreType.DMA((heads - 1,)), pltpu.SemaphoreType.DMA((heads,)),
        pltpu.SemaphoreType.DMA((9,)), pltpu.SemaphoreType.DMA((9,)),
    ]
    operands = tuple(
        x if x.size == 1 else pltpu.with_memory_space_constraint(x, pltpu.HBM) for x in operands
    )
    sds = jax.ShapeDtypeStruct
    n_blk = width // chans + 2 * (node // chans) + 6
    made = pl.pallas_call(
        functools.partial(tables_kernel, heads=heads, unit_chunk=unit_chunk, depth_chunk=depth_chunk),
        out_shape=(
            sds((2, WIDE, width), bf16), sds((2, ROWS, node), f32), sds((2, 6, chans, chans), f32),
            sds((2, WIDE, 2 * chans), f32), sds((n_blk * chans, chans), f32), sds((16, chans), f32),
        ),
        in_specs=[
            pl.BlockSpec(memory_space=pltpu.SMEM) if x.size == 1 else anywhere for x in operands
        ],
        out_specs=[inside] * 6,
        scratch_shapes=scratch,
        compiler_params=pltpu.CompilerParams(
            collective_id=0, has_side_effects=True, vmem_limit_bytes=48 << 20
        ),
        name="tables",
    )(*operands)

    operands = tuple(made) + (
        w_in, w_pairin, w_tri, vecs, row_in2, col_in2, row_pairin,
        col_pairin, row_tri, col_tri, sq_vecs,
    )
    outs = (
        sds((1, chans), f32), sds((1, chans), f32), w_in, row_in2, col_in2, w_in, w_pairin,
        row_pairin, col_pairin, w_pairin, w_tri, row_tri, col_tri, w_tri, vecs, vecs, vecs,
    )
    outs = tuple(sds(x.shape, x.dtype) for x in outs)
    scratch = (
        [like(x) for x in outs]
        + [
            vm(4 * WIDE, node, dtype=bf16), vm(width, node, dtype=bf16),
            vm((n_blk - width // chans) * chans, chans, dtype=bf16), vm(width, chans),
            vm((n_blk - width // chans) * chans, chans),
            pltpu.SemaphoreType.DMA((17,)),
        ]
    )
    res = list(
        pl.pallas_call(
            update_kernel,
            out_shape=outs,
            in_specs=[inside] * len(operands),
            out_specs=[anywhere] * len(outs),
            scratch_shapes=scratch,
            compiler_params=pltpu.CompilerParams(vmem_limit_bytes=32 << 20),
            name="update",
        )(*operands)
    )
    res[0] = res[0][0, 0]
    res[1] = res[1][0, 0]
    res[3] = res[3].reshape(-1)
    res[4] = res[4].reshape(-1)
    return tuple(res)


def solution(mesh):
    whole = P()
    in_specs = (
        P("grp", None), P("grp"), P("grp"), P("grp", None), P("grp", None, None), whole,
        P(None, None, "head"), whole, whole, P("head", None),
    ) + (whole,) * 11
    return jax.shard_map(
        shards, mesh=mesh, in_specs=in_specs, out_specs=(whole,) * 17, check_vma=False
    )
```

time: 38.2 us -> 24.9 us (0.65)
  local copies, waits for them, and re-layouts: 8.62 us -> 0.05 us
  Pallas kernels: 27.1 us -> 22.6 us
    unnamed x33 -> x22, local copies, waits for them, and re-layouts: 8.62 us -> 0.05 us
    pallas_call x1, Pallas kernels: 7.45 us -> 3.66 us  [shards(): pl.pallas_call(update_kernel, out_shape=outs, in_specs=[inside] * len(ope...]
    pallas_call x1, Pallas kernels: 19.7 us -> 18.9 us  [shards(): pl.pallas_call(functools.partial(tables_kernel, heads=heads, unit_chunk=u...]
where the time goes in v3:
time: 24.9 us; the launch traced here: 24.8 us
  Pallas kernels  22.6 us (91%)
  between operations  2.14 us (9%)
    pallas_call x1, Pallas kernels, shards(): pl.pallas_call(functools.partial(tables_kernel, heads=heads, unit_chunk=u...  18.9 us
    pallas_call x1, Pallas kernels, shards(): pl.pallas_call(update_kernel, out_shape=outs, in_specs=[inside] * len(ope...  3.66 us

profile of v3, /device:TPU:0, one launch (start us, length us, event | category | flops | bytes accessed | tf_op | source)
XLA Modules:
  0.0 24.8 jit_solution(620258402019966625)
XLA Ops:
  2.0 0.0 copy-start
  2.0 0.0 copy-start.1
  2.0 0.0 copy-start.2
  2.0 0.0 copy-start.3
  2.0 0.0 copy-start.4
  2.0 0.0 copy-start.5
  2.0 0.0 copy-start.6
  2.0 0.0 copy-start.7
  2.0 0.0 copy-start.8
  2.0 0.0 copy-start.9
  2.1 0.0 copy-start.10
  2.1 18.9 %tables.1 = (bf16[2,32,1280]{2,1,0:T(8,128)(2,1)S(1)}, f32[2,24,256]{2,1,0:T(8,128)S(1)}, f32[2,6,128,128]{3,2,1,0:T(8,128)S(1)}, f32[2,32,256]{2,1,0:T(8,128)S(...) custom-call(s32[1,256]{1,0:T(1,128)} %tokens_h.1, s32[1]{0:T(128)S(6)} %copy.38.lengths_s, s32[1]{0:T(128)S(6)} %copy.39.recycle_s, ...), custom_call_target="tpu_custom_call" | custom-call | tf_op jit(solution)/shard_map/tables/pallas_call | solution.py:693
  21.0 0.0 copy-done
  21.0 0.0 copy-done.1
  21.0 0.0 copy-done.2
  21.0 0.0 copy-done.3
  21.0 0.0 copy-done.4
  21.0 0.0 copy-done.5
  21.1 0.0 copy-done.6
  21.1 0.0 copy-done.7
  21.1 0.0 copy-done.8
  21.1 0.0 copy-done.9
  21.1 0.0 copy-done.10
  21.1 3.7 %update.1 = (f32[1,128]{1,0:T(1,128)}, f32[1,128]{1,0:T(1,128)}, f32[1280,256]{1,0:T(8,128)}, f32[10,128]{1,0:T(8,128)}, f32[2,128]{1,0:T(2,128)}, /*index=5*/f3...) custom-call(bf16[2,32,1280]{2,1,0:T(8,128)(2,1)S(1)} %get-tuple-elem, ...), custom_call_target="tpu_custom_call" | custom-call | tf_op jit(solution)/shard_map/update/pallas_call | solution.py:729
Async XLA Ops:
  2.0 19.0 %copy-start = (f32[1280,256]{1,0:T(8,128)S(1)}, f32[1280,256]{1,0:T(8,128)}, u32[]{:S(2)}) copy-start(f32[1280,256]{1,0:T(8,128)} %w_in_v.1) | copy-start | bytes 3932164
  2.0 19.0 %copy-start.1 = (f32[6,128,128]{2,1,0:T(8,128)S(1)}, f32[6,128,128]{2,1,0:T(8,128)}, u32[]{:S(2)}) copy-start(f32[6,128,128]{2,1,0:T(8,128)} %w_tri_v.1) | copy-start | bytes 1179652
  2.0 19.0 %copy-start.2 = (f32[2,256,128]{2,1,0:T(8,128)S(1)}, f32[2,256,128]{2,1,0:T(8,128)}, u32[]{:S(2)}) copy-start(f32[2,256,128]{2,1,0:T(8,128)} %w_pairin_v.1) | copy-start | bytes 786436
  2.0 19.0 %copy-start.3 = (f32[1280]{0:T(1024)S(1)}, f32[1280]{0:T(1024)}, u32[]{:S(2)}) copy-start(f32[1280]{0:T(1024)} %param.35) | copy-start | bytes 15364
  2.0 19.0 %copy-start.4 = (f32[6,128]{1,0:T(8,128)S(1)}, f32[6,128]{1,0:T(8,128)}, u32[]{:S(2)}) copy-start(f32[6,128]{1,0:T(8,128)} %row_tri_v.1) | copy-start | bytes 9220
  2.0 19.0 %copy-start.5 = (f32[4,128]{1,0:T(4,128)S(1)}, f32[4,128]{1,0:T(4,128)}, u32[]{:S(2)}) copy-start(f32[4,128]{1,0:T(4,128)} %vecs_v.1) | copy-start | bytes 6148
  2.0 19.0 %copy-start.6 = (f32[2,256]{1,0:T(2,128)S(1)}, f32[2,256]{1,0:T(2,128)}, u32[]{:S(2)}) copy-start(f32[2,256]{1,0:T(2,128)} %row_pairin_v.1) | copy-start | bytes 6148
  2.0 19.0 %copy-start.7 = (f32[6,128]{1,0:T(8,128)S(1)}, f32[6,128]{1,0:T(8,128)}, u32[]{:S(2)}) copy-start(f32[6,128]{1,0:T(8,128)} %col_tri_v.1) | copy-start | bytes 9220
  2.0 19.0 %copy-start.8 = (f32[4,128]{1,0:T(4,128)S(1)}, f32[4,128]{1,0:T(4,128)}, u32[]{:S(2)}) copy-start(f32[4,128]{1,0:T(4,128)} %sq_vecs_v.1) | copy-start | bytes 6148
  2.0 19.0 %copy-start.9 = (f32[256]{0:T(256)S(1)}, f32[256]{0:T(256)}, u32[]{:S(2)}) copy-start(f32[256]{0:T(256)} %param.36) | copy-start | bytes 3076
  2.1 19.0 %copy-start.10 = (f32[2,128]{1,0:T(2,128)S(1)}, f32[2,128]{1,0:T(2,128)}, u32[]{:S(2)}) copy-start(f32[2,128]{1,0:T(2,128)} %col_pairin_v.1) | copy-start | bytes 3076

commit v4 on v3

--- a/solution.py
+++ b/solution.py
@@ -54,26 +54,25 @@
 
 def tables_kernel(
     tokens_h, lengths_s, recycle_s, resolved_h, coords_h, embed_h, uv_h, qk_h, affine_h, out_h,
-    w_in_h, w_pairin_h, w_tri_h, vecs_h, row_in_h, row_pairin_h, row_tri_h,
+    w_in_h, w_pairin_h, w_tri_h, vecs_h, row_in_h, col_in_h, row_pairin_h, col_pairin_h, row_tri_h,
+    col_tri_h, sq_vecs_h,
     frozen_o, single_o, gtri_o, tail_o, old_o, scale_o,
+    w_in_v, w_pairin_v, w_tri_v, vecs_v, row_in_v, col_in_v, row_pairin_v, col_pairin_v, row_tri_v,
+    col_tri_v, sq_vecs_v,
     tokens_v, resolved_v, coords_v, embed_v, uv_v, qk_v, affine_v, out_v,
-    w_in_v, w_pairin_v, w_tri_v, vecs_v, row_in_v, row_pairin_v, row_tri_v,
-    emb, mixed, part, w_in_b, w_tri_b, cnt_b, true_d, cols,
+    emb, gate_x, value_x, part, w_in_b, w_tri_b, cnt_b, true_d, cols,
     pair, sb, n1, s1, pnorm, proj, sig_l, sig_r, gate, left, right, upd, n2, s2, unorm,
     branch, final, dbranch, dwork, dleft, dright, dproj, stack_d, old_v,
-    load_sem, part_send, part_recv, peer_send, peer_recv,
-    *, heads, unit_chunk, depth_chunk,
+    load_sem, part_send, part_recv, unit_send, unit_recv, peer_send, peer_recv,
+    *, heads, shared_by, unit_part,
 ):
     grp = lax.axis_index("grp")
     head = lax.axis_index("head")
     other = 1 - grp
     seq = tokens_v.shape[1]
-    units = uv_v.shape[2]
     width = emb.shape[1]
     chans = vecs_v.shape[1]
     vocab = embed_v.shape[0]
-    n_unit = units // unit_chunk
-    n_depth = units // depth_chunk
     half = width // 2
 
     loads = []
@@ -89,15 +88,15 @@
         load(tokens_h, tokens_v),
         load(affine_h, affine_v),
     ]
+    mine = grp if shared_by == 2 else 0
+    at_mine = pl.multiple_of(mine * unit_part, 128)
+    c_value = load(uv_h.at[1, :, pl.ds(at_mine, unit_part)], uv_v.at[1])
     c_qk = load(qk_h, qk_v)
-    c_uv = []
-    for c in range(n_unit):
-        s = pl.ds(c * unit_chunk, unit_chunk)
-        c_uv.append([load(uv_h.at[i, :, s], uv_v.at[i, :, s]) for i in range(2)])
+    c_gate = load(uv_h.at[0, :, pl.ds(at_mine, unit_part)], uv_v.at[0])
     c_out = []
-    for c in range(n_depth):
-        s = pl.ds(c * depth_chunk, depth_chunk)
-        c_out.append(load(out_h.at[s], out_v.at[s]))
+    for k in range(shared_by):
+        at = pl.multiple_of(lax.rem(mine + k, shared_by) * unit_part, 128)
+        c_out.append(load(out_h.at[pl.ds(at, unit_part)], out_v.at[k]))
     c_pairs = [load(resolved_h, resolved_v), load(coords_h, coords_v)]
     c_par = [
         load(w_in_h, w_in_v),
@@ -107,6 +106,10 @@
         load(row_in_h, row_in_v),
         load(row_pairin_h, row_pairin_v),
         load(row_tri_h, row_tri_v),
+        load(col_in_h, col_in_v),
+        load(col_pairin_h, col_pairin_v),
+        load(col_tri_h, col_tri_v),
+        load(sq_vecs_h, sq_vecs_v),
     ]
 
     barrier = pltpu.get_barrier_semaphore()
@@ -135,6 +138,25 @@
     cnt_row = dot_nt(ones, one_b)[0:1, :]
     key_row = dot_nt(ones, (onehot * key_ok).astype(bf16))[0:1, :]
 
+    pl.semaphore_wait(barrier, heads)
+    unit_sends = []
+
+    def swap(ref, k):
+        copy = pltpu.make_async_remote_copy(
+            src_ref=ref.at[0],
+            dst_ref=ref.at[1],
+            send_sem=unit_send.at[k],
+            recv_sem=unit_recv.at[k],
+            device_id={"grp": other},
+            device_id_type=MESH,
+        )
+        copy.start()
+        unit_sends.append(copy)
+
+    c_value.wait()
+    value_x[0] = silu(dot(normed, uv_v[1])).astype(bf16)
+    if shared_by == 2:
+        swap(value_x, 0)
     c_qk.wait()
     shared = silu(dot(normed, qk_v[...]))
     query = (shared * affine_v[0:1, :] + affine_v[1:2, :]).astype(bf16)
@@ -145,22 +167,22 @@
     attn = (top / jnp.sum(top * key_row, -1, keepdims=True)).astype(bf16).astype(f32)
     attn = jnp.concatenate(split(attn * key_row, 2), 0)
 
-    for c in range(n_unit):
-        s = slice(c * unit_chunk, (c + 1) * unit_chunk)
-        c_uv[c][0].wait()
-        ugate = silu(dot(normed, uv_v[0, :, s]))
-        c_uv[c][1].wait()
-        value = silu(dot(normed, uv_v[1, :, s])).astype(bf16)
-        seen = dot(attn, value)
-        mixed[:, s] = (ugate * (seen[0:WIDE] + seen[WIDE : 2 * WIDE])).astype(bf16)
-
-    pl.semaphore_wait(barrier, heads)
+    c_gate.wait()
+    ugate = silu(dot(normed, uv_v[0]))
+    gate_x[0] = ugate[0:ROWS]
+    if shared_by == 2:
+        swap(gate_x, 1)
 
     p = None
-    for c in range(n_depth):
-        s = slice(c * depth_chunk, (c + 1) * depth_chunk)
-        c_out[c].wait()
-        q = dot(mixed[:, s], out_v[s, :])
+    for k in range(shared_by):
+        if k == 1:
+            for c in unit_sends:
+                c.wait_recv()
+        seen = dot(attn, value_x[k])
+        seen = seen[0:ROWS] + seen[WIDE : WIDE + ROWS]
+        mixed = jnp.concatenate([gate_x[k] * seen, jnp.zeros((WIDE - ROWS, unit_part), f32)], 0)
+        c_out[k].wait()
+        q = dot(mixed.astype(bf16), out_v[k])
         p = q if p is None else p + q
     part[head, :, 0:width] = p[0:16].astype(bf16)
     part[head, :, width : width + half] = jnp.concatenate(
@@ -452,7 +474,7 @@
     tail_o[grp, ROWS + 5 : ROWS + 6, 0:chans] = jnp.broadcast_to(loss_count, (1, chans))
     give(tail_o.at[grp])
 
-    for c in sends:
+    for c in sends + unit_sends:
         c.wait_send()
     for c in peers:
         c.wait()
@@ -647,9 +669,8 @@
     units = plm_uv.shape[2]
     chans = vecs.shape[1]
     node = w_in.shape[1]
-    unit_chunk = 256 if units % 256 == 0 else 128
-    depth_chunk = units // 2 if units % 256 == 0 else units
-    n_unit, n_depth = units // unit_chunk, units // depth_chunk
+    shared_by = 2 if units % 256 == 0 else 1
+    unit_part = units // shared_by
     anywhere = pl.BlockSpec(memory_space=pl.ANY)
     inside = pl.BlockSpec(memory_space=pltpu.VMEM)
     table = ROWS * ROWS
@@ -665,13 +686,14 @@
     col_in2 = col_in.reshape(-1, chans)
     operands = (
         tokens, lengths, recycle, resolved, coords, plm_embed, plm_uv, plm_qk, plm_affine, plm_out,
-        w_in, w_pairin, w_tri, vecs, row_in2, row_pairin, row_tri,
-    )
+        w_in, w_pairin, w_tri, vecs, row_in2, col_in2, row_pairin, col_pairin, row_tri, col_tri, sq_vecs,
+    )
+    kept = operands[10:]
     scratch = [
         like(tokens), like(resolved),
-        like(coords), like(plm_embed), like(plm_uv), like(plm_qk), like(plm_affine), like(plm_out),
-        like(w_in), like(w_pairin), like(w_tri), like(vecs), like(row_in2), like(row_pairin),
-        like(row_tri), vm(WIDE, width), vm(WIDE, units, dtype=bf16),
+        like(coords), like(plm_embed), vm(2, width, unit_part, dtype=bf16), like(plm_qk),
+        like(plm_affine), vm(shared_by, unit_part, width, dtype=bf16),
+        vm(WIDE, width), vm(shared_by, ROWS, unit_part), vm(shared_by, WIDE, unit_part, dtype=bf16),
         vm(heads, 16, width + width // 2, dtype=bf16), vm(width, node, dtype=bf16),
         vm(chans, 6 * chans, dtype=bf16), vm(WIDE, chans), vm(seq, seq), vm(chans, seq),
         vm(table, chans), vm(table, chans), vm(table, chans), vm(table, chans),
@@ -681,8 +703,9 @@
         vm(table, chans), vm(table, chans), vm(table, chans, dtype=bf16), vm(table, chans),
         vm(table, chans), vm(table, chans), vm(table, 5 * chans, dtype=bf16),
         vm(3 * WIDE, chans, dtype=bf16), vm(chans, chans),
-        pltpu.SemaphoreType.DMA((13 + 2 * n_unit + n_depth,)),
+        pltpu.SemaphoreType.DMA((19 + shared_by,)),
         pltpu.SemaphoreType.DMA((heads - 1,)), pltpu.SemaphoreType.DMA((heads,)),
+        pltpu.SemaphoreType.DMA((2,)), pltpu.SemaphoreType.DMA((2,)),
         pltpu.SemaphoreType.DMA((9,)), pltpu.SemaphoreType.DMA((9,)),
     ]
     operands = tuple(
@@ -691,15 +714,16 @@
     sds = jax.ShapeDtypeStruct
     n_blk = width // chans + 2 * (node // chans) + 6
     made = pl.pallas_call(
-        functools.partial(tables_kernel, heads=heads, unit_chunk=unit_chunk, depth_chunk=depth_chunk),
+        functools.partial(tables_kernel, heads=heads, shared_by=shared_by, unit_part=unit_part),
         out_shape=(
             sds((2, WIDE, width), bf16), sds((2, ROWS, node), f32), sds((2, 6, chans, chans), f32),
             sds((2, WIDE, 2 * chans), f32), sds((n_blk * chans, chans), f32), sds((16, chans), f32),
-        ),
+        )
+        + tuple(sds(x.shape, x.dtype) for x in kept),
         in_specs=[
             pl.BlockSpec(memory_space=pltpu.SMEM) if x.size == 1 else anywhere for x in operands
         ],
-        out_specs=[inside] * 6,
+        out_specs=[inside] * (6 + len(kept)),
         scratch_shapes=scratch,
         compiler_params=pltpu.CompilerParams(
             collective_id=0, has_side_effects=True, vmem_limit_bytes=48 << 20
@@ -707,10 +731,7 @@
         name="tables",
     )(*operands)
 
-    operands = tuple(made) + (
-        w_in, w_pairin, w_tri, vecs, row_in2, col_in2, row_pairin,
-        col_pairin, row_tri, col_tri, sq_vecs,
-    )
+    operands = tuple(made)
     outs = (
         sds((1, chans), f32), sds((1, chans), f32), w_in, row_in2, col_in2, w_in, w_pairin,
         row_pairin, col_pairin, w_pairin, w_tri, row_tri, col_tri, w_tri, vecs, vecs, vecs,

time: 24.9 us -> 23.5 us (0.944)
  Pallas kernels: 22.6 us -> 21.4 us
    pallas_call x1, Pallas kernels: 18.9 us -> 17.7 us  [shards(): pl.pallas_call(functools.partial(tables_kernel, heads=heads, shared_by=sh...]
where the time goes in v4:
time: 23.5 us; the launch traced here: 23.3 us
  Pallas kernels  21.4 us (91%)
  between operations  1.96 us (8%)
    pallas_call x1, Pallas kernels, shards(): pl.pallas_call(functools.partial(tables_kernel, heads=heads, shared_by=sh...  17.7 us
    pallas_call x1, Pallas kernels, shards(): pl.pallas_call(update_kernel, out_shape=outs, in_specs=[inside] * len(ope...  3.66 us

profile of v4, /device:TPU:0, one launch (start us, length us, event | category | flops | bytes accessed | tf_op | source)
XLA Modules:
  0.0 23.3 jit_solution(13877746673959691539)
XLA Ops:
  2.0 17.7 %tables.1 = (bf16[2,32,1280]{2,1,0:T(8,128)(2,1)S(1)}, f32[2,24,256]{2,1,0:T(8,128)S(1)}, f32[2,6,128,128]{3,2,1,0:T(8,128)S(1)}, f32[2,32,256]{2,1,0:T(8,128)S(...) custom-call(s32[1,256]{1,0:T(1,128)} %tokens_h.1, ...), custom_call_target="tpu_custom_call" | custom-call | tf_op jit(solution)/shard_map/tables/pallas_call | solution.py:716
  19.7 3.7 %update.1 = (f32[1,128]{1,0:T(1,128)}, f32[1,128]{1,0:T(1,128)}, f32[1280,256]{1,0:T(8,128)}, f32[10,128]{1,0:T(8,128)}, f32[2,128]{1,0:T(2,128)}, /*index=5*/f3...) custom-call(bf16[2,32,1280]{2,1,0:T(8,128)(2,1)S(1)} %get-tuple-elem, ...), custom_call_target="tpu_custom_call" | custom-call | tf_op jit(solution)/shard_map/update/pallas_call | solution.py:750

commit v5 on v4

--- a/solution.py
+++ b/solution.py
@@ -10,6 +10,7 @@
 
 
 STEP = 10
+ORDER = (0, 1, 4, 2, 3)
 BETA = 1.0 - STEP ** (-0.8)
 RATE = 0.3
 MESH = pl.DeviceIdType.MESH
@@ -60,9 +61,10 @@
     w_in_v, w_pairin_v, w_tri_v, vecs_v, row_in_v, col_in_v, row_pairin_v, col_pairin_v, row_tri_v,
     col_tri_v, sq_vecs_v,
     tokens_v, resolved_v, coords_v, embed_v, uv_v, qk_v, affine_v, out_v,
-    emb, gate_x, value_x, part, w_in_b, w_tri_b, cnt_b, true_d, cols,
+    emb, gate_x, value_x, partial_v, part, w_in_b, w_pair_b, w_tri_b, cnt_b, true_d, cols,
     pair, sb, n1, s1, pnorm, proj, sig_l, sig_r, gate, left, right, upd, n2, s2, unorm,
-    branch, final, dbranch, dwork, dleft, dright, dproj, stack_d, old_v,
+    branch, final, dbranch, left_n, gated_b, dunorm, dpnorm, dlast, dleft, dright, dproj, stack_d,
+    old_v, one_t,
     load_sem, part_send, part_recv, unit_send, unit_recv, peer_send, peer_recv,
     *, heads, shared_by, unit_part,
 ):
@@ -74,6 +76,7 @@
     chans = vecs_v.shape[1]
     vocab = embed_v.shape[0]
     half = width // 2
+    quarter = width // 4
 
     loads = []
 
@@ -90,9 +93,9 @@
     ]
     mine = grp if shared_by == 2 else 0
     at_mine = pl.multiple_of(mine * unit_part, 128)
-    c_value = load(uv_h.at[1, :, pl.ds(at_mine, unit_part)], uv_v.at[1])
     c_qk = load(qk_h, qk_v)
     c_gate = load(uv_h.at[0, :, pl.ds(at_mine, unit_part)], uv_v.at[0])
+    c_value = load(uv_h.at[1, :, pl.ds(at_mine, unit_part)], uv_v.at[1])
     c_out = []
     for k in range(shared_by):
         at = pl.multiple_of(lax.rem(mine + k, shared_by) * unit_part, 128)
@@ -153,10 +156,6 @@
         copy.start()
         unit_sends.append(copy)
 
-    c_value.wait()
-    value_x[0] = silu(dot(normed, uv_v[1])).astype(bf16)
-    if shared_by == 2:
-        swap(value_x, 0)
     c_qk.wait()
     shared = silu(dot(normed, qk_v[...]))
     query = (shared * affine_v[0:1, :] + affine_v[1:2, :]).astype(bf16)
@@ -171,46 +170,71 @@
     ugate = silu(dot(normed, uv_v[0]))
     gate_x[0] = ugate[0:ROWS]
     if shared_by == 2:
-        swap(gate_x, 1)
-
-    p = None
-    for k in range(shared_by):
-        if k == 1:
-            for c in unit_sends:
-                c.wait_recv()
+        swap(gate_x, 0)
+    c_value.wait()
+    value_x[0] = silu(dot(normed, uv_v[1])).astype(bf16)
+    if shared_by == 2:
+        swap(value_x, 1)
+
+    def mix(k):
         seen = dot(attn, value_x[k])
         seen = seen[0:ROWS] + seen[WIDE : WIDE + ROWS]
-        mixed = jnp.concatenate([gate_x[k] * seen, jnp.zeros((WIDE - ROWS, unit_part), f32)], 0)
-        c_out[k].wait()
-        q = dot(mixed.astype(bf16), out_v[k])
-        p = q if p is None else p + q
-    part[head, :, 0:width] = p[0:16].astype(bf16)
-    part[head, :, width : width + half] = jnp.concatenate(
-        [p[16:24, 0:half], p[16:24, half:width]], 0
-    ).astype(bf16)
+        return (gate_x[k] * seen).astype(bf16)
+
+    mixed = mix(0)
+    c_out[0].wait()
+    if shared_by == 2:
+        partial_v[...] = dot(mixed, out_v[0])
+        for c in unit_sends:
+            c.wait_recv()
+        mixed = mix(1)
+        c_out[1].wait()
     sends = []
-    for d in range(1, heads):
-        copy = pltpu.make_async_remote_copy(
-            src_ref=part.at[head],
-            dst_ref=part.at[head],
-            send_sem=part_send.at[d - 1],
-            recv_sem=part_recv.at[head],
-            device_id={"head": lax.rem(head + d, heads)},
-            device_id_type=MESH,
-        )
-        copy.start()
-        sends.append(copy)
+    for n in range(2):
+        s = slice(n * half, (n + 1) * half)
+        p = dot(mixed, out_v[shared_by - 1, :, s])
+        if shared_by == 2:
+            p = p + partial_v[:, s]
+        part[head, n, :, 0:half] = p[0:16].astype(bf16)
+        part[head, n, :, half : half + quarter] = jnp.concatenate(
+            [p[16:24, 0:quarter], p[16:24, quarter:half]], 0
+        ).astype(bf16)
+        for d in range(1, heads):
+            copy = pltpu.make_async_remote_copy(
+                src_ref=part.at[head, n],
+                dst_ref=part.at[head, n],
+                send_sem=part_send.at[d - 1, n],
+                recv_sem=part_recv.at[head, n],
+                device_id={"head": lax.rem(head + d, heads)},
+                device_id_type=MESH,
+            )
+            copy.start()
+            sends.append(copy)
 
     for c in c_pairs + c_par:
         c.wait()
     w_in_b[...] = w_in_v[...].astype(bf16)
-    for m in range(6):
-        w_tri_b[:, m * chans : (m + 1) * chans] = w_tri_v[m].astype(bf16)
+    for k in range(2):
+        w_pair_b[:, k * chans : (k + 1) * chans] = w_pairin_v[k].astype(bf16)
+    v0 = vecs_v[0:1, :]
+    v1 = vecs_v[1:2, :]
+    v2 = vecs_v[2:3, :]
+    v3 = vecs_v[3:4, :]
+    gain_one = vecs_v[...].T[:, 1:2]
+    gain_two = vecs_v[...].T[:, 2:3]
+    for k, m in enumerate(ORDER + (5,)):
+        c = slice(k * chans, (k + 1) * chans)
+        w = w_tri_v[m].astype(bf16)
+        w_tri_b[0:chans, c] = w
+        w = w.astype(f32) * (gain_two if m == 5 else gain_one)
+        w = jnp.sum(w, 0, keepdims=True) * (1.0 / chans)
+        w_tri_b[chans : 2 * chans, c] = jnp.broadcast_to(w, (chans, chans)).astype(bf16)
     valid = key_ok * (resolved_v[...] > 0).astype(f32)
     cols[...] = jnp.zeros_like(cols)
     for k in range(3):
         cols[k : k + 1, :] = coords_v[k]
     cols[3:4, :] = valid
+    cols[4:5, :] = tok.astype(f32)
     one_v = (onehot * valid).astype(bf16)
     weight_j = recycle * valid
     blk = 128
@@ -218,6 +242,9 @@
     places = []
     for b in range(n_blk):
         t = cols[:, b * blk : (b + 1) * blk].T
+        hot = lax.bitwise_and(iota((blk, chans), 1), WIDE - 1) == t[:, 4:5].astype(jnp.int32)
+        hot = hot & (iota((blk, chans), 1) < 3 * WIDE)
+        one_t[b * blk : (b + 1) * blk, :] = hot.astype(f32).astype(bf16)
         places.append(t)
         d2 = None
         for k in range(3):
@@ -229,6 +256,27 @@
 
     present = cnt_b[0:ROWS, :] > 0
     sc = jnp.where((cnt_row > 0) & (cnt_col > 0), scores, 0.0)[0:ROWS]
+
+    n_chunk = ROWS // 2
+    two = 2 * ROWS
+
+    def rows(k):
+        return slice(k * two, (k + 1) * two)
+
+    def both(f, k):
+        return jnp.concatenate([f(2 * k), f(2 * k + 1)], 0)
+
+    v0c = v0 - mean_last(v0)
+    for k in range(n_chunk):
+        r = rows(k)
+        sbk = both(lambda u: jnp.broadcast_to(sc[:, u : u + 1], (ROWS, chans)), k)
+        sb[r] = sbk
+        pair[r] = sbk * v0
+        n1[r] = sbk * v0c
+    lane = iota((ROWS, chans), 1)
+    score_logit = jnp.sum(v0 * v3, -1, keepdims=True) * jnp.concatenate(
+        [sc, jnp.zeros((ROWS, chans - WIDE), f32)], 1
+    )
 
     n_in = width // chans
     n_pr = w_pairin_v.shape[1] // chans
@@ -251,24 +299,27 @@
         x = RATE * jnp.maximum(0.001, jnp.sqrt(x))
         scale_o[k : k + 1, :] = jnp.broadcast_to(x, (1, chans))
 
-    for d in range(1, heads):
-        peer = lax.rem(head + d, heads)
-        pltpu.make_async_remote_copy(
-            src_ref=part.at[peer],
-            dst_ref=part.at[peer],
-            send_sem=part_send.at[d - 1],
-            recv_sem=part_recv.at[peer],
-            device_id={"head": peer},
-            device_id_type=MESH,
-        ).wait_recv()
-    low = None
-    for k in range(heads):
-        a = part[k, :, 0:width].astype(f32)
-        b = part[k, :, width : width + half].astype(f32)
-        b = jnp.concatenate([b[0:8], b[8:16]], 1)
-        low = [a, b] if low is None else [low[0] + a, low[1] + b]
-    emb[0:16, :] += low[0]
-    emb[16:24, :] += low[1]
+    for n in range(2):
+        for d in range(1, heads):
+            peer = lax.rem(head + d, heads)
+            pltpu.make_async_remote_copy(
+                src_ref=part.at[peer, n],
+                dst_ref=part.at[peer, n],
+                send_sem=part_send.at[d - 1, n],
+                recv_sem=part_recv.at[peer, n],
+                device_id={"head": peer},
+                device_id_type=MESH,
+            ).wait_recv()
+    for n in range(2):
+        s = slice(n * half, (n + 1) * half)
+        low = None
+        for k in range(heads):
+            a = part[k, n, :, 0:half].astype(f32)
+            b = part[k, n, :, half : half + quarter].astype(f32)
+            b = jnp.concatenate([b[0:8], b[8:16]], 1)
+            low = [a, b] if low is None else [low[0] + a, low[1] + b]
+        emb[0:16, s] += low[0]
+        emb[16:24, s] += low[1]
     state = emb[0:ROWS, :]
     centre = state - mean_last(state)
     frozen = centre * lax.rsqrt(mean_last(centre * centre) + 1e-05)
@@ -294,49 +345,37 @@
     single = dot(frozen, w_in_b[...]).astype(bf16)
     single_o[grp] = single[0:ROWS].astype(f32)
     give(single_o.at[grp])
-    side_a = dot(single, w_pairin_v[0].astype(bf16))[0:ROWS]
-    side_b = dot(single, w_pairin_v[1].astype(bf16))[0:ROWS]
-    side_a = jnp.where(present, side_a, 0.0)
-    side_b = jnp.where(present, side_b, 0.0)
-    v0 = vecs_v[0:1, :]
-    v1 = vecs_v[1:2, :]
-    v2 = vecs_v[2:3, :]
-    v3 = vecs_v[3:4, :]
-    v0c = v0 - mean_last(v0)
+    side = dot(single, w_pair_b[...])[0:ROWS]
+    side_a = jnp.where(present, side[:, 0:chans], 0.0)
+    side_b = jnp.where(present, side[:, chans : 2 * chans], 0.0)
     side_ac = side_a - mean_last(side_a)
     side_bc = side_b - mean_last(side_b)
 
-    n_chunk = ROWS // 2
-    two = 2 * ROWS
-
-    def rows(k):
-        return slice(k * two, (k + 1) * two)
-
-    def both(f, k):
-        return jnp.concatenate([f(2 * k), f(2 * k + 1)], 0)
-
-    for k in range(n_chunk):
-        r = rows(k)
-        sbk = both(lambda u: jnp.broadcast_to(sc[:, u : u + 1], (ROWS, chans)), k)
-        sb[r] = sbk
-        pair[r] = sbk * v0 + both(lambda u: side_a + side_b[u : u + 1, :], k)
-        centre = sbk * v0c + both(lambda u: side_ac + side_bc[u : u + 1, :], k)
+    own = iota((ROWS, chans), 0) == lane
+    logit_b = jnp.sum(
+        jnp.where(own, jnp.sum(side_b * v3, -1, keepdims=True), 0.0), 0, keepdims=True
+    )
+    logit = score_logit + jnp.sum(side_a * v3, -1, keepdims=True) + logit_b
+    for k in range(n_chunk):
+        r = rows(k)
+        pair[r] = pair[r] + both(lambda u: side_a + side_b[u : u + 1, :], k)
+        centre = n1[r] + both(lambda u: side_ac + side_bc[u : u + 1, :], k)
         scale = lax.rsqrt(mean_last(centre * centre) + 1e-05)
         normal = centre * scale
         n1[r] = normal
         s1[r] = jnp.broadcast_to(scale, (two, chans))
         pnorm[r] = (normal * v1).astype(bf16)
-    proj[...] = dot(pnorm[...], w_tri_b[:, 0 : 5 * chans])
+    proj[...] = dot(pnorm[...], w_tri_b[0:chans, 0 : 5 * chans])
     for k in range(n_chunk):
         r = rows(k)
         sl = jax.nn.sigmoid(proj[r, chans : 2 * chans])
-        sr = jax.nn.sigmoid(proj[r, 3 * chans : 4 * chans])
+        sr = jax.nn.sigmoid(proj[r, 4 * chans : 5 * chans])
         sig_l[r] = sl
         sig_r[r] = sr
         left[r] = (sl * proj[r, 0:chans]).astype(bf16).astype(f32)
-        right[r] = (sr * proj[r, 2 * chans : 3 * chans]).astype(bf16).astype(f32)
-        gate[r] = jax.nn.sigmoid(proj[r, 4 * chans : 5 * chans])
-        dwork[r] = left[r] * both(
+        right[r] = (sr * proj[r, 3 * chans : 4 * chans]).astype(bf16).astype(f32)
+        gate[r] = jax.nn.sigmoid(proj[r, 2 * chans : 3 * chans])
+        left_n[r] = left[r] * both(
             lambda u: jnp.broadcast_to(cnt_b[u : u + 1, :], (ROWS, chans)), k
         )
 
@@ -357,7 +396,7 @@
                 dst[a * ROWS : (a + 1) * ROWS, :] = t
 
     triangle(
-        upd, lambda u: dwork[u * ROWS : (u + 1) * ROWS, :], right, lambda v, u: u * ROWS + v, False
+        upd, lambda u: left_n[u * ROWS : (u + 1) * ROWS, :], right, lambda v, u: u * ROWS + v, False
     )
     for k in range(n_chunk):
         r = rows(k)
@@ -368,35 +407,42 @@
         n2[r] = normal
         s2[r] = jnp.broadcast_to(scale, (two, chans))
         unorm[r] = (normal * v2).astype(bf16)
-    branch[...] = dot(unorm[...], w_tri_b[:, 5 * chans : 6 * chans])
-    lane = iota((ROWS, chans), 1)
-    logit = jnp.zeros((ROWS, chans), f32)
-    for k in range(n_chunk):
-        r = rows(k)
-        fin = pair[r] + gate[r] * branch[r]
-        final[r] = fin
-        col = jnp.sum(fin * v3, -1, keepdims=True)
+    branch[...] = dot(unorm[...], w_tri_b[0:chans, 5 * chans : 6 * chans])
+    gated = jnp.zeros((ROWS, chans), f32)
+    for k in range(n_chunk):
+        r = rows(k)
+        move = gate[r] * branch[r]
+        final[r] = pair[r] + move
+        col = jnp.sum(move * v3, -1, keepdims=True)
+        gated_b[r] = jnp.broadcast_to(col, (two, chans))
         for q in range(2):
-            logit = jnp.where(lane == 2 * k + q, col[q * ROWS : (q + 1) * ROWS], logit)
+            gated = jnp.where(lane == 2 * k + q, col[q * ROWS : (q + 1) * ROWS], gated)
+    logit = logit + gated
 
     dist = jnp.maximum(logit, 0.0) + jnp.log1p(jnp.exp(-jnp.abs(logit)))
     dist = jnp.concatenate([dist, jnp.zeros((WIDE - ROWS, chans), f32)], 0)
     for k, d in enumerate(split(dist, 3)):
         stack_d[k * WIDE : (k + 1) * WIDE, :] = d
     by_col = dot(stack_d[:, 0:WIDE], one_b).astype(bf16)
-    one3 = jnp.concatenate([one_b, one_b, one_b], 0)
+    for k in range(n_chunk):
+        r = rows(k)
+        sl, sr, gt = sig_l[r], sig_r[r], gate[r]
+        proj[r, 0:chans] = proj[r, 0:chans] * sl * (1.0 - sl)
+        proj[r, 3 * chans : 4 * chans] = proj[r, 3 * chans : 4 * chans] * sr * (1.0 - sr)
+        gt3 = gt * v3
+        proj[r, 2 * chans : 3 * chans] = gt3 * (1.0 - gt) * branch[r]
+        gate[r] = gt3
     loss_row = jnp.zeros((1, seq), f32)
     by_first = jnp.zeros((WIDE, seq), f32)
     for b in range(n_blk):
         s = slice(b * blk, (b + 1) * blk)
-        diff = dot_tn(one3[:, s], by_col) - true_d[s, :]
+        diff = dot(one_t[s, 0 : 3 * WIDE], by_col) - true_d[s, :]
         sq = diff * diff + 1.0
         inv = lax.rsqrt(sq)
         loss_row = loss_row + jnp.sum(
             places[b][:, 3:4] * (sq * inv - 1.0), 0, keepdims=True
         )
-        for q in split(diff * inv, 2):
-            by_first = by_first + dot(one_v[:, s], q)
+        by_first = by_first + dot(one_v[:, s], (diff * inv).astype(bf16))
     loss = jnp.sum(loss_row * weight_j, -1, keepdims=True)
     by_pair = dot_nt(jnp.concatenate(split(by_first * weight_j, 2), 0), one_b)
     by_pair = (by_pair[0:WIDE] + by_pair[WIDE : 2 * WIDE])[0:ROWS]
@@ -408,23 +454,21 @@
         g = both(lambda u: jnp.broadcast_to(dlogit[:, u : u + 1], (ROWS, chans)), k)
         g_dist = g_dist + g * final[r]
         dfinal = g * v3
-        gt = gate[r]
         pair[r] = dfinal
-        dbranch[r] = (dfinal * gt).astype(bf16)
-        dproj[r, 4 * chans : 5 * chans] = (dfinal * branch[r] * gt * (1.0 - gt)).astype(bf16)
-    dwork[...] = dot_nt(dbranch[...], w_tri_b[:, 5 * chans : 6 * chans])
+        dbranch[r] = (g * gate[r]).astype(bf16)
+        dproj[r, 2 * chans : 3 * chans] = (g * proj[r, 2 * chans : 3 * chans]).astype(bf16)
+        gated_b[r] = g * gated_b[r] * (1.0 / chans)
+    dunorm[...] = dot_nt(dbranch[...], w_tri_b[:, 5 * chans : 6 * chans])
     gtri_o[grp, 5] = dot_tn(unorm[...], dbranch[...])
-    give(gtri_o.at[grp, 5])
-    gtri_o[grp, 4] = dot_tn(pnorm[...], dproj[:, 4 * chans : 5 * chans])
-    give(gtri_o.at[grp, 4])
+    gtri_o[grp, 4] = dot_tn(pnorm[...], dproj[:, 2 * chans : 3 * chans])
+    give(gtri_o.at[grp, pl.ds(4, 2)])
     g_two = jnp.zeros((two, chans), f32)
     for k in range(n_chunk):
         r = rows(k)
-        dn = dwork[r]
+        dn = dunorm[r, 0:chans]
         normal = n2[r]
         g_two = g_two + dn * normal
-        dn = dn * v2
-        upd[r] = s2[r] * (dn - mean_last(dn) - normal * mean_last(dn * normal))
+        upd[r] = s2[r] * (dn * v2 - dunorm[r, chans : 2 * chans] - normal * gated_b[r])
     triangle(
         dleft, lambda v: upd[v * ROWS : (v + 1) * ROWS, :], right, lambda u, v: u * ROWS + v, True
     )
@@ -432,35 +476,37 @@
         r = rows(k)
         d, sl = dleft[r], sig_l[r]
         dproj[r, 0:chans] = (d * sl).astype(bf16)
-        dproj[r, chans : 2 * chans] = (d * proj[r, 0:chans] * sl * (1.0 - sl)).astype(bf16)
-    for m in range(2):
-        gtri_o[grp, m] = dot_tn(pnorm[...], dproj[:, m * chans : (m + 1) * chans])
-        give(gtri_o.at[grp, m])
+        dproj[r, chans : 2 * chans] = (d * proj[r, 0:chans]).astype(bf16)
+    dpnorm[...] = dot_nt(dproj[:, 0 : 3 * chans], w_tri_b[:, 0 : 3 * chans])
+    g = dot_tn(pnorm[...], dproj[:, 0 : 2 * chans])
+    gtri_o[grp, 0] = g[:, 0:chans]
+    gtri_o[grp, 1] = g[:, chans : 2 * chans]
+    give(gtri_o.at[grp, pl.ds(0, 2)])
     triangle(
         dright, lambda t: upd[pl.ds(t, ROWS, stride=ROWS), :], left, lambda u, t: u * ROWS + t, True
     )
     for k in range(n_chunk):
         r = rows(k)
         d, sr = dright[r], sig_r[r]
-        dproj[r, 2 * chans : 3 * chans] = (d * sr).astype(bf16)
-        dproj[r, 3 * chans : 4 * chans] = (
-            d * proj[r, 2 * chans : 3 * chans] * sr * (1.0 - sr)
-        ).astype(bf16)
-    for m in range(2, 4):
-        gtri_o[grp, m] = dot_tn(pnorm[...], dproj[:, m * chans : (m + 1) * chans])
-        give(gtri_o.at[grp, m])
-    dwork[...] = dot_nt(dproj[...], w_tri_b[:, 0 : 5 * chans])
+        dproj[r, 3 * chans : 4 * chans] = (d * sr).astype(bf16)
+        dproj[r, 4 * chans : 5 * chans] = (d * proj[r, 3 * chans : 4 * chans]).astype(bf16)
+    dlast[...] = dot_nt(dproj[:, 3 * chans : 5 * chans], w_tri_b[:, 3 * chans : 5 * chans])
+    g = dot_tn(pnorm[...], dproj[:, 3 * chans : 5 * chans])
+    gtri_o[grp, 2] = g[:, 0:chans]
+    gtri_o[grp, 3] = g[:, chans : 2 * chans]
+    give(gtri_o.at[grp, pl.ds(2, 2)])
     g_one = jnp.zeros((two, chans), f32)
     g_score = jnp.zeros((two, chans), f32)
     d_a = jnp.zeros((ROWS, chans), f32)
     tail_o[grp] = jnp.zeros((WIDE, 2 * chans), f32)
     for k in range(n_chunk):
         r = rows(k)
-        dn = dwork[r]
+        dn = dpnorm[r, 0:chans] + dlast[r, 0:chans]
+        mean = dpnorm[r, chans : 2 * chans] + dlast[r, chans : 2 * chans]
         normal = n1[r]
-        g_one = g_one + dn * normal
-        dn = dn * v1
-        dpair = pair[r] + s1[r] * (dn - mean_last(dn) - normal * mean_last(dn * normal))
+        along = dn * normal
+        g_one = g_one + along
+        dpair = pair[r] + s1[r] * (dn * v1 - mean - normal * mean_last(along * v1))
         g_score = g_score + sb[r] * dpair
         d_a = d_a + dpair[0:ROWS] + dpair[ROWS:two]
         for q in range(2):
@@ -694,19 +740,21 @@
         like(coords), like(plm_embed), vm(2, width, unit_part, dtype=bf16), like(plm_qk),
         like(plm_affine), vm(shared_by, unit_part, width, dtype=bf16),
         vm(WIDE, width), vm(shared_by, ROWS, unit_part), vm(shared_by, WIDE, unit_part, dtype=bf16),
-        vm(heads, 16, width + width // 2, dtype=bf16), vm(width, node, dtype=bf16),
-        vm(chans, 6 * chans, dtype=bf16), vm(WIDE, chans), vm(seq, seq), vm(chans, seq),
+        vm(ROWS, width), vm(heads, 2, 16, width // 2 + width // 4, dtype=bf16),
+        vm(width, node, dtype=bf16), vm(node, 2 * chans, dtype=bf16),
+        vm(2 * chans, 6 * chans, dtype=bf16), vm(WIDE, chans), vm(seq, seq), vm(chans, seq),
         vm(table, chans), vm(table, chans), vm(table, chans), vm(table, chans),
         vm(table, chans, dtype=bf16), vm(table, 5 * chans), vm(table, chans), vm(table, chans),
         vm(table, chans), vm(table, chans), vm(table, chans), vm(table, chans), vm(table, chans),
         vm(table, chans), vm(table, chans, dtype=bf16),
         vm(table, chans), vm(table, chans), vm(table, chans, dtype=bf16), vm(table, chans),
+        vm(table, chans), vm(table, 2 * chans), vm(table, 2 * chans), vm(table, 2 * chans),
         vm(table, chans), vm(table, chans), vm(table, 5 * chans, dtype=bf16),
-        vm(3 * WIDE, chans, dtype=bf16), vm(chans, chans),
+        vm(3 * WIDE, chans, dtype=bf16), vm(chans, chans), vm(seq, chans, dtype=bf16),
         pltpu.SemaphoreType.DMA((19 + shared_by,)),
-        pltpu.SemaphoreType.DMA((heads - 1,)), pltpu.SemaphoreType.DMA((heads,)),
+        pltpu.SemaphoreType.DMA((heads - 1, 2)), pltpu.SemaphoreType.DMA((heads, 2)),
         pltpu.SemaphoreType.DMA((2,)), pltpu.SemaphoreType.DMA((2,)),
-        pltpu.SemaphoreType.DMA((9,)), pltpu.SemaphoreType.DMA((9,)),
+        pltpu.SemaphoreType.DMA((6,)), pltpu.SemaphoreType.DMA((6,)),
     ]
     operands = tuple(
         x if x.size == 1 else pltpu.with_memory_space_constraint(x, pltpu.HBM) for x in operands

time: 23.5 us -> 22 us (0.936)
  Pallas kernels: 21.4 us -> 19.8 us
    pallas_call x1, Pallas kernels: 17.7 us -> 16.2 us  [shards(): pl.pallas_call(functools.partial(tables_kernel, heads=heads, shared_by=sh...]
where the time goes in v5:
time: 22 us; the launch traced here: 21.8 us
  Pallas kernels  19.8 us (90%)
  between operations  1.96 us (9%)
    pallas_call x1, Pallas kernels, shards(): pl.pallas_call(functools.partial(tables_kernel, heads=heads, shared_by=sh...  16.2 us
    pallas_call x1, Pallas kernels, shards(): pl.pallas_call(update_kernel, out_shape=outs, in_specs=[inside] * len(ope...  3.66 us

profile of v5, /device:TPU:0, one launch (start us, length us, event | category | flops | bytes accessed | tf_op | source)
XLA Modules:
  0.0 21.8 jit_solution(11319267246954416275)
XLA Ops:
  2.0 16.2 %tables.1 = (bf16[2,32,1280]{2,1,0:T(8,128)(2,1)S(1)}, f32[2,24,256]{2,1,0:T(8,128)S(1)}, f32[2,6,128,128]{3,2,1,0:T(8,128)S(1)}, f32[2,32,256]{2,1,0:T(8,128)S(...) custom-call(s32[1,256]{1,0:T(1,128)} %tokens_h.1, ...), custom_call_target="tpu_custom_call" | custom-call | tf_op jit(solution)/shard_map/tables/pallas_call | solution.py:764
  18.1 3.7 %update.1 = (f32[1,128]{1,0:T(1,128)}, f32[1,128]{1,0:T(1,128)}, f32[1280,256]{1,0:T(8,128)}, f32[10,128]{1,0:T(8,128)}, f32[2,128]{1,0:T(2,128)}, /*index=5*/f3...) custom-call(bf16[2,32,1280]{2,1,0:T(8,128)(2,1)S(1)} %get-tuple-elem, ...), custom_call_target="tpu_custom_call" | custom-call | tf_op jit(solution)/shard_map/update/pallas_call | solution.py:798

commit v6 on v5

--- a/solution.py
+++ b/solution.py
@@ -53,18 +53,71 @@
     return lax.broadcasted_iota(jnp.int32, shape, dim)
 
 
+def fresh(old, total, n):
+    return BETA * old + ((1.0 - BETA) / n * total + (1.0 - BETA) * 1e-30)
+
+
+def fold(x):
+    return jnp.sum(x.reshape(x.shape[0] // 8, 8, x.shape[1]), 0)
+
+
+def adafactor(grad, weight, new, col_old, col_new, sums, old, scale):
+    n_rows, n_cols = grad.shape
+    chans = old.shape[1]
+    blk = chans
+    halves = n_cols // chans
+    col_sum = [jnp.zeros((8, chans), f32)] * halves
+    scaled = [jnp.zeros((8, chans), f32)] * halves
+    row_sum = jnp.zeros((8, chans), f32)
+    for b in range(n_rows // blk):
+        s = slice(b * blk, (b + 1) * blk)
+        row = old[s, :] + ((1.0 - BETA) / n_cols * sums[s, :] + (1.0 - BETA) * 1e-30)
+        row_sum = row_sum + fold(row)
+        root = lax.rsqrt(row)
+        for h in range(halves):
+            c = slice(h * chans, (h + 1) * chans)
+            g = grad[s, c]
+            step = g * root
+            new[s, c] = step
+            col_sum[h] = col_sum[h] + fold(g * g)
+            scaled[h] = scaled[h] + fold(step * step)
+    row_mean = jnp.sum(row_sum, 0, keepdims=True) / n_rows
+    power = jnp.zeros((1, chans), f32)
+    by_col = []
+    for h in range(halves):
+        col = fresh(col_old(h), jnp.sum(col_sum[h], 0, keepdims=True), n_rows)
+        col_new(h, col)
+        power = power + jnp.sum(scaled[h], 0, keepdims=True) / col
+        by_col.append(lax.rsqrt(col))
+    rms = jnp.sqrt(row_mean * jnp.sum(power, -1, keepdims=True) / (n_rows * n_cols))
+    coef = scale * jnp.sqrt(row_mean) / jnp.maximum(1.0, rms)
+    by_col = [x * coef for x in by_col]
+
+    def second(b, carry):
+        s = pl.ds(b * blk, blk)
+        for h in range(halves):
+            c = slice(h * chans, (h + 1) * chans)
+            new[s, c] = weight[s, c] - new[s, c] * by_col[h]
+        return carry
+
+    if n_rows == blk:
+        second(0, 0)
+    else:
+        lax.fori_loop(0, n_rows // blk, second, 0)
+
+
 def tables_kernel(
     tokens_h, lengths_s, recycle_s, resolved_h, coords_h, embed_h, uv_h, qk_h, affine_h, out_h,
     w_in_h, w_pairin_h, w_tri_h, vecs_h, row_in_h, col_in_h, row_pairin_h, col_pairin_h, row_tri_h,
     col_tri_h, sq_vecs_h,
-    frozen_o, single_o, gtri_o, tail_o, old_o, scale_o,
+    frozen_o, single_o, tail_o, old_o, scale_o, g_tri_o, new_tri_o, row_tri_o, col_tri_o,
     w_in_v, w_pairin_v, w_tri_v, vecs_v, row_in_v, col_in_v, row_pairin_v, col_pairin_v, row_tri_v,
     col_tri_v, sq_vecs_v,
     tokens_v, resolved_v, coords_v, embed_v, uv_v, qk_v, affine_v, out_v,
     emb, gate_x, value_x, partial_v, part, w_in_b, w_pair_b, w_tri_b, cnt_b, true_d, cols,
     pair, sb, n1, s1, pnorm, proj, sig_l, sig_r, gate, left, right, upd, n2, s2, unorm,
-    branch, final, dbranch, left_n, gated_b, dunorm, dpnorm, dlast, dleft, dright, dproj, stack_d,
-    old_v, one_t,
+    branch, final, dbranch, left_n, gated_b, dunorm, dpnorm, dlast, dleft, dright, dproj,
+    old_v, one_t, gtri_x, sq_tri, sum_tri,
     load_sem, part_send, part_recv, unit_send, unit_recv, peer_send, peer_recv,
     *, heads, shared_by, unit_part,
 ):
@@ -93,9 +146,9 @@
     ]
     mine = grp if shared_by == 2 else 0
     at_mine = pl.multiple_of(mine * unit_part, 128)
-    c_qk = load(qk_h, qk_v)
     c_gate = load(uv_h.at[0, :, pl.ds(at_mine, unit_part)], uv_v.at[0])
     c_value = load(uv_h.at[1, :, pl.ds(at_mine, unit_part)], uv_v.at[1])
+    c_qk = load(qk_h, qk_v)
     c_out = []
     for k in range(shared_by):
         at = pl.multiple_of(lax.rem(mine + k, shared_by) * unit_part, 128)
@@ -156,6 +209,16 @@
         copy.start()
         unit_sends.append(copy)
 
+    c_gate.wait()
+    ugate = silu(dot(normed, uv_v[0]))
+    gate_x[0] = ugate[0:ROWS]
+    if shared_by == 2:
+        swap(gate_x, 0)
+    c_value.wait()
+    value_x[0] = silu(dot(normed, uv_v[1])).astype(bf16)
+    if shared_by == 2:
+        swap(value_x, 1)
+
     c_qk.wait()
     shared = silu(dot(normed, qk_v[...]))
     query = (shared * affine_v[0:1, :] + affine_v[1:2, :]).astype(bf16)
@@ -165,16 +228,6 @@
     top = jnp.exp(masked - jnp.max(masked, -1, keepdims=True))
     attn = (top / jnp.sum(top * key_row, -1, keepdims=True)).astype(bf16).astype(f32)
     attn = jnp.concatenate(split(attn * key_row, 2), 0)
-
-    c_gate.wait()
-    ugate = silu(dot(normed, uv_v[0]))
-    gate_x[0] = ugate[0:ROWS]
-    if shared_by == 2:
-        swap(gate_x, 0)
-    c_value.wait()
-    value_x[0] = silu(dot(normed, uv_v[1])).astype(bf16)
-    if shared_by == 2:
-        swap(value_x, 1)
 
     def mix(k):
         seen = dot(attn, value_x[k])
@@ -340,11 +393,14 @@
         )
         copy.start()
         peers.append(copy)
+        return copy
 
     give(frozen_o.at[grp])
     single = dot(frozen, w_in_b[...]).astype(bf16)
-    single_o[grp] = single[0:ROWS].astype(f32)
-    give(single_o.at[grp])
+    single_o[grp] = jnp.concatenate(
+        [single[0:ROWS].astype(f32), jnp.broadcast_to(loss_count, (8, single.shape[1]))], 0
+    )
+    c_single = give(single_o.at[grp])
     side = dot(single, w_pair_b[...])[0:ROWS]
     side_a = jnp.where(present, side[:, 0:chans], 0.0)
     side_b = jnp.where(present, side[:, chans : 2 * chans], 0.0)
@@ -419,11 +475,10 @@
             gated = jnp.where(lane == 2 * k + q, col[q * ROWS : (q + 1) * ROWS], gated)
     logit = logit + gated
 
-    dist = jnp.maximum(logit, 0.0) + jnp.log1p(jnp.exp(-jnp.abs(logit)))
+    dist = jnp.maximum(logit, 0.0) + jnp.log(1.0 + jnp.exp(-jnp.abs(logit)))
     dist = jnp.concatenate([dist, jnp.zeros((WIDE - ROWS, chans), f32)], 0)
-    for k, d in enumerate(split(dist, 3)):
-        stack_d[k * WIDE : (k + 1) * WIDE, :] = d
-    by_col = dot(stack_d[:, 0:WIDE], one_b).astype(bf16)
+    dist = jnp.concatenate(split(dist, 3), 0)
+    by_col = dot(dist[:, 0:WIDE], one_b).astype(bf16)
     for k in range(n_chunk):
         r = rows(k)
         sl, sr, gt = sig_l[r], sig_r[r], gate[r]
@@ -459,9 +514,9 @@
         dproj[r, 2 * chans : 3 * chans] = (g * proj[r, 2 * chans : 3 * chans]).astype(bf16)
         gated_b[r] = g * gated_b[r] * (1.0 / chans)
     dunorm[...] = dot_nt(dbranch[...], w_tri_b[:, 5 * chans : 6 * chans])
-    gtri_o[grp, 5] = dot_tn(unorm[...], dbranch[...])
-    gtri_o[grp, 4] = dot_tn(pnorm[...], dproj[:, 2 * chans : 3 * chans])
-    give(gtri_o.at[grp, pl.ds(4, 2)])
+    gtri_x[grp, 5] = dot_tn(unorm[...], dbranch[...])
+    gtri_x[grp, 4] = dot_tn(pnorm[...], dproj[:, 2 * chans : 3 * chans])
+    c_pair = [give(gtri_x.at[grp, pl.ds(4, 2)])]
     g_two = jnp.zeros((two, chans), f32)
     for k in range(n_chunk):
         r = rows(k)
@@ -479,9 +534,9 @@
         dproj[r, chans : 2 * chans] = (d * proj[r, 0:chans]).astype(bf16)
     dpnorm[...] = dot_nt(dproj[:, 0 : 3 * chans], w_tri_b[:, 0 : 3 * chans])
     g = dot_tn(pnorm[...], dproj[:, 0 : 2 * chans])
-    gtri_o[grp, 0] = g[:, 0:chans]
-    gtri_o[grp, 1] = g[:, chans : 2 * chans]
-    give(gtri_o.at[grp, pl.ds(0, 2)])
+    gtri_x[grp, 0] = g[:, 0:chans]
+    gtri_x[grp, 1] = g[:, chans : 2 * chans]
+    c_pair.append(give(gtri_x.at[grp, pl.ds(0, 2)]))
     triangle(
         dright, lambda t: upd[pl.ds(t, ROWS, stride=ROWS), :], left, lambda u, t: u * ROWS + t, True
     )
@@ -492,9 +547,9 @@
         dproj[r, 4 * chans : 5 * chans] = (d * proj[r, 3 * chans : 4 * chans]).astype(bf16)
     dlast[...] = dot_nt(dproj[:, 3 * chans : 5 * chans], w_tri_b[:, 3 * chans : 5 * chans])
     g = dot_tn(pnorm[...], dproj[:, 3 * chans : 5 * chans])
-    gtri_o[grp, 2] = g[:, 0:chans]
-    gtri_o[grp, 3] = g[:, chans : 2 * chans]
-    give(gtri_o.at[grp, pl.ds(2, 2)])
+    gtri_x[grp, 2] = g[:, 0:chans]
+    gtri_x[grp, 3] = g[:, chans : 2 * chans]
+    c_pair.append(give(gtri_x.at[grp, pl.ds(2, 2)]))
     g_one = jnp.zeros((two, chans), f32)
     g_score = jnp.zeros((two, chans), f32)
     d_a = jnp.zeros((ROWS, chans), f32)
@@ -518,26 +573,59 @@
         tail_o[grp, ROWS + k : ROWS + k + 1, 0:chans] = jnp.sum(g, 0, keepdims=True)
     tail_o[grp, ROWS + 4 : ROWS + 5, 0:chans] = jnp.broadcast_to(loss, (1, chans))
     tail_o[grp, ROWS + 5 : ROWS + 6, 0:chans] = jnp.broadcast_to(loss_count, (1, chans))
-    give(tail_o.at[grp])
-
-    for c in sends + unit_sends:
+    c_tail = give(tail_o.at[grp])
+
+    c_single.wait_recv()
+    inv = 1.0 / (
+        single_o[0, ROWS : ROWS + 1, 0:chans] + single_o[1, ROWS : ROWS + 1, 0:chans]
+    )
+    for pairs in ((0, 1), (2,)):
+        mats = []
+        for k in pairs:
+            c_pair[k].wait_recv()
+            first = (4, 0, 2)[k]
+            mats += [first, first + 1]
+        for m in mats:
+            g = (gtri_x[0, m] + gtri_x[1, m]) * inv
+            g_tri_o[m] = g
+            sq_tri[m * chans : (m + 1) * chans, :] = (g * g).astype(bf16)
+        for m in mats:
+            r = slice(m * chans, (m + 1) * chans)
+            sum_tri[r, :] = dot(sq_tri[r, :], jnp.ones((chans, chans), bf16))
+        for m in mats:
+            total = sum_tri[m * chans : (m + 1) * chans, :].T[0:1, :]
+            row_tri_o[m : m + 1, :] = fresh(row_tri_v[m : m + 1, :], total, chans)
+
+            def put_col(h, col, m=m):
+                col_tri_o[m : m + 1, :] = col
+
+            adafactor(
+                g_tri_o.at[m], w_tri_v.at[m], new_tri_o.at[m],
+                lambda h, m=m: col_tri_v[m : m + 1, :], put_col,
+                sum_tri.at[pl.ds(m * chans, chans)],
+                old_o.at[pl.ds((at_tri + m) * chans, chans)],
+                scale_o[3 + m : 4 + m, :],
+            )
+
+    for c in sends + unit_sends + peers:
         c.wait_send()
     for c in peers:
-        c.wait()
+        if c is not c_single and all(c is not x for x in c_pair):
+            c.wait_recv()
 
 
 def update_kernel(
-    frozen_v, single_v, gtri_v, tail_v, old_v, scale_v, w_in_v, w_pairin_v, w_tri_v, vecs_v,
+    frozen_v, single_v, tail_v, old_v, scale_v, g_tri, new_tri, row_tri_n, col_tri_n,
+    w_in_v, w_pairin_v, w_tri_v, vecs_v,
     row_in_v, col_in_v, row_pairin_v, col_pairin_v, row_tri_v, col_tri_v, sq_vecs_v,
     loss_o, count_o, g_in_o, row_in_o, col_in_o, new_in_o, g_pairin_o, row_pairin_o, col_pairin_o,
     new_pairin_o, g_tri_o, row_tri_o, col_tri_o, new_tri_o, g_vecs_o, sq_vecs_o, new_vecs_o,
     loss_s, count_s, g_in, row_in_n, col_in_n, new_in, g_pairin, row_pairin_n, col_pairin_n,
-    new_pairin, g_tri, row_tri_n, col_tri_n, new_tri, g_vecs, sq_vecs_n, new_vecs,
+    new_pairin, g_vecs, sq_vecs_n, new_vecs,
     ds_v, sq_in, sq_rest, sum_in, sum_rest, store_sem,
 ):
     chans = vecs_v.shape[1]
     width, node = w_in_v.shape
-    n_mat = w_tri_v.shape[0]
     stores = []
 
     def store(src, dst):
@@ -545,6 +633,10 @@
         stores.append(copy)
         copy.start()
 
+    store(g_tri, g_tri_o)
+    store(new_tri, new_tri_o)
+    store(row_tri_n, row_tri_o)
+    store(col_tri_n, col_tri_o)
     totals = tail_v[0, ROWS : ROWS + 8, 0:chans] + tail_v[1, ROWS : ROWS + 8, 0:chans]
     inv = 1.0 / totals[5:6, :]
     inv2 = jnp.concatenate([inv, inv], 1)
@@ -567,16 +659,14 @@
     g_in[...] = dot_tn(fz, ds_v[...])
     store(g_in, g_in_o)
 
-    sg = jnp.concatenate([single_v[0], single_v[1], single_v[0], single_v[1]], 0).astype(bf16)
+    sg = [single_v[i, 0:ROWS] for i in range(2)]
+    sg = jnp.concatenate(sg + sg, 0).astype(bf16)
     st = jnp.concatenate(
         [side_parts[i][k].astype(f32) for k in range(2) for i in range(2)], 0
     ).astype(bf16)
     for k in range(2):
         g_pairin[k] = dot_tn(sg, st[:, k * chans : (k + 1) * chans])
     store(g_pairin, g_pairin_o)
-    for m in range(n_mat):
-        g_tri[m] = (gtri_v[0, m] + gtri_v[1, m]) * inv
-    store(g_tri, g_tri_o)
     loss_s[...] = totals[4:5, :]
     count_s[...] = totals[5:6, :]
     g_vecs[...] = totals[0:4, :] * inv
@@ -587,7 +677,6 @@
     blk = chans
     n_in = width // blk
     n_pr = w_pairin_v.shape[1] // blk
-    at_tri = 2 * n_pr
     for b in range(n_in):
         g = g_in[b * blk : (b + 1) * blk, :]
         sq_in[b * blk : (b + 1) * blk, :] = (g * g).astype(bf16)
@@ -596,70 +685,19 @@
             g = g_pairin[k, b * blk : (b + 1) * blk, :]
             j = k * n_pr + b
             sq_rest[j * blk : (j + 1) * blk, :] = (g * g).astype(bf16)
-    for m in range(n_mat):
-        g = g_tri[m]
-        j = at_tri + m
-        sq_rest[j * blk : (j + 1) * blk, :] = (g * g).astype(bf16)
     sum_in[...] = dot(sq_in[...], jnp.ones((node, chans), bf16))
     sum_rest[...] = dot(sq_rest[...], jnp.ones((chans, chans), bf16))
-    lane_in = dot_nt(jnp.ones((16, node), bf16), sq_in[...])[0:1]
-    lane_rest = dot_nt(jnp.ones((16, chans), bf16), sq_rest[...])[0:1]
-
-    def fresh(old, total, n):
-        return BETA * old + ((1.0 - BETA) / n * total + (1.0 - BETA) * 1e-30)
-
     for b in range(n_in):
-        row_in_n[b : b + 1, :] = fresh(
-            row_in_v[b : b + 1, :], lane_in[:, b * blk : (b + 1) * blk], node
-        )
+        total = sum_in[b * blk : (b + 1) * blk, :].T[0:1, :]
+        row_in_n[b : b + 1, :] = fresh(row_in_v[b : b + 1, :], total, node)
     for k in range(2):
-        s = slice(k * n_pr * blk, (k + 1) * n_pr * blk)
-        row_pairin_n[k : k + 1, :] = fresh(row_pairin_v[k : k + 1, :], lane_rest[:, s], chans)
-    for m in range(n_mat):
-        s = slice((at_tri + m) * blk, (at_tri + m + 1) * blk)
-        row_tri_n[m : m + 1, :] = fresh(row_tri_v[m : m + 1, :], lane_rest[:, s], chans)
+        for b in range(n_pr):
+            j = k * n_pr + b
+            total = sum_rest[j * blk : (j + 1) * blk, :].T[0:1, :]
+            c = slice(b * blk, (b + 1) * blk)
+            row_pairin_n[k : k + 1, c] = fresh(row_pairin_v[k : k + 1, c], total, chans)
     store(row_in_n, row_in_o)
     store(row_pairin_n, row_pairin_o)
-    store(row_tri_n, row_tri_o)
-
-    def fold(x):
-        return jnp.sum(x.reshape(blk // 8, 8, x.shape[1]), 0)
-
-    def adafactor(grad, weight, new, col_old, col_new, sums, old_at, n_blk, which, n_cols):
-        n_rows = n_blk * blk
-        halves = n_cols // chans
-        col_sum = [jnp.zeros((8, chans), f32)] * halves
-        scaled = [jnp.zeros((8, chans), f32)] * halves
-        row_sum = jnp.zeros((8, chans), f32)
-        for b in range(n_blk):
-            s = slice(b * blk, (b + 1) * blk)
-            o = slice((old_at + b) * blk, (old_at + b + 1) * blk)
-            t = sums[0][(sums[1] + b) * blk : (sums[1] + b + 1) * blk, :]
-            row = old_v[o, :] + ((1.0 - BETA) / n_cols * t + (1.0 - BETA) * 1e-30)
-            row_sum = row_sum + fold(row)
-            root = lax.rsqrt(row)
-            for h in range(halves):
-                c = slice(h * chans, (h + 1) * chans)
-                g = grad[s, c]
-                step = g * root
-                new[s, c] = step
-                col_sum[h] = col_sum[h] + fold(g * g)
-                scaled[h] = scaled[h] + fold(step * step)
-        row_mean = jnp.sum(row_sum, 0, keepdims=True) / n_rows
-        power = jnp.zeros((1, chans), f32)
-        by_col = []
-        for h in range(halves):
-            col = fresh(col_old(h), jnp.sum(col_sum[h], 0, keepdims=True), n_rows)
-            col_new(h, col)
-            power = power + jnp.sum(scaled[h], 0, keepdims=True) / col
-            by_col.append(lax.rsqrt(col))
-        rms = jnp.sqrt(row_mean * jnp.sum(power, -1, keepdims=True) / (n_rows * n_cols))
-        coef = scale_v[which : which + 1, :] * jnp.sqrt(row_mean) / jnp.maximum(1.0, rms)
-        for b in range(n_blk):
-            s = slice(b * blk, (b + 1) * blk)
-            for h in range(halves):
-                c = slice(h * chans, (h + 1) * chans)
-                new[s, c] = weight[s, c] - new[s, c] * (by_col[h] * coef)
 
     def put(ref, k):
         def put_col(h, col):
@@ -669,8 +707,8 @@
         return put_col
 
     adafactor(
-        g_in, w_in_v, new_in, lambda h: col_in_v[h : h + 1, :], put(col_in_n, None), (sum_in, 0), 0,
-        n_in, 0, node,
+        g_in, w_in_v, new_in, lambda h: col_in_v[h : h + 1, :], put(col_in_n, None), sum_in,
+        old_v.at[pl.ds(0, width)], scale_v[0:1, :],
     )
     store(new_in, new_in_o)
     store(col_in_n, col_in_o)
@@ -678,18 +716,11 @@
         adafactor(
             g_pairin.at[k], w_pairin_v.at[k], new_pairin.at[k],
             lambda h, k=k: col_pairin_v[k : k + 1, :], put(col_pairin_n, k),
-            (sum_rest, k * n_pr), n_in + k * n_pr, n_pr, 1 + k, chans,
+            sum_rest.at[pl.ds(k * n_pr * blk, n_pr * blk)],
+            old_v.at[pl.ds((n_in + k * n_pr) * blk, n_pr * blk)], scale_v[1 + k : 2 + k, :],
         )
     store(new_pairin, new_pairin_o)
     store(col_pairin_n, col_pairin_o)
-    for m in range(n_mat):
-        adafactor(
-            g_tri.at[m], w_tri_v.at[m], new_tri.at[m],
-            lambda h, m=m: col_tri_v[m : m + 1, :], put(col_tri_n, m),
-            (sum_rest, at_tri + m), n_in + at_tri + m, 1, 3 + m, chans,
-        )
-    store(new_tri, new_tri_o)
-    store(col_tri_n, col_tri_o)
 
     g = g_vecs[...]
     sq = BETA * sq_vecs_v[...] + (1.0 - BETA) * (g * g + 1e-30)
@@ -750,7 +781,8 @@
         vm(table, chans), vm(table, chans), vm(table, chans, dtype=bf16), vm(table, chans),
         vm(table, chans), vm(table, 2 * chans), vm(table, 2 * chans), vm(table, 2 * chans),
         vm(table, chans), vm(table, chans), vm(table, 5 * chans, dtype=bf16),
-        vm(3 * WIDE, chans, dtype=bf16), vm(chans, chans), vm(seq, chans, dtype=bf16),
+        vm(chans, chans), vm(seq, chans, dtype=bf16),
+        vm(2, 6, chans, chans), vm(6 * chans, chans, dtype=bf16), vm(6 * chans, chans),
         pltpu.SemaphoreType.DMA((19 + shared_by,)),
         pltpu.SemaphoreType.DMA((heads - 1, 2)), pltpu.SemaphoreType.DMA((heads, 2)),
         pltpu.SemaphoreType.DMA((2,)), pltpu.SemaphoreType.DMA((2,)),
@@ -764,14 +796,15 @@
     made = pl.pallas_call(
         functools.partial(tables_kernel, heads=heads, shared_by=shared_by, unit_part=unit_part),
         out_shape=(
-            sds((2, WIDE, width), bf16), sds((2, ROWS, node), f32), sds((2, 6, chans, chans), f32),
-            sds((2, WIDE, 2 * chans), f32), sds((n_blk * chans, chans), f32), sds((16, chans), f32),
+            sds((2, WIDE, width), bf16), sds((2, WIDE, node), f32), sds((2, WIDE, 2 * chans), f32),
+            sds((n_blk * chans, chans), f32), sds((16, chans), f32), sds(w_tri.shape, f32),
+            sds(w_tri.shape, f32), sds(row_tri.shape, f32), sds(col_tri.shape, f32),
         )
         + tuple(sds(x.shape, x.dtype) for x in kept),
         in_specs=[
             pl.BlockSpec(memory_space=pltpu.SMEM) if x.size == 1 else anywhere for x in operands
         ],
-        out_specs=[inside] * (6 + len(kept)),
+        out_specs=[inside] * (9 + len(kept)),
         scratch_shapes=scratch,
         compiler_params=pltpu.CompilerParams(
             collective_id=0, has_side_effects=True, vmem_limit_bytes=48 << 20
@@ -786,11 +819,10 @@
     )
     outs = tuple(sds(x.shape, x.dtype) for x in outs)
     scratch = (
-        [like(x) for x in outs]
+        [like(x) for k, x in enumerate(outs) if k not in (10, 11, 12, 13)]
         + [
             vm(4 * WIDE, node, dtype=bf16), vm(width, node, dtype=bf16),
-            vm((n_blk - width // chans) * chans, chans, dtype=bf16), vm(width, chans),
-            vm((n_blk - width // chans) * chans, chans),
+            vm(2 * node, chans, dtype=bf16), vm(width, chans), vm(2 * node, chans),
             pltpu.SemaphoreType.DMA((17,)),
         ]
     )

time: 22 us -> 20.9 us (0.950)
  Pallas kernels: 19.8 us -> 18.6 us
    pallas_call x1, Pallas kernels: 3.66 us -> 2.85 us  [shards(): pl.pallas_call(update_kernel, out_shape=outs, in_specs=[inside] * len(ope...]
    pallas_call x1, Pallas kernels: 16.2 us -> 15.8 us  [shards(): pl.pallas_call(functools.partial(tables_kernel, heads=heads, shared_by=sh...]
where the time goes in v6:
time: 20.9 us; the launch traced here: 20.6 us
  Pallas kernels  18.6 us (89%)
  between operations  1.96 us (9%)
    pallas_call x1, Pallas kernels, shards(): pl.pallas_call(functools.partial(tables_kernel, heads=heads, shared_by=sh...  15.8 us
    pallas_call x1, Pallas kernels, shards(): pl.pallas_call(update_kernel, out_shape=outs, in_specs=[inside] * len(ope...  2.85 us

profile of v6, /device:TPU:0, one launch (start us, length us, event | category | flops | bytes accessed | tf_op | source)
XLA Modules:
  0.0 20.6 jit_solution(5509757320635595504)
XLA Ops:
  2.0 15.8 %tables.1 = (bf16[2,32,1280]{2,1,0:T(8,128)(2,1)S(1)}, f32[2,32,256]{2,1,0:T(8,128)S(1)}, f32[2,32,256]{2,1,0:T(8,128)S(1)}, f32[2560,128]{1,0:T(8,128)S(1)}, f3...) custom-call(s32[1,256]{1,0:T(1,128)} %tokens_h.1, ...), custom_call_target="tpu_custom_call" | custom-call | tf_op jit(solution)/shard_map/tables/pallas_call | solution.py:796
  17.7 2.8 %update.1 = (f32[1,128]{1,0:T(1,128)}, f32[1,128]{1,0:T(1,128)}, f32[1280,256]{1,0:T(8,128)}, f32[10,128]{1,0:T(8,128)}, f32[2,128]{1,0:T(2,128)}, /*index=5*/f3...) custom-call(bf16[2,32,1280]{2,1,0:T(8,128)(2,1)S(1)} %get-tuple-elem, ...), custom_call_target="tpu_custom_call" | custom-call | tf_op jit(solution)/shard_map/update/pallas_call | solution.py:830

commit v7 on v6

--- a/solution.py
+++ b/solution.py
@@ -114,9 +114,9 @@
     w_in_v, w_pairin_v, w_tri_v, vecs_v, row_in_v, col_in_v, row_pairin_v, col_pairin_v, row_tri_v,
     col_tri_v, sq_vecs_v,
     tokens_v, resolved_v, coords_v, embed_v, uv_v, qk_v, affine_v, out_v,
-    emb, gate_x, value_x, partial_v, part, w_in_b, w_pair_b, w_tri_b, cnt_b, true_d, cols,
+    emb, item_x, gate_x, value_x, partial_v, part, w_in_b, w_pair_b, w_tri_b, cnt_b, true_d, cols,
     pair, sb, n1, s1, pnorm, proj, sig_l, sig_r, gate, left, right, upd, n2, s2, unorm,
-    branch, final, dbranch, left_n, gated_b, dunorm, dpnorm, dlast, dleft, dright, dproj,
+    branch, final, dbranch, left_n, gated_b, dunorm, dpnorm, dlast, dleft, dright, upd_t, dproj,
     old_v, one_t, gtri_x, sq_tri, sum_tri,
     load_sem, part_send, part_recv, unit_send, unit_recv, peer_send, peer_recv,
     *, heads, shared_by, unit_part,
@@ -124,6 +124,13 @@
     grp = lax.axis_index("grp")
     head = lax.axis_index("head")
     other = 1 - grp
+    turned = lax.rem(head, 2)
+    item = lax.rem(grp + head, 2)
+
+    def partner(d):
+        peer = lax.rem(head + d, heads)
+        return {"grp": lax.rem(item + peer, 2), "head": peer}
+
     seq = tokens_v.shape[1]
     width = emb.shape[1]
     chans = vecs_v.shape[1]
@@ -142,6 +149,8 @@
     c_small = [
         load(embed_h, embed_v),
         load(tokens_h, tokens_v),
+        load(resolved_h, resolved_v),
+        load(coords_h, coords_v),
         load(affine_h, affine_v),
     ]
     mine = grp if shared_by == 2 else 0
@@ -153,7 +162,6 @@
     for k in range(shared_by):
         at = pl.multiple_of(lax.rem(mine + k, shared_by) * unit_part, 128)
         c_out.append(load(out_h.at[pl.ds(at, unit_part)], out_v.at[k]))
-    c_pairs = [load(resolved_h, resolved_v), load(coords_h, coords_v)]
     c_par = [
         load(w_in_h, w_in_v),
         load(w_pairin_h, w_pairin_v),
@@ -171,8 +179,7 @@
     barrier = pltpu.get_barrier_semaphore()
     pl.semaphore_signal(barrier, inc=1, device_id={"grp": other}, device_id_type=MESH)
     for d in range(1, heads):
-        peer = lax.rem(head + d, heads)
-        pl.semaphore_signal(barrier, inc=1, device_id={"head": peer}, device_id_type=MESH)
+        pl.semaphore_signal(barrier, inc=1, device_id=partner(d), device_id_type=MESH)
 
     for c in c_small:
         c.wait()
@@ -182,18 +189,13 @@
     centre = e - mean_last(e)
     normed = (centre * lax.rsqrt(mean_last(centre * centre) + 1e-05)).astype(bf16)
 
-    length = lengths_s[0]
-    recycle = recycle_s[0].astype(f32)
-    tok = tokens_v[...]
-    onehot = (iota((WIDE, seq), 0) == tok).astype(f32)
-    key_ok = (iota((1, seq), 1) < length).astype(f32)
-    one_b = onehot.astype(bf16)
-    cnt_col = jnp.sum(onehot, -1, keepdims=True)
-    cnt_b[...] = jnp.broadcast_to(cnt_col, (WIDE, chans))
-    ones = jnp.ones((16, seq), bf16)
-    cnt_row = dot_nt(ones, one_b)[0:1, :]
-    key_row = dot_nt(ones, (onehot * key_ok).astype(bf16))[0:1, :]
-
+    key_ok = (iota((1, seq), 1) < lengths_s[0]).astype(f32)
+    for k in range(3):
+        item_x[0, k : k + 1, :] = coords_v[k]
+    item_x[0, 3:4, :] = key_ok * (resolved_v[...] > 0).astype(f32)
+    item_x[0, 4:5, :] = tokens_v[...].astype(f32)
+    item_x[0, 5:6, :] = key_ok
+    item_x[0, 6:8, :] = jnp.broadcast_to(recycle_s[0].astype(f32), (2, seq))
     pl.semaphore_wait(barrier, heads)
     unit_sends = []
 
@@ -208,6 +210,9 @@
         )
         copy.start()
         unit_sends.append(copy)
+        return copy
+
+    c_item = swap(item_x, 2)
 
     c_gate.wait()
     ugate = silu(dot(normed, uv_v[0]))
@@ -219,6 +224,19 @@
     if shared_by == 2:
         swap(value_x, 1)
 
+    c_item.wait_recv()
+    cols[0:8, :] = jnp.where(turned > 0, item_x[1], item_x[0])
+    valid = cols[3:4, :]
+    key_ok = cols[5:6, :]
+    recycle = cols[6:7, 0:1]
+    onehot = (iota((WIDE, seq), 0) == cols[4:5, :].astype(jnp.int32)).astype(f32)
+    one_b = onehot.astype(bf16)
+    cnt_col = jnp.sum(onehot, -1, keepdims=True)
+    cnt_b[...] = jnp.broadcast_to(cnt_col, (WIDE, chans))
+    ones = jnp.ones((16, seq), bf16)
+    cnt_row = dot_nt(ones, one_b)[0:1, :]
+    key_row = dot_nt(ones, (onehot * key_ok).astype(bf16))[0:1, :]
+
     c_qk.wait()
     shared = silu(dot(normed, qk_v[...]))
     query = (shared * affine_v[0:1, :] + affine_v[1:2, :]).astype(bf16)
@@ -238,7 +256,7 @@
     c_out[0].wait()
     if shared_by == 2:
         partial_v[...] = dot(mixed, out_v[0])
-        for c in unit_sends:
+        for c in unit_sends[1:]:
             c.wait_recv()
         mixed = mix(1)
         c_out[1].wait()
@@ -258,13 +276,13 @@
                 dst_ref=part.at[head, n],
                 send_sem=part_send.at[d - 1, n],
                 recv_sem=part_recv.at[head, n],
-                device_id={"head": lax.rem(head + d, heads)},
+                device_id=partner(d),
                 device_id_type=MESH,
             )
             copy.start()
             sends.append(copy)
 
-    for c in c_pairs + c_par:
+    for c in c_par:
         c.wait()
     w_in_b[...] = w_in_v[...].astype(bf16)
     for k in range(2):
@@ -282,12 +300,7 @@
         w = w.astype(f32) * (gain_two if m == 5 else gain_one)
         w = jnp.sum(w, 0, keepdims=True) * (1.0 / chans)
         w_tri_b[chans : 2 * chans, c] = jnp.broadcast_to(w, (chans, chans)).astype(bf16)
-    valid = key_ok * (resolved_v[...] > 0).astype(f32)
-    cols[...] = jnp.zeros_like(cols)
-    for k in range(3):
-        cols[k : k + 1, :] = coords_v[k]
-    cols[3:4, :] = valid
-    cols[4:5, :] = tok.astype(f32)
+    cols[8:chans, :] = jnp.zeros((chans - 8, seq), f32)
     one_v = (onehot * valid).astype(bf16)
     weight_j = recycle * valid
     blk = 128
@@ -360,7 +373,7 @@
                 dst_ref=part.at[peer, n],
                 send_sem=part_send.at[d - 1, n],
                 recv_sem=part_recv.at[peer, n],
-                device_id={"head": peer},
+                device_id=partner(d),
                 device_id_type=MESH,
             ).wait_recv()
     for n in range(2):
@@ -377,7 +390,7 @@
     centre = state - mean_last(state)
     frozen = centre * lax.rsqrt(mean_last(centre * centre) + 1e-05)
     frozen = jnp.concatenate([frozen, jnp.zeros((WIDE - ROWS, width), f32)], 0).astype(bf16)
-    frozen_o[grp] = frozen
+    frozen_o[item] = frozen
 
     peers = []
 
@@ -395,12 +408,12 @@
         peers.append(copy)
         return copy
 
-    give(frozen_o.at[grp])
+    give(frozen_o.at[item])
     single = dot(frozen, w_in_b[...]).astype(bf16)
-    single_o[grp] = jnp.concatenate(
+    single_o[item] = jnp.concatenate(
         [single[0:ROWS].astype(f32), jnp.broadcast_to(loss_count, (8, single.shape[1]))], 0
     )
-    c_single = give(single_o.at[grp])
+    c_single = give(single_o.at[item])
     side = dot(single, w_pair_b[...])[0:ROWS]
     side_a = jnp.where(present, side[:, 0:chans], 0.0)
     side_b = jnp.where(present, side[:, chans : 2 * chans], 0.0)
@@ -514,9 +527,9 @@
         dproj[r, 2 * chans : 3 * chans] = (g * proj[r, 2 * chans : 3 * chans]).astype(bf16)
         gated_b[r] = g * gated_b[r] * (1.0 / chans)
     dunorm[...] = dot_nt(dbranch[...], w_tri_b[:, 5 * chans : 6 * chans])
-    gtri_x[grp, 5] = dot_tn(unorm[...], dbranch[...])
-    gtri_x[grp, 4] = dot_tn(pnorm[...], dproj[:, 2 * chans : 3 * chans])
-    c_pair = [give(gtri_x.at[grp, pl.ds(4, 2)])]
+    gtri_x[item, 5] = dot_tn(unorm[...], dbranch[...])
+    gtri_x[item, 4] = dot_tn(pnorm[...], dproj[:, 2 * chans : 3 * chans])
+    c_pair = [give(gtri_x.at[item, pl.ds(4, 2)])]
     g_two = jnp.zeros((two, chans), f32)
     for k in range(n_chunk):
         r = rows(k)
@@ -534,11 +547,13 @@
         dproj[r, chans : 2 * chans] = (d * proj[r, 0:chans]).astype(bf16)
     dpnorm[...] = dot_nt(dproj[:, 0 : 3 * chans], w_tri_b[:, 0 : 3 * chans])
     g = dot_tn(pnorm[...], dproj[:, 0 : 2 * chans])
-    gtri_x[grp, 0] = g[:, 0:chans]
-    gtri_x[grp, 1] = g[:, chans : 2 * chans]
-    c_pair.append(give(gtri_x.at[grp, pl.ds(0, 2)]))
+    gtri_x[item, 0] = g[:, 0:chans]
+    gtri_x[item, 1] = g[:, chans : 2 * chans]
+    c_pair.append(give(gtri_x.at[item, pl.ds(0, 2)]))
+    for t in range(vocab):
+        upd_t[t * ROWS : (t + 1) * ROWS, :] = upd[pl.ds(t, ROWS, stride=ROWS), :]
     triangle(
-        dright, lambda t: upd[pl.ds(t, ROWS, stride=ROWS), :], left, lambda u, t: u * ROWS + t, True
+        dright, lambda t: upd_t[t * ROWS : (t + 1) * ROWS, :], left, lambda u, t: u * ROWS + t, True
     )
     for k in range(n_chunk):
         r = rows(k)
@@ -547,13 +562,13 @@
         dproj[r, 4 * chans : 5 * chans] = (d * proj[r, 3 * chans : 4 * chans]).astype(bf16)
     dlast[...] = dot_nt(dproj[:, 3 * chans : 5 * chans], w_tri_b[:, 3 * chans : 5 * chans])
     g = dot_tn(pnorm[...], dproj[:, 3 * chans : 5 * chans])
-    gtri_x[grp, 2] = g[:, 0:chans]
-    gtri_x[grp, 3] = g[:, chans : 2 * chans]
-    c_pair.append(give(gtri_x.at[grp, pl.ds(2, 2)]))
+    gtri_x[item, 2] = g[:, 0:chans]
+    gtri_x[item, 3] = g[:, chans : 2 * chans]
+    c_pair.append(give(gtri_x.at[item, pl.ds(2, 2)]))
     g_one = jnp.zeros((two, chans), f32)
     g_score = jnp.zeros((two, chans), f32)
     d_a = jnp.zeros((ROWS, chans), f32)
-    tail_o[grp] = jnp.zeros((WIDE, 2 * chans), f32)
+    tail_o[item] = jnp.zeros((WIDE, 2 * chans), f32)
     for k in range(n_chunk):
         r = rows(k)
         dn = dpnorm[r, 0:chans] + dlast[r, 0:chans]
@@ -565,15 +580,15 @@
         g_score = g_score + sb[r] * dpair
         d_a = d_a + dpair[0:ROWS] + dpair[ROWS:two]
         for q in range(2):
-            tail_o[grp, 2 * k + q : 2 * k + q + 1, chans : 2 * chans] = jnp.sum(
+            tail_o[item, 2 * k + q : 2 * k + q + 1, chans : 2 * chans] = jnp.sum(
                 dpair[q * ROWS : (q + 1) * ROWS], 0, keepdims=True
             )
-    tail_o[grp, 0:ROWS, 0:chans] = d_a
+    tail_o[item, 0:ROWS, 0:chans] = d_a
     for k, g in enumerate((g_score, g_one, g_two, g_dist)):
-        tail_o[grp, ROWS + k : ROWS + k + 1, 0:chans] = jnp.sum(g, 0, keepdims=True)
-    tail_o[grp, ROWS + 4 : ROWS + 5, 0:chans] = jnp.broadcast_to(loss, (1, chans))
-    tail_o[grp, ROWS + 5 : ROWS + 6, 0:chans] = jnp.broadcast_to(loss_count, (1, chans))
-    c_tail = give(tail_o.at[grp])
+        tail_o[item, ROWS + k : ROWS + k + 1, 0:chans] = jnp.sum(g, 0, keepdims=True)
+    tail_o[item, ROWS + 4 : ROWS + 5, 0:chans] = jnp.broadcast_to(loss, (1, chans))
+    tail_o[item, ROWS + 5 : ROWS + 6, 0:chans] = jnp.broadcast_to(loss_count, (1, chans))
+    c_tail = give(tail_o.at[item])
 
     c_single.wait_recv()
     inv = 1.0 / (
@@ -770,7 +785,7 @@
         like(tokens), like(resolved),
         like(coords), like(plm_embed), vm(2, width, unit_part, dtype=bf16), like(plm_qk),
         like(plm_affine), vm(shared_by, unit_part, width, dtype=bf16),
-        vm(WIDE, width), vm(shared_by, ROWS, unit_part), vm(shared_by, WIDE, unit_part, dtype=bf16),
+        vm(WIDE, width), vm(2, 8, seq), vm(shared_by, ROWS, unit_part), vm(shared_by, WIDE, unit_part, dtype=bf16),
         vm(ROWS, width), vm(heads, 2, 16, width // 2 + width // 4, dtype=bf16),
         vm(width, node, dtype=bf16), vm(node, 2 * chans, dtype=bf16),
         vm(2 * chans, 6 * chans, dtype=bf16), vm(WIDE, chans), vm(seq, seq), vm(chans, seq),
@@ -780,12 +795,12 @@
         vm(table, chans), vm(table, chans, dtype=bf16),
         vm(table, chans), vm(table, chans), vm(table, chans, dtype=bf16), vm(table, chans),
         vm(table, chans), vm(table, 2 * chans), vm(table, 2 * chans), vm(table, 2 * chans),
-        vm(table, chans), vm(table, chans), vm(table, 5 * chans, dtype=bf16),
+        vm(table, chans), vm(table, chans), vm(table, chans), vm(table, 5 * chans, dtype=bf16),
         vm(chans, chans), vm(seq, chans, dtype=bf16),
         vm(2, 6, chans, chans), vm(6 * chans, chans, dtype=bf16), vm(6 * chans, chans),
         pltpu.SemaphoreType.DMA((19 + shared_by,)),
         pltpu.SemaphoreType.DMA((heads - 1, 2)), pltpu.SemaphoreType.DMA((heads, 2)),
-        pltpu.SemaphoreType.DMA((2,)), pltpu.SemaphoreType.DMA((2,)),
+        pltpu.SemaphoreType.DMA((3,)), pltpu.SemaphoreType.DMA((3,)),
         pltpu.SemaphoreType.DMA((6,)), pltpu.SemaphoreType.DMA((6,)),
     ]
     operands = tuple(

time: 20.9 us -> 20.7 us (level)
  no operation moved by 1% of the time
where the time goes in v7:
time: 20.7 us; the launch traced here: 20.5 us
  Pallas kernels  18.6 us (90%)
  between operations  1.96 us (9%)
    pallas_call x1, Pallas kernels, shards(): pl.pallas_call(functools.partial(tables_kernel, heads=heads, shared_by=sh...  15.7 us
    pallas_call x1, Pallas kernels, shards(): pl.pallas_call(update_kernel, out_shape=outs, in_specs=[inside] * len(ope...  2.85 us

profile of v7, /device:TPU:0, one launch (start us, length us, event | category | flops | bytes accessed | tf_op | source)
XLA Modules:
  0.0 20.5 jit_solution(13133518598955431495)
XLA Ops:
  2.0 15.7 %tables.1 = (bf16[2,32,1280]{2,1,0:T(8,128)(2,1)S(1)}, f32[2,32,256]{2,1,0:T(8,128)S(1)}, f32[2,32,256]{2,1,0:T(8,128)S(1)}, f32[2560,128]{1,0:T(8,128)S(1)}, f3...) custom-call(s32[1,256]{1,0:T(1,128)} %tokens_h.1, ...), custom_call_target="tpu_custom_call" | custom-call | tf_op jit(solution)/shard_map/tables/pallas_call | solution.py:811
  17.7 2.8 %update.1 = (f32[1,128]{1,0:T(1,128)}, f32[1,128]{1,0:T(1,128)}, f32[1280,256]{1,0:T(8,128)}, f32[10,128]{1,0:T(8,128)}, f32[2,128]{1,0:T(2,128)}, /*index=5*/f3...) custom-call(bf16[2,32,1280]{2,1,0:T(8,128)(2,1)S(1)} %get-tuple-elem, ...), custom_call_target="tpu_custom_call" | custom-call | tf_op jit(solution)/shard_map/update/pallas_call | solution.py:845

commit v8 on v7

--- a/solution.py
+++ b/solution.py
@@ -32,8 +32,12 @@
     return lax.dot_general(a, b, (((0,), (0,)), ((), ())), preferred_element_type=f32)
 
 
+def sigmoid(x):
+    return 0.5 * jnp.tanh(0.5 * x) + 0.5
+
+
 def silu(x):
-    return x * jax.nn.sigmoid(x)
+    return x * sigmoid(x)
 
 
 def mean_last(x):
@@ -100,8 +104,9 @@
             new[s, c] = weight[s, c] - new[s, c] * by_col[h]
         return carry
 
-    if n_rows == blk:
-        second(0, 0)
+    if n_rows <= 2 * blk:
+        for b in range(n_rows // blk):
+            second(b, 0)
     else:
         lax.fori_loop(0, n_rows // blk, second, 0)
 
@@ -437,19 +442,19 @@
     proj[...] = dot(pnorm[...], w_tri_b[0:chans, 0 : 5 * chans])
     for k in range(n_chunk):
         r = rows(k)
-        sl = jax.nn.sigmoid(proj[r, chans : 2 * chans])
-        sr = jax.nn.sigmoid(proj[r, 4 * chans : 5 * chans])
+        sl = sigmoid(proj[r, chans : 2 * chans])
+        sr = sigmoid(proj[r, 4 * chans : 5 * chans])
         sig_l[r] = sl
         sig_r[r] = sr
         left[r] = (sl * proj[r, 0:chans]).astype(bf16).astype(f32)
         right[r] = (sr * proj[r, 3 * chans : 4 * chans]).astype(bf16).astype(f32)
-        gate[r] = jax.nn.sigmoid(proj[r, 2 * chans : 3 * chans])
+        gate[r] = sigmoid(proj[r, 2 * chans : 3 * chans])
         left_n[r] = left[r] * both(
             lambda u: jnp.broadcast_to(cnt_b[u : u + 1, :], (ROWS, chans)), k
         )
 
     def triangle(dst, moving, fixed, row_of, weighted):
-        group = 4
+        group = 8
         for a0 in range(0, ROWS, group):
             total = [None] * group
             for b in range(vocab):
@@ -514,7 +519,7 @@
     loss = jnp.sum(loss_row * weight_j, -1, keepdims=True)
     by_pair = dot_nt(jnp.concatenate(split(by_first * weight_j, 2), 0), one_b)
     by_pair = (by_pair[0:WIDE] + by_pair[WIDE : 2 * WIDE])[0:ROWS]
-    dlogit = by_pair * jax.nn.sigmoid(logit)[:, 0:WIDE]
+    dlogit = by_pair * sigmoid(logit)[:, 0:WIDE]
 
     g_dist = jnp.zeros((two, chans), f32)
     for k in range(n_chunk):

time: 20.7 us -> 20.7 us (level)
  no operation moved by 1% of the time
where the time goes in v8:
time: 20.7 us; the launch traced here: 20.5 us
  Pallas kernels  18.5 us (89%)
  between operations  1.96 us (9%)
    pallas_call x1, Pallas kernels, shards(): pl.pallas_call(functools.partial(tables_kernel, heads=heads, shared_by=sh...  15.7 us
    pallas_call x1, Pallas kernels, shards(): pl.pallas_call(update_kernel, out_shape=outs, in_specs=[inside] * len(ope...  2.84 us

profile of v8, /device:TPU:0, one launch (start us, length us, event | category | flops | bytes accessed | tf_op | source)
XLA Modules:
  0.0 20.5 jit_solution(9949441665287876618)
XLA Ops:
  2.0 15.7 %tables.1 = (bf16[2,32,1280]{2,1,0:T(8,128)(2,1)S(1)}, f32[2,32,256]{2,1,0:T(8,128)S(1)}, f32[2,32,256]{2,1,0:T(8,128)S(1)}, f32[2560,128]{1,0:T(8,128)S(1)}, f3...) custom-call(s32[1,256]{1,0:T(1,128)} %tokens_h.1, ...), custom_call_target="tpu_custom_call" | custom-call | tf_op jit(solution)/shard_map/tables/pallas_call | solution.py:816
  17.7 2.8 %update.1 = (f32[1,128]{1,0:T(1,128)}, f32[1,128]{1,0:T(1,128)}, f32[1280,256]{1,0:T(8,128)}, f32[10,128]{1,0:T(8,128)}, f32[2,128]{1,0:T(2,128)}, /*index=5*/f3...) custom-call(bf16[2,32,1280]{2,1,0:T(8,128)(2,1)S(1)} %get-tuple-elem, ...), custom_call_target="tpu_custom_call" | custom-call | tf_op jit(solution)/shard_map/update/pallas_call | solution.py:850

commit v9 on v8

--- a/solution.py
+++ b/solution.py
@@ -413,12 +413,10 @@
         peers.append(copy)
         return copy
 
-    give(frozen_o.at[item])
     single = dot(frozen, w_in_b[...]).astype(bf16)
     single_o[item] = jnp.concatenate(
         [single[0:ROWS].astype(f32), jnp.broadcast_to(loss_count, (8, single.shape[1]))], 0
     )
-    c_single = give(single_o.at[item])
     side = dot(single, w_pair_b[...])[0:ROWS]
     side_a = jnp.where(present, side[:, 0:chans], 0.0)
     side_b = jnp.where(present, side[:, chans : 2 * chans], 0.0)
@@ -472,6 +470,8 @@
     triangle(
         upd, lambda u: left_n[u * ROWS : (u + 1) * ROWS, :], right, lambda v, u: u * ROWS + v, False
     )
+    give(frozen_o.at[item])
+    c_single = give(single_o.at[item])
     for k in range(n_chunk):
         r = rows(k)
         x = upd[r]

time: 20.7 us -> 20.7 us (level)
  no operation moved by 1% of the time
where the time goes in v9:
time: 20.7 us; the launch traced here: 20.6 us
  Pallas kernels  18.6 us (90%)
  between operations  1.96 us (9%)
    pallas_call x1, Pallas kernels, shards(): pl.pallas_call(functools.partial(tables_kernel, heads=heads, shared_by=sh...  15.8 us
    pallas_call x1, Pallas kernels, shards(): pl.pallas_call(update_kernel, out_shape=outs, in_specs=[inside] * len(ope...  2.85 us

profile of v9, /device:TPU:0, one launch (start us, length us, event | category | flops | bytes accessed | tf_op | source)
XLA Modules:
  0.0 20.6 jit_solution(11145391109543869311)
XLA Ops:
  2.0 15.8 %tables.1 = (bf16[2,32,1280]{2,1,0:T(8,128)(2,1)S(1)}, f32[2,32,256]{2,1,0:T(8,128)S(1)}, f32[2,32,256]{2,1,0:T(8,128)S(1)}, f32[2560,128]{1,0:T(8,128)S(1)}, f3...) custom-call(s32[1,256]{1,0:T(1,128)} %tokens_h.1, ...), custom_call_target="tpu_custom_call" | custom-call | tf_op jit(solution)/shard_map/tables/pallas_call | solution.py:816
  17.7 2.8 %update.1 = (f32[1,128]{1,0:T(1,128)}, f32[1,128]{1,0:T(1,128)}, f32[1280,256]{1,0:T(8,128)}, f32[10,128]{1,0:T(8,128)}, f32[2,128]{1,0:T(2,128)}, /*index=5*/f3...) custom-call(bf16[2,32,1280]{2,1,0:T(8,128)(2,1)S(1)} %get-tuple-elem, ...), custom_call_target="tpu_custom_call" | custom-call | tf_op jit(solution)/shard_map/update/pallas_call | solution.py:850
